TPU v7x, 256 devices: a whole 4x4x8 slice. The times are simulated.
256 devices in a mesh: owner: 8 (over y, x_lo), tile: 32 (over z, x_hi, core).
Axes of the slice: x: 4 (x_hi: 2, x_lo: 2; x = x_hi * 2 + x_lo), y: 4, z: 8, core: 2. Of those that a mesh axis runs over, the one named last changes fastest.
Arguments:
- embeddings: bfloat16 [65536, 768], P(('owner', 'tile'))
- cluster_id: int32 [65536], P(('owner', 'tile')), may hold values from 0 to 15, as said below
- order_rank: int32 [65536], P(('owner', 'tile')), may hold values from 0 to 65535, each once
- row_count: int32 [256], P(('owner', 'tile')), may hold values from 1 to 256, 49152 in all
Outputs:
- dup_score: float32 [65536], P(('owner', 'tile'))
Inputs may be any that keep to these rules, and one draw needn't show every extreme that they name: cluster_id mod 8 is the owner group of the cluster; among the live rows of one device at most 48 belong to one owner group, and some device has exactly 48 for one group.
All inputs are finite; a program needn't handle non-finite values. No bound on the sum of `row_count` on one device may be relied on, other than what follows from the above.
Results may differ from a plain program's by a relative error of at most 0.00052.
Values may be sent and summed in bfloat16 or wider, within the bound.
No kernel may reach another device: no remote copies, remote signals or barrier semaphores. Data moves between devices by JAX's collectives and lax.ppermute only.
A program may use at most 128 MiB of HBM per device.

v0:
```python
import jax
import jax.numpy as jnp
from jax import lax
from jax.sharding import PartitionSpec as P

norm_eps = 1e-06


def normalize_rows(embeddings):
    widened = embeddings.astype(jnp.float32)
    return (
        widened * lax.rsqrt(jnp.sum(widened * widened, axis=1, keepdims=True) + norm_eps)
    ).astype(jnp.bfloat16)


def earlier_match(queries, carried, pieces):
    query_rows, query_ids, query_ranks = queries
    piece_rows, piece_ids, piece_ranks = pieces
    scores = lax.dot_general(
        query_rows, piece_rows, (((1,), (1,)), ((), ())), preferred_element_type=jnp.float32
    )
    allowed = (
        (query_ids[:, None] == piece_ids[None, :])
        & (piece_ids[None, :] >= 0)
        & (piece_ranks[None, :] < query_ranks[:, None])
    )
    return jnp.maximum(carried, jnp.max(jnp.where(allowed, scores, -1.0), axis=1))


def body(embeddings, cluster_id, order_rank, row_count):
    row_local = embeddings.shape[0]
    owners = lax.axis_size("owner")
    capacity = 3 * row_local // (2 * owners)
    slot_total = owners * capacity
    unit_rows = normalize_rows(embeddings)
    position = jnp.arange(row_local, dtype=jnp.int32)
    live_row = position < row_count[0]
    target = cluster_id % owners
    chosen = (
        (target[:, None] == jnp.arange(owners, dtype=jnp.int32)[None, :]) & live_row[:, None]
    ).astype(jnp.int32)
    before = jnp.cumsum(chosen, axis=0) - chosen
    within = jnp.sum(before * chosen, axis=1)
    slot_of = jnp.where(live_row, target * capacity + within, slot_total)
    source = jnp.full((slot_total,), row_local, jnp.int32).at[slot_of].set(position, mode="drop")
    filled = source < row_local
    source_row = jnp.minimum(source, row_local - 1)
    send_rows = jnp.where(filled[:, None], unit_rows[source_row], jnp.zeros((), jnp.bfloat16))
    send_ids = jnp.where(filled, cluster_id[source_row], -1)
    send_ranks = jnp.where(filled, order_rank[source_row], 0)
    start_best = jnp.full((slot_total,), -1.0, jnp.float32)
    arrived_rows, arrived_ids, arrived_ranks = (
        lax.all_to_all(send_rows, "owner", split_axis=0, concat_axis=0, tiled=True),
        lax.all_to_all(send_ids, "owner", split_axis=0, concat_axis=0, tiled=True),
        lax.all_to_all(send_ranks, "owner", split_axis=0, concat_axis=0, tiled=True),
    )
    queries = (arrived_rows, arrived_ids, arrived_ranks)
    best_score = earlier_match(
        queries,
        start_best,
        (
            lax.all_gather(arrived_rows, "tile", axis=0, tiled=True),
            lax.all_gather(arrived_ids, "tile", axis=0, tiled=True),
            lax.all_gather(arrived_ranks, "tile", axis=0, tiled=True),
        ),
    )
    answered = lax.all_to_all(best_score, "owner", split_axis=0, concat_axis=0, tiled=True)
    picked = answered[jnp.minimum(slot_of, slot_total - 1)]
    return jnp.where(live_row, picked, 0.0)


def solution(mesh):
    return jax.shard_map(
        body,
        mesh=mesh,
        in_specs=(
            P(("owner", "tile"), None),
            P(("owner", "tile")),
            P(("owner", "tile")),
            P(("owner", "tile")),
        ),
        out_specs=P(("owner", "tile")),
        check_vma=False,
    )
```

profile of v0, /device:TPU:1, one launch (start us, length us, event | category | flops | bytes accessed | tf_op | source)
XLA Modules:
  0.0 219.7 jit_solution(10258283949866499232)
XLA Ops:
  6.5 0.0 copy-start
  6.5 0.0 all-gather.4.cloned.1.call-start
  6.5 0.7 fusion.12
  7.2 0.7 and_select_fusion
  7.9 1.2 fusion
  9.1 1.1 fusion.1
  10.9 0.6 reduce-window.6
  11.5 0.2 slice_reduce_fusion
  11.7 0.1 fusion.3
  11.8 0.7 compare_select_fusion.1
  12.6 1.4 scatter_custom_fusion
  14.0 3.6 %gather_fusion = s32[384]{0:T(512)S(1)} fusion(s32[256]{0:T(256)} %param.5, s32[1024]{0:T(1024)S(1)} %pad_clamp_fusion.1), kind=kCustom, calls=%fused_computation | custom fusion | bytes 4608 | tf_op jit(solution)/shard_map/gather | solution.py:49
  17.6 2.2 gather_fusion.2
  19.8 0.1 broadcast_in_dim.59
  19.9 0.1 broadcast_select_fusion
  20.0 15.6 %all_to_all.39 = bf16[8,48,768]{2,1,0:T(8,128)(2,1)} all-to-all(bf16[8,48,768]{2,1,0:T(8,128)(2,1)S(1)} %broadcast_select_fusion), channel_id=1, replica_groups=mesh['owner'=8,'tile'=32] {'owner'}, dimensions={0} | all-to-all | bytes 1179648 | tf_op jit(solution)/shard_map/all_to_all | solution.py:53
  35.6 0.0 all-gather.4.cloned.1.call-update
  35.6 0.0 copy-done
  35.6 2.8 %gather_fusion.1 = s32[384]{0:T(512)S(1)} fusion(s32[256]{0:T(256)S(1)} %copy-done, s32[1024]{0:T(1024)S(1)} %pad_clamp_fusion.1), kind=kCustom, calls=%fused_computation.1 | custom fusion | bytes 4608 | tf_op jit(solution)/shard_map/gather | solution.py:50
  38.4 0.7 all_to_all.28
  39.1 3.3 %all-to-all-start.1 = ((s32[8,48,1]{1,2,0:T(1,128)}), s32[8,48,1]{1,2,0:T(1,128)S(1)}, u32[]{:S(2)}, u32[]{:S(2)}) async-start(s32[8,48,1]{1,2,0:T(1,128)} %bitcast.6), calls=%async_computation.1 | async-start | bytes 8192 | tf_op jit(solution)/shard_map/all_to_all | solution.py:55
  42.4 0.7 all_to_all.26
  43.1 4.3 %all-to-all-done.1 = s32[8,48,1]{1,2,0:T(1,128)S(1)} async-done(((s32[8,48,1]{1,2,0:T(1,128)}), s32[8,48,1]{1,2,0:T(1,128)S(1)}, u32[]{:S(2)}, u32[]{:S(2)}) %all-to-all-start.1) | async-done | bytes 1568 | tf_op jit(solution)/shard_map/all_to_all | solution.py:55
  47.4 3.3 %all-to-all-start = ((s32[8,48,1]{1,2,0:T(1,128)}), s32[8,48,1]{1,2,0:T(1,128)S(1)}, u32[]{:S(2)}, u32[]{:S(2)}) async-start(s32[8,48,1]{1,2,0:T(1,128)} %bitcast.4), calls=%async_computation | async-start | bytes 8192 | tf_op jit(solution)/shard_map/all_to_all | solution.py:54
  50.7 0.5 broadcast.102
  51.2 0.7 reduce.15
  51.9 0.1 reshape.115
  52.0 3.8 %all-to-all-done = s32[8,48,1]{1,2,0:T(1,128)S(1)} async-done(((s32[8,48,1]{1,2,0:T(1,128)}), s32[8,48,1]{1,2,0:T(1,128)S(1)}, u32[]{:S(2)}, u32[]{:S(2)}) %all-to-all-start) | async-done | bytes 1568 | tf_op jit(solution)/shard_map/all_to_all | solution.py:54
  55.8 0.1 reshape.113
  55.8 0.1 all_to_all.30
  55.9 0.7 reduce.16
  56.6 0.1 eq.47
  56.7 48.7 %all-gather.1 = s32[32,1,384]{2,1,0:T(1,128)S(1)} all-gather(s32[1,1,384]{2,1,0:T(1,128)S(1)} %reshape.115), channel_id=1, replica_groups=mesh['owner'=8,'tile'=32] {'tile'}, dimensions={0}, use_global_device_ids=true | all-gather | bytes 50688 | tf_op jit(solution)/shard_map/all_gather | solution.py:64
  105.4 37.5 %all-gather = s32[32,1,384]{2,1,0:T(1,128)S(1)} all-gather(s32[1,1,384]{2,1,0:T(1,128)S(1)} %reshape.113), channel_id=1, replica_groups=mesh['owner'=8,'tile'=32] {'tile'}, dimensions={0}, use_global_device_ids=true | all-gather | bytes 50688 | tf_op jit(solution)/shard_map/all_gather | solution.py:63
  142.9 44.4 %all-gather.4.cloned.1.call-done = bf16[12288,768]{1,0:T(8,128)(2,1)} async-done(((bf16[384,768]{1,0:T(8,128)(2,1)}), bf16[12288,768]{1,0:T(8,128)(2,1)}) %all-gather.4.cloned.1.call-update) | async-done | bytes 18874384 | tf_op jit(solution)/shard_map/all_gather | solution.py:62
  187.3 12.1 %select_reduce_fusion = f32[384]{0:T(512)S(1)} fusion(bf16[384,768]{1,0:T(8,128)(2,1)} %bitcast.31, bf16[12288,768]{1,0:T(8,128)(2,1)} %all-gather.4.cloned.1.call-done, s32[12288]{0:T(1024)S(1)} %bitcast.34, s32[12288]{0:T(1024)S(1)} %bitcast.33, s32[384]{0:T(512)S(1)} %all_to_all.30, s32[384]{0:T(512)S(1)} %eq.47, ...), kind=kOutput, calls=%fused_computation.5 | convolution fusion | flops 7276068352 | bytes 19579392 | tf_op jit(solution)/shard_map/dot_general | solution.py:19
  199.4 0.7 max_broadcast_in_dim.14
  200.1 4.0 %all-to-all-start.3 = ((f32[8,48,1]{1,2,0:T(1,128)}), f32[8,48,1]{1,2,0:T(1,128)S(1)}, u32[]{:S(2)}, u32[]{:S(2)}) async-start(f32[8,48,1]{1,2,0:T(1,128)} %bitcast.10), calls=%async_computation.3 | async-start | bytes 8192 | tf_op jit(solution)/shard_map/all_to_all | solution.py:67
  204.1 5.0 %all-to-all-done.3 = f32[8,48,1]{1,2,0:T(1,128)S(1)} async-done(((f32[8,48,1]{1,2,0:T(1,128)}), f32[8,48,1]{1,2,0:T(1,128)S(1)}, u32[]{:S(2)}, u32[]{:S(2)}) %all-to-all-start.3) | async-done | bytes 1568 | tf_op jit(solution)/shard_map/all_to_all | solution.py:67
  209.1 0.5 broadcast.104
  209.6 0.7 reduce.17
  210.3 0.1 all_to_all.34
  210.3 1.9 gather_fusion.3
  212.3 0.6 broadcast_select_fusion.3
  (14 shorter events, 0.1 us)
Async XLA Ops:
  6.5 29.1 %copy-start = (s32[256]{0:T(256)S(1)}, s32[256]{0:T(256)}, u32[]{:S(2)}) copy-start(s32[256]{0:T(256)} %param.6) | copy-start | bytes 3076
  6.5 180.7 %all-gather.4.cloned.1.call-start = ((), (), s32[]{:S(2)}) async-start(), calls=%async_computation.4 | async-start | bytes 19464192 | tf_op jit(solution)/shard_map/all_gather | solution.py:62
  39.1 8.3 %all-to-all-start.1 = ((s32[8,48,1]{1,2,0:T(1,128)}), s32[8,48,1]{1,2,0:T(1,128)S(1)}, u32[]{:S(2)}, u32[]{:S(2)}) async-start(s32[8,48,1]{1,2,0:T(1,128)} %bitcast.6), calls=%async_computation.1 | async-start | bytes 8192 | tf_op jit(solution)/shard_map/all_to_all | solution.py:55
  47.4 8.4 %all-to-all-start = ((s32[8,48,1]{1,2,0:T(1,128)}), s32[8,48,1]{1,2,0:T(1,128)S(1)}, u32[]{:S(2)}, u32[]{:S(2)}) async-start(s32[8,48,1]{1,2,0:T(1,128)} %bitcast.4), calls=%async_computation | async-start | bytes 8192 | tf_op jit(solution)/shard_map/all_to_all | solution.py:54
  200.1 9.0 %all-to-all-start.3 = ((f32[8,48,1]{1,2,0:T(1,128)}), f32[8,48,1]{1,2,0:T(1,128)S(1)}, u32[]{:S(2)}, u32[]{:S(2)}) async-start(f32[8,48,1]{1,2,0:T(1,128)} %bitcast.10), calls=%async_computation.3 | async-start | bytes 8192 | tf_op jit(solution)/shard_map/all_to_all | solution.py:67
Sparse Core Ops, SparseCore 0:
  35.7 151.5 all-gather.3
where the time goes:
time: 220 us
  blocking collectives  102 us (46%)
  waiting for transfers between devices  57.4 us (26%)
  local copies, waits for them, and re-layouts  15.7 us (7%)
  between operations  14.2 us (6%)
  matrix products  12.1 us (6%)
  starting transfers between devices  10.7 us (5%)
  other arithmetic  7.83 us (4%)
    all_gather x1, blocking collectives, body(): lax.all_gather(arrived_ranks, 'tile', axis=0, tiled=True)  48.7 us
    all_gather x1, waiting for transfers between devices, body(): lax.all_gather(arrived_rows, 'tile', axis=0, tiled=True)  44.4 us
    all_gather x1, blocking collectives, body(): lax.all_gather(arrived_ids, 'tile', axis=0, tiled=True)  37.5 us
    all_to_all x1, blocking collectives, body(): lax.all_to_all(send_rows, 'owner', split_axis=0, concat_axis=0, tiled=True)  15.6 us
    dot_general x1, matrix products, earlier_match(): lax.dot_general(query_rows, piece_rows, (((1,), (1,)), ((), ())), preferr...  12.1 us
    all_to_all x1, waiting for transfers between devices, body(): lax.all_to_all(best_score, 'owner', split_axis=0, concat_axis=0, tiled=True)  4.99 us
  transfers between devices with their start and end apart: 4, of which 4 were waited for; matrix products, arithmetic and copies ran while one was open for 2% of the time, Pallas kernels for 0%

commit v1 on v0

v1 whole, which is shorter than its diff:
```python
import functools

import jax
import jax.numpy as jnp
from jax import lax
from jax.experimental import pallas as pl
from jax.experimental.pallas import tpu as pltpu
from jax.sharding import Mesh, PartitionSpec as P

norm_eps = 1e-06
ROWS = 256
WIDTH = 768
META = 128
GROUPS = 8
SLOTS = 48
ROUTED = GROUPS * SLOTS
CAP = 304
HELD = CAP - 3
CAPL = 384
LAST = CAP - 16
NEVER = 512.0
PIECES = (1, 1, 2, 1, 1, 1, 1)
OVER = 100.0
VMEM_LIMIT = 50 * 1024 * 1024
PLANE = ("y", "xl", "xh", "core")
COLUMN = ("z", "core")
RETURN = ("xl", "z", "xh", "core")


def dot(a, b, contract):
    return lax.dot_general(a, b, (contract, ((), ())), preferred_element_type=jnp.float32)


def iota(shape, axis):
    return lax.broadcasted_iota(jnp.int32, shape, axis)


def split3(v):
    hi = v.astype(jnp.bfloat16)
    rest = v - hi.astype(jnp.float32)
    mid = rest.astype(jnp.bfloat16)
    low = (rest - mid.astype(jnp.float32)).astype(jnp.bfloat16)
    return hi, mid, low


def pick_rows(v, one_hot):
    n = v.shape[0]
    parts = dot(jnp.concatenate(split3(v), axis=0), one_hot, ((1,), (0,)))
    return (parts[:n] + parts[n : 2 * n]) + parts[2 * n :]


def call(kernel, out, *args, smem=(), smem_out=(), cost=1, scratch=()):
    space = lambda i, scalars: pl.BlockSpec(memory_space=pltpu.SMEM if i in scalars else pltpu.VMEM)
    out_specs = space(0, smem_out)
    if isinstance(out, tuple):
        out_specs = tuple(space(i, smem_out) for i in range(len(out)))
    return pl.pallas_call(
        kernel,
        out_shape=out,
        in_specs=[space(i, smem) for i in range(len(args))],
        out_specs=out_specs,
        scratch_shapes=list(scratch),
        cost_estimate=pl.CostEstimate(
            flops=2 * cost * CAP * CAP * WIDTH, bytes_accessed=4 * CAP * WIDTH, transcendentals=0
        ),
        compiler_params=pltpu.CompilerParams(vmem_limit_bytes=VMEM_LIMIT),
    )(*args)


def signed(core, value):
    return jnp.where(core == 0, value, -value)


def slot_kernel(place_ref, count_ref, id_ref, rank_ref, where_ref, marks_ref, slot_ref):
    ids = id_ref[...]
    ranks = rank_ref[...]
    live = iota((1, ROWS), 1) < count_ref[0]
    target = ids & (GROUPS - 1)
    chosen = jnp.where((iota((GROUPS, ROWS), 0) == target) & live, 1.0, 0.0)
    upper = jnp.where(iota((ROWS, ROWS), 0) < iota((ROWS, ROWS), 1), 1.0, 0.0).astype(jnp.bfloat16)
    before = dot(chosen.astype(jnp.bfloat16), upper, ((1,), (0,)))
    within = jnp.sum(before * chosen, axis=0, keepdims=True).astype(jnp.int32)
    steps = signed(place_ref[1], target - place_ref[2]) & (GROUPS - 1)
    at = jnp.where(steps == 3, 4, jnp.where(steps == 4, 3, steps))
    slot = jnp.where(live, at * SLOTS + within, -1)
    where_to = jnp.where(iota((ROUTED, ROWS), 0) == slot, 1.0, 0.0).astype(jnp.bfloat16)
    high = ranks >> 8
    row = iota((META, ROWS), 0)
    meta = jnp.where(
        row == 0, ids + 1, jnp.where(row == 1, high, jnp.where(row == 2, ranks - (high << 8), 0))
    )
    meta = meta.astype(jnp.float32).astype(jnp.bfloat16)
    where_ref[...] = where_to
    marks_ref[...] = dot(where_to, meta, ((1,), (1,))).astype(jnp.bfloat16)
    slot_ref[0:1, :] = jnp.where(live, target, -1)
    slot_ref[1:2, :] = within
    slot_ref[2:8, :] = jnp.zeros((6, ROWS), jnp.int32)


def piece_kernel(emb_ref, where_ref, marks_ref, *out_refs):
    x = emb_ref[...].astype(jnp.float32)
    unit = (x * lax.rsqrt(jnp.sum(x * x, axis=1, keepdims=True) + norm_eps)).astype(jnp.bfloat16)
    rows = dot(where_ref[...], unit, ((1,), (0,))).astype(jnp.bfloat16)
    at = 0
    for ref in out_refs:
        size = ref.shape[0]
        ref[:, :WIDTH] = rows[at : at + size]
        ref[:, WIDTH:] = marks_ref[at : at + size, :]
        at += size


def collect_kernel(*refs):
    out_ref = refs[-1]
    for i, ref in enumerate(refs[:-1]):
        out_ref[i * SLOTS : (i + 1) * SLOTS, :] = ref[:SLOTS, :]


def compact_kernel(place_ref, *refs):
    *parts, block_ref, both_ref = refs
    both = 2 * ROUTED
    at = 0
    for ref in parts:
        both_ref[at : at + ref.shape[0], :] = ref[...]
        at += ref.shape[0]
    eye = jnp.where(iota((8, META), 0) == iota((8, META), 1), 1.0, 0.0).astype(jnp.bfloat16)
    meta = dot(eye, both_ref[:, WIDTH:], ((1,), (1,)))
    mine = place_ref[2] + GROUPS * place_ref[1] + 1
    ones = jnp.where(meta[0:1, :] == mine.astype(jnp.float32), 1.0, 0.0)
    chunks = [ones[:, i : i + META] for i in range(0, both, META)]
    upper = jnp.where(iota((META, META), 0) < iota((META, META), 1), 1.0, 0.0).astype(jnp.bfloat16)
    stacked = jnp.concatenate(chunks + [jnp.zeros((8 - len(chunks), META), jnp.float32)], axis=0)
    before = dot(stacked.astype(jnp.bfloat16), upper, ((1,), (0,)))
    total, counted = jnp.zeros((1, 1), jnp.float32), []
    for i, chunk in enumerate(chunks):
        counted.append(jnp.where(chunk > 0.5, before[i : i + 1, :] + total, -1.0))
        total = total + jnp.sum(chunk, axis=1, keepdims=True)
    pos = jnp.concatenate(counted, axis=1).astype(jnp.int32)
    where_to = jnp.where((iota((CAPL, both), 0) == pos) & (pos < HELD), 1.0, 0.0).astype(jnp.bfloat16)
    rows = dot(where_to[:CAP, :], both_ref[:, :WIDTH], ((1,), (0,)))
    ranks = dot(meta.astype(jnp.bfloat16), where_to, ((1,), (1,)))
    lane = iota((1, CAPL), 1)
    filled = (lane.astype(jnp.float32) < total) & (lane < HELD)
    high = jnp.where(filled, ranks[1:2, :], NEVER)
    high = jnp.where((lane == CAPL - 1) & (total > HELD), 2 * NEVER, high)
    low = jnp.where(filled, ranks[2:3, :], 0.0)
    place = pos + 1
    marks = (jnp.concatenate([high, low], axis=1), (place >> 8).astype(jnp.float32), (place & 255).astype(jnp.float32))
    row = iota((16, WIDTH), 0)
    last = rows[LAST:, :]
    for i, mark in enumerate(marks):
        last = jnp.where(row == 13 + i, mark, last)
    block_ref[:LAST, :] = rows[:LAST, :].astype(jnp.bfloat16)
    block_ref[LAST:, :] = last.astype(jnp.bfloat16)


def row_ranks(block):
    tail = block[LAST:, :].astype(jnp.float32)
    return (256.0 * tail[13:14, :CAPL] + tail[13:14, CAPL:])[:, :CAP]


def column_ranks(block, eye):
    high = dot(eye, block[LAST:, :CAPL], ((1,), (1,)))
    low = dot(eye, block[LAST:, CAPL:], ((1,), (1,)))
    return 256.0 * high[:, 13:14] + low[:, 13:14]


def slot_places(block):
    both = 2 * ROUTED
    tail = block[LAST:, :].astype(jnp.float32)
    first = iota((16, both), 0) * SLOTS
    lane = iota((16, both), 1)
    here = (lane >= first) & (lane < first + SLOTS)
    parts = jnp.concatenate([jnp.where(here, tail[i : i + 1, :], 0.0) for i in (14, 15)], axis=0)
    slot = iota((both, META), 0)
    slot = slot - SLOTS * ((slot * 1366) >> 16)
    fold = jnp.where(slot == iota((both, META), 1), 1.0, 0.0).astype(jnp.bfloat16)
    folded = dot(parts.astype(jnp.bfloat16), fold, ((1,), (0,)))
    return (256.0 * folded[:16] + folded[16:]).astype(jnp.int32) - 1


def make_eye():
    return jnp.where(iota((CAP, CAPL), 0) == iota((CAP, CAPL), 1), 1.0, 0.0).astype(jnp.bfloat16)


def earlier_best(query, query_ranks, key, key_ranks):
    scores = dot(key[...], query[...], ((1,), (1,)))
    return jnp.max(jnp.where(key_ranks < query_ranks, scores, -1.0), axis=0, keepdims=True)


def by_core(place_ref, run, a, b):
    pl.when(place_ref[1] == 0)(lambda: run(a, b))
    pl.when(place_ref[1] == 1)(lambda: run(b, a))


def near_kernel(place_ref, own, a_first, a_second, b_first, b_second, best_ref, columns_ref, places_ref):
    def run(xs, ys):
        eye = make_eye()
        keys = (own,) + ys
        key_ranks = [column_ranks(key, eye) for key in keys]
        for i, columns in enumerate(key_ranks):
            columns_ref[i] = jnp.broadcast_to(columns, (CAP, META))
        best_ref[...] = jnp.full((8, CAPL), -1.0, jnp.float32)
        for i, query in enumerate((own,) + xs):
            ranks = row_ranks(query)
            best = jnp.full((1, CAP), -1.0, jnp.float32)
            for key, columns in zip(keys, key_ranks):
                best = jnp.maximum(best, earlier_best(query, ranks, key, columns))
            best_ref[i : i + 1, :CAP] = best
            places_ref[16 * i : 16 * (i + 1), :] = slot_places(query)

    by_core(place_ref, run, (a_first, a_second), (b_first, b_second))


def mid_kernel(
    place_ref, own, a_first, a_second, b_first, b_second, a_far, near_ref, columns_ref,
    best_ref, column_ref, places_ref,
):
    best_ref[...] = near_ref[...]

    def x_far(a, b):
        ranks = row_ranks(a_far)
        best = jnp.full((1, CAP), -1.0, jnp.float32)
        for i, key in enumerate((own,) + b):
            best = jnp.maximum(best, earlier_best(a_far, ranks, key, columns_ref[i, :, 0:1]))
        best_ref[3:4, :CAP] = best
        column_ref[...] = jnp.zeros((CAP, META), jnp.float32)
        places_ref[...] = slot_places(a_far)

    def y_far(b, a):
        columns = column_ranks(a_far, make_eye())
        column_ref[...] = jnp.broadcast_to(columns, (CAP, META))
        for i, query in enumerate((own,) + b):
            best = earlier_best(query, row_ranks(query), a_far, columns)
            best_ref[i : i + 1, :CAP] = jnp.maximum(best_ref[i : i + 1, :CAP], best)
        places_ref[...] = jnp.zeros((16, META), jnp.int32)

    a, b = (a_first, a_second), (b_first, b_second)
    pl.when(place_ref[1] == 0)(lambda: x_far(a, b))
    pl.when(place_ref[1] == 1)(lambda: y_far(b, a))


def far_kernel(
    place_ref, own, a_first, a_second, b_first, b_second, a_far, b_far,
    columns_ref, near_places, mid_ref, column_ref, mid_places, out_ref, best_ref, places_ref,
):
    best_ref[...] = mid_ref[...]
    places_ref[:48, :] = near_places[...]

    def y_far():
        columns = column_ranks(b_far, make_eye())
        for i, query in enumerate((own, a_first, a_second, a_far)):
            best = earlier_best(query, row_ranks(query), b_far, columns)
            best_ref[i : i + 1, :CAP] = jnp.maximum(best_ref[i : i + 1, :CAP], best)
        places_ref[48:, :] = mid_places[...]

    def x_far():
        ranks = row_ranks(b_far)
        best = earlier_best(b_far, ranks, a_far, column_ref[:, 0:1])
        for i, key in enumerate((own, a_first, a_second)):
            best = jnp.maximum(best, earlier_best(b_far, ranks, key, columns_ref[i, :, 0:1]))
        best_ref[3:4, :CAP] = best
        places_ref[48:, :] = slot_places(b_far)

    pl.when(place_ref[1] == 0)(y_far)
    pl.when(place_ref[1] == 1)(x_far)
    over = 0.0
    for block in (own, a_first, a_second, b_first, b_second, a_far, b_far):
        tail = block[LAST:, CAPL - META : CAPL].astype(jnp.float32)
        over = jnp.maximum(over, tail[13:14, META - 1 :])
    over = jnp.where(over > NEVER, 1.0, 0.0)
    my_x, my_core, my_z = place_ref[0], place_ref[1], place_ref[2]
    rows = jnp.concatenate([jnp.broadcast_to(best_ref[i : i + 1, :], (16, CAPL)) for i in range(4)], axis=0)
    places = places_ref[...]
    found = jnp.full((64, META), -1.0, jnp.float32)
    for part in range(CAPL // META):
        values = rows[:, part * META : (part + 1) * META]
        picked = jnp.take_along_axis(values, places & (META - 1), axis=1, mode="promise_in_bounds")
        found = jnp.where((places >> 7) == part, picked, found)
    found = found + OVER * over
    messages = GROUPS * 8
    row, column = iota((messages, messages), 0), iota((messages, messages), 1)
    core = row & 1
    away = my_z - ((row >> 2) & 7)
    steps = jnp.where(core == 0, away, -away) & 7
    x_away = signed(my_core, (row >> 5) + (row & 2) - my_x) & 3
    block = jnp.where(x_away == 2, 3, jnp.where(x_away == 3, 2, x_away))
    wanted = block * 16 + (core ^ my_core) * GROUPS + steps
    order = jnp.where(column == wanted, 1.0, 0.0).astype(jnp.bfloat16)
    high, mid, low = split3(found)
    c = ((1,), (0,))
    out = (dot(order, high, c) + dot(order, mid, c)) + dot(order, low, c)
    for i in range(messages):
        out_ref[i] = out[i : i + 1, :]


def final_kernel(slot_ref, ans_ref, out_ref, flag_ref):
    target, within = slot_ref[0:1, :], slot_ref[1:2, :]
    one_hot = jnp.where(iota((META, ROWS), 0) == within, 1.0, 0.0).astype(jnp.bfloat16)
    groups = []
    for g in range(GROUPS):
        rows = [ans_ref[xl * 32 + g * 4 + i] for xl in range(2) for i in range(4)]
        groups.append(functools.reduce(jnp.maximum, rows))
    best = jnp.concatenate(groups, axis=0)
    got = pick_rows(best, one_hot)
    out_ref[...] = jnp.sum(jnp.where(iota((GROUPS, ROWS), 0) == target, got, 0.0), axis=0, keepdims=True)
    flag_ref[0] = jnp.where(jnp.max(best) > 0.5 * OVER, 1, 0).astype(jnp.int32)


def slow_path(arrived, target, within, live):
    flat = arrived
    rows, meta = flat[:, :WIDTH], flat[:, WIDTH : WIDTH + 3].astype(jnp.float32)
    ids = meta[:, 0]
    ranks = 256.0 * meta[:, 1] + meta[:, 2]
    ring = ("y", "xl", "xh", "core")
    size = 32

    def step(_, carry):
        moving, best = carry
        m = moving[:, WIDTH : WIDTH + 3].astype(jnp.float32)
        scores = dot(rows, moving[:, :WIDTH], ((1,), (1,)))
        allowed = (
            (ids[:, None] == m[None, :, 0])
            & (m[None, :, 0] > 0)
            & ((256.0 * m[:, 1] + m[:, 2])[None, :] < ranks[:, None])
        )
        best = jnp.maximum(best, jnp.max(jnp.where(allowed, scores, -1.0), axis=1))
        moving = lax.ppermute(moving, ring, [(i, (i + 1) % size) for i in range(size)])
        return moving, best

    _, best = lax.fori_loop(0, size, step, (flat, jnp.full((ROUTED,), -1.0, jnp.float32)))
    steps = signed(lax.axis_index("core"), lax.axis_index("z") - jnp.arange(GROUPS)) & (GROUPS - 1)
    answered = lax.all_to_all(best.reshape(GROUPS, SLOTS)[steps], "z", 0, 0, tiled=True)
    picked = answered[jnp.maximum(target, 0), jnp.minimum(within, SLOTS - 1)]
    return jnp.where(live, picked, 0.0)


def column_shift(steps):
    pairs = []
    for z in range(8):
        for core in range(2):
            to = (z + (steps if core == 0 else -steps)) % 8
            pairs.append((z * 2 + core, to * 2 + core))
    return pairs


def plane_shift(step, axis):
    def flat(x, y, core):
        return ((y % 4 * 2 + x % 4 % 2) * 2 + x % 4 // 2) * 2 + core

    pairs = []
    for core in range(2):
        s = step if core == 0 else -step
        dx, dy = (s, 0) if core == axis else (0, s)
        for x in range(4):
            for y in range(4):
                pairs.append((flat(x + dx, y + dy, core), flat(x, y, core)))
    return pairs


def body(embeddings, cluster_id, order_rank, row_count):
    f32, bf16, i32 = jnp.float32, jnp.bfloat16, jnp.int32
    shape = jax.ShapeDtypeStruct
    place = jnp.stack(
        [lax.axis_index("xh") * 2 + lax.axis_index("xl"), lax.axis_index("core"), lax.axis_index("z")]
    ).astype(i32)
    where_to, marks, slots = call(
        slot_kernel,
        (shape((ROUTED, ROWS), bf16), shape((ROUTED, META), bf16), shape((8, ROWS), i32)),
        place,
        row_count,
        cluster_id.reshape(1, ROWS),
        order_rank.reshape(1, ROWS),
        smem=(0, 1),
    )
    pieces = call(
        piece_kernel,
        tuple(shape((n * SLOTS, WIDTH + META), bf16) for n in PIECES),
        embeddings,
        where_to,
        marks,
    )
    send = lambda v, steps: lax.ppermute(v, COLUMN, column_shift(steps))
    two_four = send(pieces[2], 2)
    three, five, six = send(pieces[3], 3), send(pieces[4], 5), send(pieces[5], 6)
    four = send(two_four[SLOTS:], 2)
    one, seven = send(pieces[1], 1), send(pieces[6], 7)
    arrived = call(
        collect_kernel,
        shape((ROUTED, WIDTH + META), bf16),
        pieces[0],
        one,
        two_four,
        three,
        four,
        five,
        six,
        seven,
    )
    other = lax.ppermute(arrived, "core", [(0, 1), (1, 0)])
    block = call(
        compact_kernel,
        shape((CAP, WIDTH), bf16),
        place,
        arrived,
        other,
        smem=(0,),
        scratch=[pltpu.VMEM((2 * ROUTED, WIDTH + META), bf16)],
    )
    bring = lambda v, step, axis: lax.ppermute(v, PLANE, plane_shift(step, axis))
    a_first, b_first = bring(block, 1, 0), bring(block, 1, 1)
    a_second, b_second = bring(block, -1, 0), bring(block, -1, 1)
    a_far, b_far = bring(a_first, 1, 0), bring(b_first, 1, 1)
    blocks = (block, a_first, a_second, b_first, b_second)
    best_shape, column_shape, places_shape = shape((8, CAPL), f32), shape((CAP, META), f32), shape((16, META), i32)
    near, columns, near_places = call(
        near_kernel,
        (best_shape, shape((3, CAP, META), f32), shape((48, META), i32)),
        place,
        *blocks,
        smem=(0,),
        cost=9,
    )
    mid, column, mid_places = call(
        mid_kernel,
        (best_shape, column_shape, places_shape),
        place,
        *blocks,
        a_far,
        near,
        columns,
        smem=(0,),
        cost=3,
    )
    message = call(
        far_kernel,
        shape((64, 1, META), f32),
        place,
        *blocks,
        a_far,
        b_far,
        columns,
        near_places,
        mid,
        column,
        mid_places,
        smem=(0,),
        cost=4,
        scratch=[pltpu.VMEM((8, CAPL), f32), pltpu.VMEM((64, META), i32)],
    )
    answer = lax.all_to_all(message, RETURN, split_axis=0, concat_axis=0, tiled=True)
    out, flag = call(final_kernel, (shape((1, ROWS), f32), shape((1,), i32)), slots, answer, smem_out=(1,))
    target, within = slots[0], slots[1]
    return lax.cond(
        flag[0] > 0,
        lambda: slow_path(arrived, target, within, target >= 0),
        lambda: out.reshape(ROWS),
    )


def solution(mesh):
    axes = ("y", "xl", "z", "xh", "core")
    fine = Mesh(mesh.devices.reshape(4, 2, 8, 2, 2), axes)
    return jax.shard_map(
        body,
        mesh=fine,
        in_specs=(P(axes, None), P(axes), P(axes), P(axes)),
        out_specs=P(axes),
        check_vma=False,
    )
```

time: 220 us -> 78.9 us (0.36)
  blocking collectives: 102 us -> 0 us
  waiting for transfers between devices: 57.4 us -> 28.6 us
  starting transfers between devices: 10.7 us -> 35.1 us
  local copies, waits for them, and re-layouts: 15.7 us -> 1.93 us
  between operations: 14.2 us -> 1.46 us
  matrix products: 12.1 us -> 0 us
  Pallas kernels: 0 us -> 11.5 us
  other arithmetic: 7.83 us -> 0.08 us
    all_gather x2 -> x0, blocking collectives: 86.2 us -> none  [the longest x1 48.7 us: body(): lax.all_gather(arrived_ranks, 'tile', axis=0, tiled=True)]
    all_gather x1 -> x0, waiting for transfers between devices: 44.4 us -> none  [body(): lax.all_gather(arrived_rows, 'tile', axis=0, tiled=True)]
    ppermute x0 -> x14, starting transfers between devices: none -> 24.1 us  [the longest x7 15.6 us: body(): send = lambda v, steps: lax.ppermute(v, COLUMN, column_shift(steps))]
    ppermute x0 -> x14, waiting for transfers between devices: none -> 19.4 us  [the longest x6 9.35 us: body(): lax.ppermute(v, PLANE, plane_shift(step, axis))]
    all_to_all x1 -> x0, blocking collectives: 15.6 us -> none  [body(): lax.all_to_all(send_rows, 'owner', split_axis=0, concat_axis=0, tiled=True)]
    dot_general x1 -> x0, matrix products: 12.1 us -> none  [earlier_match(): lax.dot_general(query_rows, piece_rows, (((1,), (1,)), ((), ())), preferr...]
    pallas_call x0 -> x8, Pallas kernels: none -> 11.5 us  [call(): pl.pallas_call(kernel, out_shape=out, in_specs=[space(i, smem) for i in r...]
    gather x4 -> x0, local copies, waits for them, and re-layouts: 10.5 us -> none  [the longest x1 3.62 us: body(): send_ids = jnp.where(filled, cluster_id[source_row], -1)]
  transfers between devices with their start and end apart: 4 -> 15, of which waited for: 4 -> 10; matrix products, arithmetic and copies ran while one was open for 2% -> 0% of each run, Pallas kernels for 0% -> 7%
where the time goes in v1:
time: 78.9 us; the launch traced here: 78.6 us
  starting transfers between devices  35.1 us (44%)
  waiting for transfers between devices  28.6 us (36%)
  Pallas kernels  11.5 us (15%)
  local copies, waits for them, and re-layouts  1.93 us (2%)
  between operations  1.46 us (2%)
    ppermute x7, starting transfers between devices, body(): send = lambda v, steps: lax.ppermute(v, COLUMN, column_shift(steps))  15.6 us
    pallas_call x8, Pallas kernels, call(): pl.pallas_call(kernel, out_shape=out, in_specs=[space(i, smem) for i in r...  11.5 us
    all_to_all x1, starting transfers between devices, body(): lax.all_to_all(message, RETURN, split_axis=0, concat_axis=0, tiled=True)  11 us
    ppermute x6, waiting for transfers between devices, body(): lax.ppermute(v, PLANE, plane_shift(step, axis))  9.35 us
    all_to_all x1, waiting for transfers between devices, body(): lax.all_to_all(message, RETURN, split_axis=0, concat_axis=0, tiled=True)  9.17 us
    ppermute x7, waiting for transfers between devices, body(): send = lambda v, steps: lax.ppermute(v, COLUMN, column_shift(steps))  8.27 us
    ppermute x6, starting transfers between devices, body(): lax.ppermute(v, PLANE, plane_shift(step, axis))  7.3 us
    unnamed x8, local copies, waits for them, and re-layouts  1.92 us
  transfers between devices with their start and end apart: 15, of which 10 were waited for; matrix products, arithmetic and copies ran while one was open for 0% of the time, Pallas kernels for 7%

profile of v1, /device:TPU:1, one launch (start us, length us, event | category | flops | bytes accessed | tf_op | source)
XLA Modules:
  0.0 78.6 jit_solution(12103409588399856443)
XLA Ops:
  0.0 0.0 copy-start
  0.7 0.1 pad_add_fusion.place_ref
  0.8 0.0 copy-start.1
  0.8 0.7 copy-done.1
  1.5 0.0 copy-start.2
  1.5 0.7 copy-done.2
  2.1 0.9 %shard_map.48 = (bf16[384,256]{1,0:T(8,128)(2,1)S(1)}, bf16[384,128]{1,0:T(8,128)(2,1)S(1)}, s32[8,256]{1,0:T(8,128)S(1)}) custom-call(s32[3]{0:T(128)S(1)} %pad_add_fusion.place_ref, s32[1]{0:T(128)S(6)} %copy.25.count_ref, s32[1,256]{1,0:T(1,128)S(1)} %bitcast.21, s32[1,256]{1,0:T(1,128)S(1)} %bitcast.22), custom_call_target="tpu_custom_call" | custom-call | flops 141950976 | bytes 933888 | tf_op jit(solution)/shard_map/pallas_call | solution.py:57
  3.1 0.0 copy-done
  3.1 0.4 shard_map.49
  3.5 6.9 %collective-permute-start.2 = (bf16[96,896]{1,0:T(8,128)(2,1)S(1)}, bf16[96,896]{1,0:T(8,128)(2,1)S(1)}, u32[]{:S(2)}, u32[]{:S(2)}) collective-permute-start(bf16[96,896]{1,0:T(8,128)(2,1)S(1)} %get-tuple-element.75), channel_id=1, source_target_pairs={{0,8},{1,25},{4,12},{5,29},{8,16},{9,1},{12,20},{13,5},{16,24},{17... | collective-permute-start | bytes 516104 | tf_op jit(solution)/shard_map/ppermute | solution.py:382
  10.4 0.7 collective-permute-start.1
  11.2 0.5 collective-permute-start.3
  11.7 2.7 %collective-permute-start.5 = (bf16[48,896]{1,0:T(8,128)(2,1)S(1)}, bf16[48,896]{1,0:T(8,128)(2,1)S(1)}, u32[]{:S(2)}, u32[]{:S(2)}) collective-permute-start(bf16[48,896]{1,0:T(8,128)(2,1)S(1)} %get-tuple-element.77), channel_id=1, source_target_pairs={{0,20},{1,13},{4,24},{5,17},{8,28},{9,21},{12,0},{13,25},{16,4},{1... | collective-permute-start | bytes 258056 | tf_op jit(solution)/shard_map/ppermute | solution.py:382
  14.4 2.4 %collective-permute-start.6 = (bf16[48,896]{1,0:T(8,128)(2,1)S(1)}, bf16[48,896]{1,0:T(8,128)(2,1)S(1)}, u32[]{:S(2)}, u32[]{:S(2)}) collective-permute-start(bf16[48,896]{1,0:T(8,128)(2,1)S(1)} %get-tuple-element.78), channel_id=1, source_target_pairs={{0,24},{1,9},{4,28},{5,13},{8,0},{9,17},{12,4},{13,21},{16,8},{17,... | collective-permute-start | bytes 258056 | tf_op jit(solution)/shard_map/ppermute | solution.py:382
  16.8 0.0 collective-permute-done.2.refs_2_
  16.8 0.0 collective-permute-start.7
  16.9 0.9 %collective-permute-done.1.refs_1_ = bf16[48,896]{1,0:T(8,128)(2,1)S(1)} collective-permute-done((bf16[48,896]{1,0:T(8,128)(2,1)S(1)}, bf16[48,896]{1,0:T(8,128)(2,1)S(1)}, u32[]{:S(2)}, u32[]{:S(2)}) %collective-permute-start.1) | collective-permute-done | bytes 86048 | tf_op jit(solution)/shard_map/ppermute | solution.py:382
  17.8 2.3 %collective-permute-start.4 = (bf16[48,896]{1,0:T(8,128)(2,1)S(1)}, bf16[48,896]{1,0:T(8,128)(2,1)S(1)}, u32[]{:S(2)}, u32[]{:S(2)}) collective-permute-start(bf16[48,896]{1,0:T(8,128)(2,1)S(1)} %slice.59), channel_id=1, source_target_pairs={{0,8},{1,25},{4,12},{5,29},{8,16},{9,1},{12,20},{13,5},{16,24},{17... | collective-permute-start | bytes 258056 | tf_op jit(solution)/shard_map/ppermute | solution.py:382
  20.1 1.6 %collective-permute-done.3.refs_3_ = bf16[48,896]{1,0:T(8,128)(2,1)S(1)} collective-permute-done((bf16[48,896]{1,0:T(8,128)(2,1)S(1)}, bf16[48,896]{1,0:T(8,128)(2,1)S(1)}, u32[]{:S(2)}, u32[]{:S(2)}) %collective-permute-start.3) | collective-permute-done | bytes 86048 | tf_op jit(solution)/shard_map/ppermute | solution.py:382
  21.7 0.0 collective-permute-done.5.refs_5_
  21.7 1.9 %collective-permute-done.6.refs_6_ = bf16[48,896]{1,0:T(8,128)(2,1)S(1)} collective-permute-done((bf16[48,896]{1,0:T(8,128)(2,1)S(1)}, bf16[48,896]{1,0:T(8,128)(2,1)S(1)}, u32[]{:S(2)}, u32[]{:S(2)}) %collective-permute-start.6) | collective-permute-done | bytes 86048 | tf_op jit(solution)/shard_map/ppermute | solution.py:382
  23.5 3.9 %collective-permute-done.7.refs_7_ = bf16[48,896]{1,0:T(8,128)(2,1)S(1)} collective-permute-done((bf16[48,896]{1,0:T(8,128)(2,1)S(1)}, bf16[48,896]{1,0:T(8,128)(2,1)S(1)}, u32[]{:S(2)}, u32[]{:S(2)}) %collective-permute-start.7) | collective-permute-done | bytes 86048 | tf_op jit(solution)/shard_map/ppermute | solution.py:382
  27.4 0.0 collective-permute-done.4.refs_4_
  27.4 0.1 shard_map.50.refs_0_
  27.5 1.2 %collective-permute-start.8 = (bf16[384,896]{1,0:T(8,128)(2,1)S(1)}, bf16[384,896]{1,0:T(8,128)(2,1)S(1)}, u32[]{:S(2)}, u32[]{:S(2)}) collective-permute-start(bf16[384,896]{1,0:T(8,128)(2,1)S(1)} %shard_map.50.refs_0_), channel_id=1, source_target_pairs={{0,1},{1,0},{2,3},{3,2},{4,5},{5,4},{6,7},{7,6},{8,9},{9,8},{10,11... | collective-permute-start | bytes 2064392 | tf_op jit(solution)/shard_map/ppermute | solution.py:399
  28.7 1.8 %collective-permute-done.8.refs_1_ = bf16[384,896]{1,0:T(8,128)(2,1)S(1)} collective-permute-done((bf16[384,896]{1,0:T(8,128)(2,1)S(1)}, bf16[384,896]{1,0:T(8,128)(2,1)S(1)}, u32[]{:S(2)}, u32[]{:S(2)}) %collective-permute-start.8) | collective-permute-done | bytes 688160 | tf_op jit(solution)/shard_map/ppermute | solution.py:399
  30.5 1.5 %shard_map.51.own = bf16[304,768]{1,0:T(8,128)(2,1)S(1)} custom-call(s32[3]{0:T(128)S(1)} %pad_add_fusion.place_ref, bf16[384,896]{1,0:T(8,128)(2,1)S(1)} %shard_map.50.refs_0_, bf16[384,896]{1,0:T(8,128)(2,1)S(1)} %collective-permute-done.8.refs_1_), custom_call_target="tpu_custom_call" | custom-call | flops 141950976 | bytes 933888 | tf_op jit(solution)/shard_map/pallas_call | solution.py:57
  32.0 1.4 %collective-permute-start.9 = (bf16[304,768]{1,0:T(8,128)(2,1)S(1)}, bf16[304,768]{1,0:T(8,128)(2,1)S(1)}, u32[]{:S(2)}, u32[]{:S(2)}) collective-permute-start(bf16[304,768]{1,0:T(8,128)(2,1)S(1)} %shard_map.51.own), channel_id=1, source_target_pairs={{32,0},{96,64},{160,128},{224,192},{2,32},{66,96},{130,160},{194,2... | collective-permute-start | bytes 1400840 | tf_op jit(solution)/shard_map/ppermute | solution.py:409
  33.4 1.2 %collective-permute-start.11 = (bf16[304,768]{1,0:T(8,128)(2,1)S(1)}, bf16[304,768]{1,0:T(8,128)(2,1)S(1)}, u32[]{:S(2)}, u32[]{:S(2)}) collective-permute-start(bf16[304,768]{1,0:T(8,128)(2,1)S(1)} %shard_map.51.own), channel_id=1, source_target_pairs={{64,0},{128,64},{192,128},{0,192},{96,32},{160,96},{224,160},{32,2... | collective-permute-start | bytes 1400840 | tf_op jit(solution)/shard_map/ppermute | solution.py:409
  34.6 1.5 %collective-permute-start.10 = (bf16[304,768]{1,0:T(8,128)(2,1)S(1)}, bf16[304,768]{1,0:T(8,128)(2,1)S(1)}, u32[]{:S(2)}, u32[]{:S(2)}) collective-permute-start(bf16[304,768]{1,0:T(8,128)(2,1)S(1)} %shard_map.51.own), channel_id=1, source_target_pairs={{34,0},{98,64},{162,128},{226,192},{0,32},{64,96},{128,160},{192,2... | collective-permute-start | bytes 1400840 | tf_op jit(solution)/shard_map/ppermute | solution.py:409
  36.1 1.5 %collective-permute-start.12 = (bf16[304,768]{1,0:T(8,128)(2,1)S(1)}, bf16[304,768]{1,0:T(8,128)(2,1)S(1)}, u32[]{:S(2)}, u32[]{:S(2)}) collective-permute-start(bf16[304,768]{1,0:T(8,128)(2,1)S(1)} %shard_map.51.own), channel_id=1, source_target_pairs={{192,0},{0,64},{64,128},{128,192},{224,32},{32,96},{96,160},{160,2... | collective-permute-start | bytes 1400840 | tf_op jit(solution)/shard_map/ppermute | solution.py:409
  37.6 3.2 %collective-permute-done.9.a_first = bf16[304,768]{1,0:T(8,128)(2,1)S(1)} collective-permute-done((bf16[304,768]{1,0:T(8,128)(2,1)S(1)}, bf16[304,768]{1,0:T(8,128)(2,1)S(1)}, u32[]{:S(2)}, u32[]{:S(2)}) %collective-permute-start.9) | collective-permute-done | bytes 466976 | tf_op jit(solution)/shard_map/ppermute | solution.py:409
  40.8 0.3 collective-permute-start.13
  41.1 0.9 %collective-permute-done.11.b_first = bf16[304,768]{1,0:T(8,128)(2,1)S(1)} collective-permute-done((bf16[304,768]{1,0:T(8,128)(2,1)S(1)}, bf16[304,768]{1,0:T(8,128)(2,1)S(1)}, u32[]{:S(2)}, u32[]{:S(2)}) %collective-permute-start.11) | collective-permute-done | bytes 466976 | tf_op jit(solution)/shard_map/ppermute | solution.py:409
  42.0 1.4 %collective-permute-start.14 = (bf16[304,768]{1,0:T(8,128)(2,1)S(1)}, bf16[304,768]{1,0:T(8,128)(2,1)S(1)}, u32[]{:S(2)}, u32[]{:S(2)}) collective-permute-start(bf16[304,768]{1,0:T(8,128)(2,1)S(1)} %collective-permute-done.11.b_first), channel_id=1, source_target_pairs={{64,0},{128,64},{192,128},{0,192},{96,32},{160,96},{224,160},{32,2... | collective-permute-start | bytes 1400840 | tf_op jit(solution)/shard_map/ppermute | solution.py:409
  43.4 2.8 %collective-permute-done.10.a_second = bf16[304,768]{1,0:T(8,128)(2,1)S(1)} collective-permute-done((bf16[304,768]{1,0:T(8,128)(2,1)S(1)}, bf16[304,768]{1,0:T(8,128)(2,1)S(1)}, u32[]{:S(2)}, u32[]{:S(2)}) %collective-permute-start.10) | collective-permute-done | bytes 466976 | tf_op jit(solution)/shard_map/ppermute | solution.py:409
  46.2 0.0 collective-permute-done.12.b_second
  46.2 3.7 %shard_map.52 = (f32[8,384]{1,0:T(8,128)S(1)}, f32[3,304,128]{2,1,0:T(8,128)S(1)}, s32[48,128]{1,0:T(8,128)S(1)}) custom-call(s32[3]{0:T(128)S(1)} %pad_add_fusion.place_ref, bf16[304,768]{1,0:T(8,128)(2,1)S(1)} %shard_map.51.own, bf16[304,768]{1,0:T(8,128)(2,1)S(1)} %collective-permute-done.9.a_first, ...), custom_call_target="tpu_custom_call" | custom-call | flops 1277558784 | bytes 933888 | tf_op jit(solution)/shard_map/pallas_call | solution.py:57
  49.9 2.5 %collective-permute-done.13.a_far = bf16[304,768]{1,0:T(8,128)(2,1)S(1)} collective-permute-done((bf16[304,768]{1,0:T(8,128)(2,1)S(1)}, bf16[304,768]{1,0:T(8,128)(2,1)S(1)}, u32[]{:S(2)}, u32[]{:S(2)}) %collective-permute-start.13) | collective-permute-done | bytes 466976 | tf_op jit(solution)/shard_map/ppermute | solution.py:409
  52.3 1.6 %shard_map.53 = (f32[8,384]{1,0:T(8,128)S(1)}, f32[304,128]{1,0:T(8,128)S(1)}, s32[16,128]{1,0:T(8,128)S(1)}) custom-call(s32[3]{0:T(128)S(1)} %pad_add_fusion.place_ref, bf16[304,768]{1,0:T(8,128)(2,1)S(1)} %shard_map.51.own, bf16[304,768]{1,0:T(8,128)(2,1)S(1)} %collective-permute-done.9.a_first, bf16[304,768]{1,0:T(8,128)(2,1)S(1)} %collective-permute-done.10.a_second, ...), custom_call_target="tpu_custom_call" | custom-call | flops 425852928 | bytes 933888 | tf_op jit(solution)/shard_map/pallas_call | solution.py:57
  53.9 0.0 collective-permute-done.14.b_far
  53.9 2.6 %shard_map.54 = f32[64,1,128]{2,1,0:T(1,128)} custom-call(s32[3]{0:T(128)S(1)} %pad_add_fusion.place_ref, bf16[304,768]{1,0:T(8,128)(2,1)S(1)} %shard_map.51.own, bf16[304,768]{1,0:T(8,128)(2,1)S(1)} %collective-permute-done.9.a_first, bf16[304,768]{1,0:T(8,128)(2,1)S(1)} %collective-permute-done.10.a_second, ...), custom_call_target="tpu_custom_call" | custom-call | flops 567803904 | bytes 933888 | tf_op jit(solution)/shard_map/pallas_call | solution.py:57
  56.5 11.0 %all-to-all-start.1 = ((f32[64,1,128]{2,1,0:T(1,128)}), f32[64,1,128]{2,1,0:T(1,128)S(1)}, u32[]{:S(2)}, u32[]{:S(2)}) async-start(f32[64,1,128]{2,1,0:T(1,128)} %shard_map.54), calls=%async_computation.1 | async-start | bytes 65536 | tf_op jit(solution)/shard_map/all_to_all | solution.py:450
  67.5 9.2 %all-to-all-done.1.ans_ref = f32[64,1,128]{2,1,0:T(1,128)S(1)} async-done(((f32[64,1,128]{2,1,0:T(1,128)}), f32[64,1,128]{2,1,0:T(1,128)S(1)}, u32[]{:S(2)}, u32[]{:S(2)}) %all-to-all-start.1) | async-done | bytes 32800 | tf_op jit(solution)/shard_map/all_to_all | solution.py:450
  76.7 0.7 shard_map.55
  78.0 0.0 copy-start.3
  78.0 0.6 copy-done.3
  (2 shorter events, 0.0 us)
Async XLA Ops:
  0.0 3.1 %copy-start = (bf16[256,768]{1,0:T(8,128)(2,1)S(1)}, bf16[256,768]{1,0:T(8,128)(2,1)}, u32[]{:S(2)}) copy-start(bf16[256,768]{1,0:T(8,128)(2,1)} %emb_ref.1) | copy-start | bytes 1179652
  0.8 0.7 copy-start.1
  1.5 0.7 copy-start.2
  3.5 13.3 %collective-permute-start.2 = (bf16[96,896]{1,0:T(8,128)(2,1)S(1)}, bf16[96,896]{1,0:T(8,128)(2,1)S(1)}, u32[]{:S(2)}, u32[]{:S(2)}) collective-permute-start(bf16[96,896]{1,0:T(8,128)(2,1)S(1)} %get-tuple-element.75), channel_id=1, source_target_pairs={{0,8},{1,25},{4,12},{5,29},{8,16},{9,1},{12,20},{13,5},{16,24},{17... | collective-permute-start | bytes 516104 | tf_op jit(solution)/shard_map/ppermute | solution.py:382
  10.4 7.3 %collective-permute-start.1 = (bf16[48,896]{1,0:T(8,128)(2,1)S(1)}, bf16[48,896]{1,0:T(8,128)(2,1)S(1)}, u32[]{:S(2)}, u32[]{:S(2)}) collective-permute-start(bf16[48,896]{1,0:T(8,128)(2,1)S(1)} %get-tuple-element.74), channel_id=1, source_target_pairs={{0,4},{1,29},{4,8},{5,1},{8,12},{9,5},{12,16},{13,9},{16,20},{17,1... | collective-permute-start | bytes 258056 | tf_op jit(solution)/shard_map/ppermute | solution.py:382
  11.2 10.5 %collective-permute-start.3 = (bf16[48,896]{1,0:T(8,128)(2,1)S(1)}, bf16[48,896]{1,0:T(8,128)(2,1)S(1)}, u32[]{:S(2)}, u32[]{:S(2)}) collective-permute-start(bf16[48,896]{1,0:T(8,128)(2,1)S(1)} %get-tuple-element.76), channel_id=1, source_target_pairs={{0,12},{1,21},{4,16},{5,25},{8,20},{9,29},{12,24},{13,1},{16,28},{... | collective-permute-start | bytes 258056 | tf_op jit(solution)/shard_map/ppermute | solution.py:382
  11.7 10.0 %collective-permute-start.5 = (bf16[48,896]{1,0:T(8,128)(2,1)S(1)}, bf16[48,896]{1,0:T(8,128)(2,1)S(1)}, u32[]{:S(2)}, u32[]{:S(2)}) collective-permute-start(bf16[48,896]{1,0:T(8,128)(2,1)S(1)} %get-tuple-element.77), channel_id=1, source_target_pairs={{0,20},{1,13},{4,24},{5,17},{8,28},{9,21},{12,0},{13,25},{16,4},{1... | collective-permute-start | bytes 258056 | tf_op jit(solution)/shard_map/ppermute | solution.py:382
  14.4 9.1 %collective-permute-start.6 = (bf16[48,896]{1,0:T(8,128)(2,1)S(1)}, bf16[48,896]{1,0:T(8,128)(2,1)S(1)}, u32[]{:S(2)}, u32[]{:S(2)}) collective-permute-start(bf16[48,896]{1,0:T(8,128)(2,1)S(1)} %get-tuple-element.78), channel_id=1, source_target_pairs={{0,24},{1,9},{4,28},{5,13},{8,0},{9,17},{12,4},{13,21},{16,8},{17,... | collective-permute-start | bytes 258056 | tf_op jit(solution)/shard_map/ppermute | solution.py:382
  16.8 10.6 %collective-permute-start.7 = (bf16[48,896]{1,0:T(8,128)(2,1)S(1)}, bf16[48,896]{1,0:T(8,128)(2,1)S(1)}, u32[]{:S(2)}, u32[]{:S(2)}) collective-permute-start(bf16[48,896]{1,0:T(8,128)(2,1)S(1)} %get-tuple-element.79), channel_id=1, source_target_pairs={{0,28},{1,5},{4,0},{5,9},{8,4},{9,13},{12,8},{13,17},{16,12},{17,2... | collective-permute-start | bytes 258056 | tf_op jit(solution)/shard_map/ppermute | solution.py:382
  17.8 9.7 %collective-permute-start.4 = (bf16[48,896]{1,0:T(8,128)(2,1)S(1)}, bf16[48,896]{1,0:T(8,128)(2,1)S(1)}, u32[]{:S(2)}, u32[]{:S(2)}) collective-permute-start(bf16[48,896]{1,0:T(8,128)(2,1)S(1)} %slice.59), channel_id=1, source_target_pairs={{0,8},{1,25},{4,12},{5,29},{8,16},{9,1},{12,20},{13,5},{16,24},{17... | collective-permute-start | bytes 258056 | tf_op jit(solution)/shard_map/ppermute | solution.py:382
  27.5 3.0 %collective-permute-start.8 = (bf16[384,896]{1,0:T(8,128)(2,1)S(1)}, bf16[384,896]{1,0:T(8,128)(2,1)S(1)}, u32[]{:S(2)}, u32[]{:S(2)}) collective-permute-start(bf16[384,896]{1,0:T(8,128)(2,1)S(1)} %shard_map.50.refs_0_), channel_id=1, source_target_pairs={{0,1},{1,0},{2,3},{3,2},{4,5},{5,4},{6,7},{7,6},{8,9},{9,8},{10,11... | collective-permute-start | bytes 2064392 | tf_op jit(solution)/shard_map/ppermute | solution.py:399
  32.0 8.8 %collective-permute-start.9 = (bf16[304,768]{1,0:T(8,128)(2,1)S(1)}, bf16[304,768]{1,0:T(8,128)(2,1)S(1)}, u32[]{:S(2)}, u32[]{:S(2)}) collective-permute-start(bf16[304,768]{1,0:T(8,128)(2,1)S(1)} %shard_map.51.own), channel_id=1, source_target_pairs={{32,0},{96,64},{160,128},{224,192},{2,32},{66,96},{130,160},{194,2... | collective-permute-start | bytes 1400840 | tf_op jit(solution)/shard_map/ppermute | solution.py:409
  33.4 8.6 %collective-permute-start.11 = (bf16[304,768]{1,0:T(8,128)(2,1)S(1)}, bf16[304,768]{1,0:T(8,128)(2,1)S(1)}, u32[]{:S(2)}, u32[]{:S(2)}) collective-permute-start(bf16[304,768]{1,0:T(8,128)(2,1)S(1)} %shard_map.51.own), channel_id=1, source_target_pairs={{64,0},{128,64},{192,128},{0,192},{96,32},{160,96},{224,160},{32,2... | collective-permute-start | bytes 1400840 | tf_op jit(solution)/shard_map/ppermute | solution.py:409
  34.6 11.6 %collective-permute-start.10 = (bf16[304,768]{1,0:T(8,128)(2,1)S(1)}, bf16[304,768]{1,0:T(8,128)(2,1)S(1)}, u32[]{:S(2)}, u32[]{:S(2)}) collective-permute-start(bf16[304,768]{1,0:T(8,128)(2,1)S(1)} %shard_map.51.own), channel_id=1, source_target_pairs={{34,0},{98,64},{162,128},{226,192},{0,32},{64,96},{128,160},{192,2... | collective-permute-start | bytes 1400840 | tf_op jit(solution)/shard_map/ppermute | solution.py:409
  36.1 10.1 %collective-permute-start.12 = (bf16[304,768]{1,0:T(8,128)(2,1)S(1)}, bf16[304,768]{1,0:T(8,128)(2,1)S(1)}, u32[]{:S(2)}, u32[]{:S(2)}) collective-permute-start(bf16[304,768]{1,0:T(8,128)(2,1)S(1)} %shard_map.51.own), channel_id=1, source_target_pairs={{192,0},{0,64},{64,128},{128,192},{224,32},{32,96},{96,160},{160,2... | collective-permute-start | bytes 1400840 | tf_op jit(solution)/shard_map/ppermute | solution.py:409
  40.8 11.6 %collective-permute-start.13 = (bf16[304,768]{1,0:T(8,128)(2,1)S(1)}, bf16[304,768]{1,0:T(8,128)(2,1)S(1)}, u32[]{:S(2)}, u32[]{:S(2)}) collective-permute-start(bf16[304,768]{1,0:T(8,128)(2,1)S(1)} %collective-permute-done.9.a_first), channel_id=1, source_target_pairs={{32,0},{96,64},{160,128},{224,192},{2,32},{66,96},{130,160},{194,2... | collective-permute-start | bytes 1400840 | tf_op jit(solution)/shard_map/ppermute | solution.py:409
  42.0 11.9 %collective-permute-start.14 = (bf16[304,768]{1,0:T(8,128)(2,1)S(1)}, bf16[304,768]{1,0:T(8,128)(2,1)S(1)}, u32[]{:S(2)}, u32[]{:S(2)}) collective-permute-start(bf16[304,768]{1,0:T(8,128)(2,1)S(1)} %collective-permute-done.11.b_first), channel_id=1, source_target_pairs={{64,0},{128,64},{192,128},{0,192},{96,32},{160,96},{224,160},{32,2... | collective-permute-start | bytes 1400840 | tf_op jit(solution)/shard_map/ppermute | solution.py:409
  56.5 20.1 %all-to-all-start.1 = ((f32[64,1,128]{2,1,0:T(1,128)}), f32[64,1,128]{2,1,0:T(1,128)S(1)}, u32[]{:S(2)}, u32[]{:S(2)}) async-start(f32[64,1,128]{2,1,0:T(1,128)} %shard_map.54), calls=%async_computation.1 | async-start | bytes 65536 | tf_op jit(solution)/shard_map/all_to_all | solution.py:450
  78.0 0.6 copy-start.3

commit v2 on v1

v2 whole, which is shorter than its diff:
```python
import functools

import jax
import jax.numpy as jnp
from jax import lax
from jax.experimental import pallas as pl
from jax.experimental.pallas import tpu as pltpu
from jax.sharding import Mesh, PartitionSpec as P

norm_eps = 1e-06
ROWS = 256
WIDTH = 768
META = 128
GROUPS = 8
SLOTS = 48
ROUTED = GROUPS * SLOTS
CAP = 304
HELD = CAP - 3
CAPL = 384
LAST = CAP - 16
NEVER = 512.0
CHUNKS = WIDTH // META
PIECE = CHUNKS * SLOTS + 16
MARKS = 32
PIECES = (1, 1, 2, 1, 1, 1, 1)
OVER = 100.0
VMEM_LIMIT = 50 * 1024 * 1024
PLANE = ("y", "xl", "xh", "core")
COLUMN = ("z", "core")
RETURN = ("xl", "z", "xh", "core")


def dot(a, b, contract):
    return lax.dot_general(a, b, (contract, ((), ())), preferred_element_type=jnp.float32)


def iota(shape, axis):
    return lax.broadcasted_iota(jnp.int32, shape, axis)


def split3(v):
    hi = v.astype(jnp.bfloat16)
    rest = v - hi.astype(jnp.float32)
    mid = rest.astype(jnp.bfloat16)
    low = (rest - mid.astype(jnp.float32)).astype(jnp.bfloat16)
    return hi, mid, low


def pick_rows(v, one_hot):
    n = v.shape[0]
    parts = dot(jnp.concatenate(split3(v), axis=0), one_hot, ((1,), (0,)))
    return (parts[:n] + parts[n : 2 * n]) + parts[2 * n :]


def call(kernel, out, *args, smem=(), smem_out=(), cost=1, scratch=()):
    space = lambda i, scalars: pl.BlockSpec(memory_space=pltpu.SMEM if i in scalars else pltpu.VMEM)
    out_specs = space(0, smem_out)
    if isinstance(out, tuple):
        out_specs = tuple(space(i, smem_out) for i in range(len(out)))
    return pl.pallas_call(
        kernel,
        out_shape=out,
        in_specs=[space(i, smem) for i in range(len(args))],
        out_specs=out_specs,
        scratch_shapes=list(scratch),
        cost_estimate=pl.CostEstimate(
            flops=2 * cost * CAP * CAP * WIDTH, bytes_accessed=4 * CAP * WIDTH, transcendentals=0
        ),
        compiler_params=pltpu.CompilerParams(vmem_limit_bytes=VMEM_LIMIT),
    )(*args)


def signed(core, value):
    return jnp.where(core == 0, value, -value)


def prep_kernel(count_ref, emb_ref, id_ref, rank_ref, *out_refs):
    slot_ref = out_refs[-1]
    x = emb_ref[...].astype(jnp.float32)
    unit = (x * lax.rsqrt(jnp.sum(x * x, axis=1, keepdims=True) + norm_eps)).astype(jnp.bfloat16)
    ids = id_ref[...]
    ranks = rank_ref[...]
    live = iota((1, ROWS), 1) < count_ref[0]
    target = ids & (GROUPS - 1)
    chosen = jnp.where((iota((GROUPS, ROWS), 0) == target) & live, 1.0, 0.0)
    upper = jnp.where(iota((ROWS, ROWS), 0) < iota((ROWS, ROWS), 1), 1.0, 0.0).astype(jnp.bfloat16)
    before = dot(chosen.astype(jnp.bfloat16), upper, ((1,), (0,)))
    within = jnp.sum(before * chosen, axis=0, keepdims=True).astype(jnp.int32)
    steps = signed(lax.axis_index("core"), target - lax.axis_index("z")) & (GROUPS - 1)
    at = jnp.where(steps == 3, 4, jnp.where(steps == 4, 3, steps))
    slot = jnp.where(live, at * SLOTS + within, -1)
    where_to = jnp.where(iota((ROUTED, ROWS), 0) == slot, 1.0, 0.0).astype(jnp.bfloat16)
    high = ranks >> 8
    row = iota((16, ROWS), 0)
    meta = jnp.where(
        row == 0, ids + 1, jnp.where(row == 1, high, jnp.where(row == 2, ranks - (high << 8), 0))
    )
    meta = meta.astype(jnp.float32).astype(jnp.bfloat16)
    rows = dot(where_to, unit, ((1,), (0,))).astype(jnp.bfloat16)
    marks = dot(meta, where_to, ((1,), (1,)))
    at = 0
    for ref in out_refs[:-1]:
        for first in range(0, ref.shape[0], PIECE):
            for i in range(CHUNKS):
                ref[first + i * SLOTS : first + (i + 1) * SLOTS, :] = rows[
                    at : at + SLOTS, i * META : (i + 1) * META
                ]
            tail = jnp.concatenate(
                [marks[:, at : at + SLOTS], jnp.zeros((16, META - SLOTS), jnp.float32)], axis=1
            )
            ref[first + CHUNKS * SLOTS : first + PIECE, :] = tail.astype(jnp.bfloat16)
            at += SLOTS
    slot_ref[0:1, :] = jnp.where(live, target, -1)
    slot_ref[1:2, :] = within
    slot_ref[2:8, :] = jnp.zeros((6, ROWS), jnp.int32)


def collect_kernel(*refs):
    out_ref = refs[-1]
    marks = []
    for j, ref in enumerate(refs[:-1]):
        for i in range(CHUNKS):
            out_ref[j * SLOTS : (j + 1) * SLOTS, i * META : (i + 1) * META] = ref[
                i * SLOTS : (i + 1) * SLOTS, :
            ]
        marks.append(ref[CHUNKS * SLOTS : PIECE, :].astype(jnp.float32))
    by_kind = [mark[i : i + 1, :] for i in range(3) for mark in marks]
    kinds = jnp.concatenate(by_kind + [jnp.zeros((MARKS - 3 * GROUPS, META), jnp.float32)], axis=0)
    out_ref[ROUTED:, :META] = kinds.astype(jnp.bfloat16)
    out_ref[ROUTED:, META:] = jnp.zeros((MARKS, WIDTH - META), jnp.bfloat16)


def slot_fold(both):
    slot = iota((both, META), 0)
    slot = slot - SLOTS * ((slot * 1366) >> 16)
    return jnp.where(slot == iota((both, META), 1), 1.0, 0.0).astype(jnp.bfloat16)


def place_rows(arrived_ref, first):
    marks = arrived_ref[ROUTED:, :META]
    spread = dot(marks, slot_fold(ROUTED), ((1,), (1,)))
    here = iota((GROUPS, ROUTED), 0) == ((iota((GROUPS, ROUTED), 1) * 1366) >> 16)
    meta = [
        jnp.sum(jnp.where(here, spread[GROUPS * i : GROUPS * (i + 1), :], 0.0), axis=0, keepdims=True)
        for i in range(3)
    ]
    mine = lax.axis_index("z") + GROUPS * lax.axis_index("core") + 1
    ones = jnp.where(meta[0] == mine.astype(jnp.float32), 1.0, 0.0)
    chunks = [ones[:, i : i + META] for i in range(0, ROUTED, META)]
    upper = jnp.where(iota((META, META), 0) < iota((META, META), 1), 1.0, 0.0).astype(jnp.bfloat16)
    stacked = jnp.concatenate(chunks + [jnp.zeros((8 - len(chunks), META), jnp.float32)], axis=0)
    before = dot(stacked.astype(jnp.bfloat16), upper, ((1,), (0,)))
    total, counted = first, []
    for i, chunk in enumerate(chunks):
        counted.append(jnp.where(chunk > 0.5, before[i : i + 1, :] + total, -1.0))
        total = total + jnp.sum(chunk, axis=1, keepdims=True)
    pos = jnp.concatenate(counted, axis=1).astype(jnp.int32)
    where_to = jnp.where((iota((CAPL, ROUTED), 0) == pos) & (pos < HELD), 1.0, 0.0).astype(jnp.bfloat16)
    meta = jnp.concatenate(meta + [jnp.zeros((5, ROUTED), jnp.float32)], axis=0)
    ranks = dot(meta.astype(jnp.bfloat16), where_to, ((1,), (1,)))
    return pos, where_to, ranks, total


def first_kernel(own_ref, rows_ref, pos_ref, ranks_ref, total_ref):
    pos, where_to, ranks, total = place_rows(own_ref, jnp.zeros((1, 1), jnp.float32))
    rows_ref[...] = dot(where_to[:CAP, :], own_ref[:ROUTED, :], ((1,), (0,))).astype(jnp.bfloat16)
    pos_ref[...] = jnp.broadcast_to(pos, (8, ROUTED))
    ranks_ref[...] = ranks
    total_ref[...] = jnp.broadcast_to(total, (8, META))


def compact_kernel(other_ref, rows_ref, pos_ref, ranks_ref, total_ref, block_ref):
    other_pos, where_to, other_ranks, total = place_rows(other_ref, total_ref[0:1, 0:1])
    rows = dot(where_to[:CAP, :], other_ref[:ROUTED, :], ((1,), (0,))) + rows_ref[...].astype(jnp.float32)
    pos = jnp.concatenate([pos_ref[0:1, :], other_pos], axis=1)
    ranks = ranks_ref[...] + other_ranks
    lane = iota((1, CAPL), 1)
    filled = (lane.astype(jnp.float32) < total) & (lane < HELD)
    high = jnp.where(filled, ranks[1:2, :], NEVER)
    high = jnp.where((lane == CAPL - 1) & (total > HELD), 2 * NEVER, high)
    low = jnp.where(filled, ranks[2:3, :], 0.0)
    place = pos + 1
    marks = (jnp.concatenate([high, low], axis=1), (place >> 8).astype(jnp.float32), (place & 255).astype(jnp.float32))
    row = iota((16, WIDTH), 0)
    last = rows[LAST:, :]
    for i, mark in enumerate(marks):
        last = jnp.where(row == 13 + i, mark, last)
    block_ref[:LAST, :] = rows[:LAST, :].astype(jnp.bfloat16)
    block_ref[LAST:, :] = last.astype(jnp.bfloat16)


def row_ranks(block):
    tail = block[LAST:, :].astype(jnp.float32)
    return (256.0 * tail[13:14, :CAPL] + tail[13:14, CAPL:])[:, :CAP]


def column_ranks(block, eye):
    high = dot(eye, block[LAST:, :CAPL], ((1,), (1,)))
    low = dot(eye, block[LAST:, CAPL:], ((1,), (1,)))
    return 256.0 * high[:, 13:14] + low[:, 13:14]


def slot_places(block):
    both = 2 * ROUTED
    tail = block[LAST:, :].astype(jnp.float32)
    first = iota((16, both), 0) * SLOTS
    lane = iota((16, both), 1)
    here = (lane >= first) & (lane < first + SLOTS)
    parts = jnp.concatenate([jnp.where(here, tail[i : i + 1, :], 0.0) for i in (14, 15)], axis=0)
    folded = dot(parts.astype(jnp.bfloat16), slot_fold(both), ((1,), (0,)))
    return (256.0 * folded[:16] + folded[16:]).astype(jnp.int32) - 1


def make_eye():
    return jnp.where(iota((CAP, CAPL), 0) == iota((CAP, CAPL), 1), 1.0, 0.0).astype(jnp.bfloat16)


def earlier_best(query, query_ranks, key, key_ranks):
    scores = dot(key[...], query[...], ((1,), (1,)))
    return jnp.max(jnp.where(key_ranks < query_ranks, scores, -1.0), axis=0, keepdims=True)


def own_kernel(own, best_ref, columns_ref, places_ref):
    columns = column_ranks(own, make_eye())
    columns_ref[...] = jnp.broadcast_to(columns, (CAP, META))
    best_ref[...] = jnp.full((8, CAPL), -1.0, jnp.float32)
    best_ref[0:1, :CAP] = earlier_best(own, row_ranks(own), own, columns)
    places_ref[...] = slot_places(own)


def near_kernel(
    own, x_first, x_second, y_first, y_second, own_best, own_columns, best_ref, columns_ref, places_ref
):
    eye = make_eye()
    ys = (y_first, y_second)
    columns = [column_ranks(key, eye) for key in ys]
    for i in range(2):
        columns_ref[i] = jnp.broadcast_to(columns[i], (CAP, META))
    best_ref[...] = own_best[...]
    for i, query in enumerate((own, x_first, x_second)):
        ranks = row_ranks(query)
        if i == 0:
            best = own_best[0:1, :CAP]
        else:
            best = earlier_best(query, ranks, own, own_columns[:, 0:1])
            places_ref[16 * (i - 1) : 16 * i, :] = slot_places(query)
        for key, ranked in zip(ys, columns):
            best = jnp.maximum(best, earlier_best(query, ranks, key, ranked))
        best_ref[i : i + 1, :CAP] = best


def mid_kernel(own, y_first, y_second, x_far, own_columns, columns_ref, out_ref, places_ref):
    ranks = row_ranks(x_far)
    best = earlier_best(x_far, ranks, own, own_columns[:, 0:1])
    for i, key in enumerate((y_first, y_second)):
        best = jnp.maximum(best, earlier_best(x_far, ranks, key, columns_ref[i, :, 0:1]))
    out_ref[...] = jnp.full((8, CAPL), -1.0, jnp.float32)
    out_ref[0:1, :CAP] = best
    places_ref[...] = slot_places(x_far)


def far_kernel(
    own, x_first, x_second, y_first, y_second, x_far, y_far,
    own_places, near_ref, near_places, mid_ref, mid_places, out_ref,
):
    queries, keys = (own, x_first, x_second, x_far), (y_first, y_second, y_far)
    far_columns = column_ranks(y_far, make_eye())
    over = 0.0
    for block in queries + keys:
        tail = block[LAST:, CAPL - META : CAPL].astype(jnp.float32)
        over = jnp.maximum(over, tail[13:14, META - 1 :])
    over = jnp.where(over > NEVER, 1.0, 0.0)
    my_core, my_z = lax.axis_index("core"), lax.axis_index("z")
    my_x = 2 * lax.axis_index("xh") + lax.axis_index("xl")
    rows = []
    for i, query in enumerate(queries):
        best = earlier_best(query, row_ranks(query), y_far, far_columns)
        best = jnp.maximum(best, near_ref[i : i + 1, :CAP] if i < 3 else mid_ref[0:1, :CAP])
        best = jnp.concatenate([best, jnp.full((1, CAPL - CAP), -1.0, jnp.float32)], axis=1)
        rows.append(jnp.broadcast_to(best, (16, CAPL)))
    rows = jnp.concatenate(rows, axis=0)
    places = jnp.concatenate([own_places[...], near_places[...], mid_places[...]], axis=0)
    found = jnp.full((64, META), -1.0, jnp.float32)
    for part in range(CAPL // META):
        values = rows[:, part * META : (part + 1) * META]
        picked = jnp.take_along_axis(values, places & (META - 1), axis=1, mode="promise_in_bounds")
        found = jnp.where((places >> 7) == part, picked, found)
    found = found + OVER * over
    messages = GROUPS * 8
    row, column = iota((messages, messages), 0), iota((messages, messages), 1)
    core = row & 1
    away = my_z - ((row >> 2) & 7)
    steps = jnp.where(core == 0, away, -away) & 7
    x_away = signed(my_core, (row >> 5) + (row & 2) - my_x) & 3
    block = jnp.where(x_away == 2, 3, jnp.where(x_away == 3, 2, x_away))
    wanted = block * 16 + (core ^ my_core) * GROUPS + steps
    order = jnp.where(column == wanted, 1.0, 0.0).astype(jnp.bfloat16)
    out = dot(jnp.concatenate([order] * 3, axis=1), jnp.concatenate(split3(found), axis=0), ((1,), (0,)))
    for i in range(messages):
        out_ref[i] = out[i : i + 1, :]


def final_kernel(slot_ref, ans_ref, out_ref, flag_ref):
    target, within = slot_ref[0:1, :], slot_ref[1:2, :]
    one_hot = jnp.where(iota((META, ROWS), 0) == within, 1.0, 0.0).astype(jnp.bfloat16)
    groups = []
    for g in range(GROUPS):
        rows = [ans_ref[xl * 32 + g * 4 + i] for xl in range(2) for i in range(4)]
        groups.append(functools.reduce(jnp.maximum, rows))
    best = jnp.concatenate(groups, axis=0)
    got = pick_rows(best, one_hot)
    out_ref[...] = jnp.sum(jnp.where(iota((GROUPS, ROWS), 0) == target, got, 0.0), axis=0, keepdims=True)
    flag_ref[0] = jnp.where(jnp.max(best) > 0.5 * OVER, 1, 0).astype(jnp.int32)


def slow_path(arrived, target, within, live):
    def unpack(v):
        marks = v[ROUTED : ROUTED + 3 * GROUPS, :SLOTS].astype(jnp.float32).reshape(3, ROUTED)
        return v[:ROUTED], marks[0], 256.0 * marks[1] + marks[2]

    rows, ids, ranks = unpack(arrived)
    ring = ("y", "xl", "xh", "core")
    size = 32

    def step(_, carry):
        moving, best = carry
        key_rows, key_ids, key_ranks = unpack(moving)
        scores = dot(rows, key_rows, ((1,), (1,)))
        allowed = (
            (ids[:, None] == key_ids[None, :])
            & (key_ids[None, :] > 0)
            & (key_ranks[None, :] < ranks[:, None])
        )
        best = jnp.maximum(best, jnp.max(jnp.where(allowed, scores, -1.0), axis=1))
        moving = lax.ppermute(moving, ring, [(i, (i + 1) % size) for i in range(size)])
        return moving, best

    _, best = lax.fori_loop(0, size, step, (arrived, jnp.full((ROUTED,), -1.0, jnp.float32)))
    steps = signed(lax.axis_index("core"), lax.axis_index("z") - jnp.arange(GROUPS)) & (GROUPS - 1)
    answered = lax.all_to_all(best.reshape(GROUPS, SLOTS)[steps], "z", 0, 0, tiled=True)
    picked = answered[jnp.maximum(target, 0), jnp.minimum(within, SLOTS - 1)]
    return jnp.where(live, picked, 0.0)


def column_shift(steps):
    pairs = []
    for z in range(8):
        for core in range(2):
            to = (z + (steps if core == 0 else -steps)) % 8
            pairs.append((z * 2 + core, to * 2 + core))
    return pairs


def plane_shift(dx, dy):
    def flat(x, y, core):
        return ((y % 4 * 2 + x % 4 % 2) * 2 + x % 4 // 2) * 2 + core

    pairs = []
    for core in range(2):
        s = 1 if core == 0 else -1
        for x in range(4):
            for y in range(4):
                pairs.append((flat(x + s * dx, y + s * dy, core), flat(x, y, core)))
    return pairs


def body(embeddings, cluster_id, order_rank, row_count):
    f32, bf16, i32 = jnp.float32, jnp.bfloat16, jnp.int32
    shape = jax.ShapeDtypeStruct
    *pieces, slots = call(
        prep_kernel,
        tuple(shape((n * PIECE, META), bf16) for n in PIECES) + (shape((8, ROWS), i32),),
        row_count,
        embeddings,
        cluster_id.reshape(1, ROWS),
        order_rank.reshape(1, ROWS),
        smem=(0,),
    )
    send = lambda v, steps: lax.ppermute(v, COLUMN, column_shift(steps))
    two_four = send(pieces[2], 2)
    three, five, six = send(pieces[3], 3), send(pieces[4], 5), send(pieces[5], 6)
    four = send(two_four[PIECE:], 2)
    one, seven = send(pieces[1], 1), send(pieces[6], 7)
    arrived = call(
        collect_kernel,
        shape((ROUTED + MARKS, WIDTH), bf16),
        pieces[0],
        one,
        two_four,
        three,
        four,
        five,
        six,
        seven,
    )
    other = lax.ppermute(arrived, "core", [(0, 1), (1, 0)])
    first = call(
        first_kernel,
        (
            shape((CAP, WIDTH), bf16),
            shape((8, ROUTED), i32),
            shape((8, CAPL), f32),
            shape((8, META), f32),
        ),
        arrived,
    )
    block = call(compact_kernel, shape((CAP, WIDTH), bf16), other, *first)
    bring = lambda v, dx, dy: lax.ppermute(v, PLANE, plane_shift(dx, dy))
    x_first, y_first = bring(block, 1, 0), bring(block, 0, -1)
    best_shape, places_shape = shape((8, CAPL), f32), shape((16, META), i32)
    own_best, own_columns, own_places = call(
        own_kernel, (best_shape, shape((CAP, META), f32), places_shape), block
    )
    own, own_best = lax.optimization_barrier((block, own_best))
    x_second, y_second = bring(own, -1, 0), bring(own, 0, 1)
    x_far, y_far = bring(x_first, 1, 0), bring(y_first, 0, -1)
    near_blocks = (block, x_first, x_second, y_first, y_second)
    near, columns, near_places = call(
        near_kernel,
        (best_shape, shape((2, CAP, META), f32), shape((32, META), i32)),
        *near_blocks,
        own_best,
        own_columns,
        cost=8,
    )
    mid, mid_places = call(
        mid_kernel,
        (best_shape, places_shape),
        block,
        y_first,
        y_second,
        x_far,
        own_columns,
        columns,
        cost=3,
    )
    message = call(
        far_kernel,
        shape((64, 1, META), f32),
        *near_blocks,
        x_far,
        y_far,
        own_places,
        near,
        near_places,
        mid,
        mid_places,
        cost=4,
    )
    answer = lax.all_to_all(message, RETURN, split_axis=0, concat_axis=0, tiled=True)
    out, flag = call(final_kernel, (shape((1, ROWS), f32), shape((1,), i32)), slots, answer, smem_out=(1,))
    target, within = slots[0], slots[1]
    return lax.cond(
        flag[0] > 0,
        lambda: slow_path(arrived, target, within, target >= 0),
        lambda: out.reshape(ROWS),
    )


def solution(mesh):
    axes = ("y", "xl", "z", "xh", "core")
    fine = Mesh(mesh.devices.reshape(4, 2, 8, 2, 2), axes)
    return jax.shard_map(
        body,
        mesh=fine,
        in_specs=(P(axes, None), P(axes), P(axes), P(axes)),
        out_specs=P(axes),
        check_vma=False,
    )
```

time: 78.9 us -> 75.4 us (0.956)
  waiting for transfers between devices: 28.6 us -> 23.4 us
  starting transfers between devices: 35.1 us -> 39 us
  Pallas kernels: 11.5 us -> 9.02 us
    pallas_call x8 -> x9, Pallas kernels: 11.5 us -> 9.02 us  [call(): pl.pallas_call(kernel, out_shape=out, in_specs=[space(i, smem) for i in r...]
    ppermute x6, starting transfers between devices: 7.3 us -> 9.6 us  [body(): bring = lambda v, dx, dy: lax.ppermute(v, PLANE, plane_shift(dx, dy))]
    ppermute x6, waiting for transfers between devices: 9.35 us -> 7.14 us  [body(): bring = lambda v, dx, dy: lax.ppermute(v, PLANE, plane_shift(dx, dy))]
    ppermute x7, waiting for transfers between devices: 8.27 us -> 6.21 us  [body(): send = lambda v, steps: lax.ppermute(v, COLUMN, column_shift(steps))]
    ppermute x1, waiting for transfers between devices: 1.77 us -> 0.92 us  [body(): other = lax.ppermute(arrived, 'core', [(0, 1), (1, 0)])]
    ppermute x7, starting transfers between devices: 15.6 us -> 16.5 us  [body(): send = lambda v, steps: lax.ppermute(v, COLUMN, column_shift(steps))]
  transfers between devices with their start and end apart: 15 -> 15, of which waited for: 10 -> 9; matrix products, arithmetic and copies ran while one was open for 0% -> 0% of each run, Pallas kernels for 7% -> 6%
where the time goes in v2:
time: 75.4 us; the launch traced here: 75.2 us
  starting transfers between devices  39 us (52%)
  waiting for transfers between devices  23.4 us (31%)
  Pallas kernels  9.02 us (12%)
  local copies, waits for them, and re-layouts  2.24 us (3%)
  between operations  1.42 us (2%)
    ppermute x7, starting transfers between devices, body(): send = lambda v, steps: lax.ppermute(v, COLUMN, column_shift(steps))  16.5 us
    all_to_all x1, starting transfers between devices, body(): lax.all_to_all(message, RETURN, split_axis=0, concat_axis=0, tiled=True)  11.7 us
    ppermute x6, starting transfers between devices, body(): bring = lambda v, dx, dy: lax.ppermute(v, PLANE, plane_shift(dx, dy))  9.6 us
    all_to_all x1, waiting for transfers between devices, body(): lax.all_to_all(message, RETURN, split_axis=0, concat_axis=0, tiled=True)  9.16 us
    pallas_call x9, Pallas kernels, call(): pl.pallas_call(kernel, out_shape=out, in_specs=[space(i, smem) for i in r...  9.02 us
    ppermute x6, waiting for transfers between devices, body(): bring = lambda v, dx, dy: lax.ppermute(v, PLANE, plane_shift(dx, dy))  7.14 us
    ppermute x7, waiting for transfers between devices, body(): send = lambda v, steps: lax.ppermute(v, COLUMN, column_shift(steps))  6.21 us
    unnamed x8, local copies, waits for them, and re-layouts  2.23 us
  transfers between devices with their start and end apart: 15, of which 9 were waited for; matrix products, arithmetic and copies ran while one was open for 0% of the time, Pallas kernels for 6%

profile of v2, /device:TPU:1, one launch (start us, length us, event | category | flops | bytes accessed | tf_op | source)
XLA Modules:
  0.0 75.2 jit_solution(1532731307748475587)
XLA Ops:
  0.7 0.0 copy-start.2
  0.7 0.0 copy-start.1
  0.7 0.7 copy-done.2
  1.3 0.0 copy-done.1
  1.3 0.0 copy-start
  1.4 1.0 %copy-done = bf16[256,768]{1,0:T(8,128)(2,1)S(1)} copy-done((bf16[256,768]{1,0:T(8,128)(2,1)S(1)}, bf16[256,768]{1,0:T(8,128)(2,1)}, u32[]{:S(2)}) %copy-start) | copy-done | bytes 393240
  2.3 0.5 shard_map.48
  2.9 6.9 %collective-permute-start.2 = (bf16[608,128]{1,0:T(8,128)(2,1)S(1)}, bf16[608,128]{1,0:T(8,128)(2,1)S(1)}, u32[]{:S(2)}, u32[]{:S(2)}) collective-permute-start(bf16[608,128]{1,0:T(8,128)(2,1)S(1)} %get-tuple-element.79), channel_id=1, source_target_pairs={{0,8},{1,25},{4,12},{5,29},{8,16},{9,1},{12,20},{13,5},{16,24},{17... | collective-permute-start | bytes 466952 | tf_op jit(solution)/shard_map/ppermute | solution.py:379
  9.8 0.7 collective-permute-start.1
  10.6 0.5 collective-permute-start.3
  11.1 2.7 %collective-permute-start.5 = (bf16[304,128]{1,0:T(8,128)(2,1)S(1)}, bf16[304,128]{1,0:T(8,128)(2,1)S(1)}, u32[]{:S(2)}, u32[]{:S(2)}) collective-permute-start(bf16[304,128]{1,0:T(8,128)(2,1)S(1)} %get-tuple-element.81), channel_id=1, source_target_pairs={{0,20},{1,13},{4,24},{5,17},{8,28},{9,21},{12,0},{13,25},{16,4},{1... | collective-permute-start | bytes 233480 | tf_op jit(solution)/shard_map/ppermute | solution.py:379
  13.8 2.4 %collective-permute-start.6 = (bf16[304,128]{1,0:T(8,128)(2,1)S(1)}, bf16[304,128]{1,0:T(8,128)(2,1)S(1)}, u32[]{:S(2)}, u32[]{:S(2)}) collective-permute-start(bf16[304,128]{1,0:T(8,128)(2,1)S(1)} %get-tuple-element.82), channel_id=1, source_target_pairs={{0,24},{1,9},{4,28},{5,13},{8,0},{9,17},{12,4},{13,21},{16,8},{17,... | collective-permute-start | bytes 233480 | tf_op jit(solution)/shard_map/ppermute | solution.py:379
  16.2 0.0 collective-permute-done.2.refs_2_
  16.2 0.0 collective-permute-start.7
  16.2 0.1 collective-permute-done.1.refs_1_
  16.3 3.1 %collective-permute-start.4 = (bf16[304,128]{1,0:T(8,128)(2,1)S(1)}, bf16[304,128]{1,0:T(8,128)(2,1)S(1)}, u32[]{:S(2)}, u32[]{:S(2)}) collective-permute-start(bf16[304,128]{1,0:T(8,128)(2,1)S(1)} %slice.65), channel_id=1, source_target_pairs={{0,8},{1,25},{4,12},{5,29},{8,16},{9,1},{12,20},{13,5},{16,24},{17... | collective-permute-start | bytes 233480 | tf_op jit(solution)/shard_map/ppermute | solution.py:379
  19.4 0.0 collective-permute-done.3.refs_3_
  19.4 1.3 %collective-permute-done.5.refs_5_ = bf16[304,128]{1,0:T(8,128)(2,1)S(1)} collective-permute-done((bf16[304,128]{1,0:T(8,128)(2,1)S(1)}, bf16[304,128]{1,0:T(8,128)(2,1)S(1)}, u32[]{:S(2)}, u32[]{:S(2)}) %collective-permute-start.5) | collective-permute-done | bytes 77856 | tf_op jit(solution)/shard_map/ppermute | solution.py:379
  20.7 1.7 %collective-permute-done.6.refs_6_ = bf16[304,128]{1,0:T(8,128)(2,1)S(1)} collective-permute-done((bf16[304,128]{1,0:T(8,128)(2,1)S(1)}, bf16[304,128]{1,0:T(8,128)(2,1)S(1)}, u32[]{:S(2)}, u32[]{:S(2)}) %collective-permute-start.6) | collective-permute-done | bytes 77856 | tf_op jit(solution)/shard_map/ppermute | solution.py:379
  22.5 3.1 %collective-permute-done.7.refs_7_ = bf16[304,128]{1,0:T(8,128)(2,1)S(1)} collective-permute-done((bf16[304,128]{1,0:T(8,128)(2,1)S(1)}, bf16[304,128]{1,0:T(8,128)(2,1)S(1)}, u32[]{:S(2)}, u32[]{:S(2)}) %collective-permute-start.7) | collective-permute-done | bytes 77856 | tf_op jit(solution)/shard_map/ppermute | solution.py:379
  25.6 0.0 collective-permute-done.4.refs_4_
  25.6 0.1 shard_map.49.own_ref
  25.7 1.2 %collective-permute-start.8 = (bf16[416,768]{1,0:T(8,128)(2,1)S(1)}, bf16[416,768]{1,0:T(8,128)(2,1)S(1)}, u32[]{:S(2)}, u32[]{:S(2)}) collective-permute-start(bf16[416,768]{1,0:T(8,128)(2,1)S(1)} %shard_map.49.own_ref), channel_id=1, source_target_pairs={{0,1},{1,0},{2,3},{3,2},{4,5},{5,4},{6,7},{7,6},{8,9},{9,8},{10,11... | collective-permute-start | bytes 1916936 | tf_op jit(solution)/shard_map/ppermute | solution.py:396
  26.9 0.8 %shard_map.50 = (bf16[304,768]{1,0:T(8,128)(2,1)S(1)}, s32[8,384]{1,0:T(8,128)S(1)}, f32[8,384]{1,0:T(8,128)S(1)}, f32[8,128]{1,0:T(8,128)S(1)}) custom-call(bf16[416,768]{1,0:T(8,128)(2,1)S(1)} %shard_map.49.own_ref), custom_call_target="tpu_custom_call" | custom-call | flops 141950976 | bytes 933888 | tf_op jit(solution)/shard_map/pallas_call | solution.py:60
  27.7 0.9 %collective-permute-done.8.other_ref = bf16[416,768]{1,0:T(8,128)(2,1)S(1)} collective-permute-done((bf16[416,768]{1,0:T(8,128)(2,1)S(1)}, bf16[416,768]{1,0:T(8,128)(2,1)S(1)}, u32[]{:S(2)}, u32[]{:S(2)}) %collective-permute-start.8) | collective-permute-done | bytes 639008 | tf_op jit(solution)/shard_map/ppermute | solution.py:396
  28.6 0.8 %shard_map.51.own = bf16[304,768]{1,0:T(8,128)(2,1)S(1)} custom-call(bf16[416,768]{1,0:T(8,128)(2,1)S(1)} %collective-permute-done.8.other_ref, bf16[304,768]{1,0:T(8,128)(2,1)S(1)} %get-tuple-element.84.rows_ref, s32[8,384]{1,0:T(8,128)S(1)} %get-tuple-element.85.pos_ref, f32[8,384]{1,0:T(8,128)S(1)} %get-tuple-element.86.ranks_ref, ...), custom_call_target="tpu_custom_call" | custom-call | flops 141950976 | bytes 933888 | tf_op jit(solution)/shard_map/pallas_call | solution.py:60
  29.5 1.3 %collective-permute-start.9 = (bf16[304,768]{1,0:T(8,128)(2,1)S(1)}, bf16[304,768]{1,0:T(8,128)(2,1)S(1)}, u32[]{:S(2)}, u32[]{:S(2)}) collective-permute-start(bf16[304,768]{1,0:T(8,128)(2,1)S(1)} %shard_map.51.own), channel_id=1, source_target_pairs={{32,0},{96,64},{160,128},{224,192},{2,32},{66,96},{130,160},{194,2... | collective-permute-start | bytes 1400840 | tf_op jit(solution)/shard_map/ppermute | solution.py:408
  30.7 2.7 %collective-permute-start.11 = (bf16[304,768]{1,0:T(8,128)(2,1)S(1)}, bf16[304,768]{1,0:T(8,128)(2,1)S(1)}, u32[]{:S(2)}, u32[]{:S(2)}) collective-permute-start(bf16[304,768]{1,0:T(8,128)(2,1)S(1)} %shard_map.51.own), channel_id=1, source_target_pairs={{192,0},{0,64},{64,128},{128,192},{224,32},{32,96},{96,160},{160,2... | collective-permute-start | bytes 1400840 | tf_op jit(solution)/shard_map/ppermute | solution.py:408
  33.5 0.6 shard_map.52
  34.0 1.6 %collective-permute-start.10 = (bf16[304,768]{1,0:T(8,128)(2,1)S(1)}, bf16[304,768]{1,0:T(8,128)(2,1)S(1)}, u32[]{:S(2)}, u32[]{:S(2)}) collective-permute-start(bf16[304,768]{1,0:T(8,128)(2,1)S(1)} %shard_map.51.own), channel_id=1, source_target_pairs={{34,0},{98,64},{162,128},{226,192},{0,32},{64,96},{128,160},{192,2... | collective-permute-start | bytes 1400840 | tf_op jit(solution)/shard_map/ppermute | solution.py:408
  35.6 0.0 collective-permute-start.12
  35.6 2.9 %collective-permute-done.9.x_first = bf16[304,768]{1,0:T(8,128)(2,1)S(1)} collective-permute-done((bf16[304,768]{1,0:T(8,128)(2,1)S(1)}, bf16[304,768]{1,0:T(8,128)(2,1)S(1)}, u32[]{:S(2)}, u32[]{:S(2)}) %collective-permute-start.9) | collective-permute-done | bytes 466976 | tf_op jit(solution)/shard_map/ppermute | solution.py:408
  38.5 0.6 collective-permute-start.13
  39.1 1.5 %collective-permute-done.11.y_first = bf16[304,768]{1,0:T(8,128)(2,1)S(1)} collective-permute-done((bf16[304,768]{1,0:T(8,128)(2,1)S(1)}, bf16[304,768]{1,0:T(8,128)(2,1)S(1)}, u32[]{:S(2)}, u32[]{:S(2)}) %collective-permute-start.11) | collective-permute-done | bytes 466976 | tf_op jit(solution)/shard_map/ppermute | solution.py:408
  40.6 3.4 %collective-permute-start.14 = (bf16[304,768]{1,0:T(8,128)(2,1)S(1)}, bf16[304,768]{1,0:T(8,128)(2,1)S(1)}, u32[]{:S(2)}, u32[]{:S(2)}) collective-permute-start(bf16[304,768]{1,0:T(8,128)(2,1)S(1)} %collective-permute-done.11.y_first), channel_id=1, source_target_pairs={{192,0},{0,64},{64,128},{128,192},{224,32},{32,96},{96,160},{160,2... | collective-permute-start | bytes 1400840 | tf_op jit(solution)/shard_map/ppermute | solution.py:408
  44.0 0.0 collective-permute-done.10.x_second
  44.0 2.8 %collective-permute-done.12.y_second = bf16[304,768]{1,0:T(8,128)(2,1)S(1)} collective-permute-done((bf16[304,768]{1,0:T(8,128)(2,1)S(1)}, bf16[304,768]{1,0:T(8,128)(2,1)S(1)}, u32[]{:S(2)}, u32[]{:S(2)}) %collective-permute-start.12) | collective-permute-done | bytes 466976 | tf_op jit(solution)/shard_map/ppermute | solution.py:408
  46.8 2.5 %shard_map.53 = (f32[8,384]{1,0:T(8,128)S(1)}, f32[2,304,128]{2,1,0:T(8,128)S(1)}, s32[32,128]{1,0:T(8,128)S(1)}) custom-call(bf16[304,768]{1,0:T(8,128)(2,1)S(1)} %shard_map.51.own, bf16[304,768]{1,0:T(8,128)(2,1)S(1)} %collective-permute-done.9.x_first, bf16[304,768]{1,0:T(8,128)(2,1)S(1)} %collective-permute-done.10.x_second, ...), custom_call_target="tpu_custom_call" | custom-call | flops 1135607808 | bytes 933888 | tf_op jit(solution)/shard_map/pallas_call | solution.py:60
  49.3 0.0 collective-permute-done.13.x_far
  49.3 0.9 %shard_map.54 = (f32[8,384]{1,0:T(8,128)S(1)}, s32[16,128]{1,0:T(8,128)S(1)}) custom-call(bf16[304,768]{1,0:T(8,128)(2,1)S(1)} %shard_map.51.own, bf16[304,768]{1,0:T(8,128)(2,1)S(1)} %collective-permute-done.11.y_first, bf16[304,768]{1,0:T(8,128)(2,1)S(1)} %collective-permute-done.12.y_second, bf16[304,768]{1,0:T(8,128)(2,1)S(1)} %collective-permute-done.13.x_far, ...), custom_call_target="tpu_custom_call" | custom-call | flops 425852928 | bytes 933888 | tf_op jit(solution)/shard_map/pallas_call | solution.py:60
  50.2 0.0 collective-permute-done.14.y_far
  50.2 2.1 %shard_map.55 = f32[64,1,128]{2,1,0:T(1,128)} custom-call(bf16[304,768]{1,0:T(8,128)(2,1)S(1)} %shard_map.51.own, bf16[304,768]{1,0:T(8,128)(2,1)S(1)} %collective-permute-done.9.x_first, bf16[304,768]{1,0:T(8,128)(2,1)S(1)} %collective-permute-done.10.x_second, bf16[304,768]{1,0:T(8,128)(2,1)S(1)} %collective-permute-done.11.y_first, ...), custom_call_target="tpu_custom_call" | custom-call | flops 567803904 | bytes 933888 | tf_op jit(solution)/shard_map/pallas_call | solution.py:60
  52.4 11.7 %all-to-all-start.1 = ((f32[64,1,128]{2,1,0:T(1,128)}), f32[64,1,128]{2,1,0:T(1,128)S(1)}, u32[]{:S(2)}, u32[]{:S(2)}) async-start(f32[64,1,128]{2,1,0:T(1,128)} %shard_map.55), calls=%async_computation.1 | async-start | bytes 65536 | tf_op jit(solution)/shard_map/all_to_all | solution.py:450
  64.1 9.2 %all-to-all-done.1.ans_ref = f32[64,1,128]{2,1,0:T(1,128)S(1)} async-done(((f32[64,1,128]{2,1,0:T(1,128)}), f32[64,1,128]{2,1,0:T(1,128)S(1)}, u32[]{:S(2)}, u32[]{:S(2)}) %all-to-all-start.1) | async-done | bytes 32800 | tf_op jit(solution)/shard_map/all_to_all | solution.py:450
  73.3 0.7 shard_map.56
  74.6 0.0 copy-start.3
  74.6 0.6 copy-done.3
  (2 shorter events, 0.0 us)
Async XLA Ops:
  0.7 0.7 copy-start.2
  0.7 0.7 copy-start.1
  1.3 1.0 %copy-start = (bf16[256,768]{1,0:T(8,128)(2,1)S(1)}, bf16[256,768]{1,0:T(8,128)(2,1)}, u32[]{:S(2)}) copy-start(bf16[256,768]{1,0:T(8,128)(2,1)} %emb_ref.1) | copy-start | bytes 1179652
  2.9 13.3 %collective-permute-start.2 = (bf16[608,128]{1,0:T(8,128)(2,1)S(1)}, bf16[608,128]{1,0:T(8,128)(2,1)S(1)}, u32[]{:S(2)}, u32[]{:S(2)}) collective-permute-start(bf16[608,128]{1,0:T(8,128)(2,1)S(1)} %get-tuple-element.79), channel_id=1, source_target_pairs={{0,8},{1,25},{4,12},{5,29},{8,16},{9,1},{12,20},{13,5},{16,24},{17... | collective-permute-start | bytes 466952 | tf_op jit(solution)/shard_map/ppermute | solution.py:379
  9.8 6.5 %collective-permute-start.1 = (bf16[304,128]{1,0:T(8,128)(2,1)S(1)}, bf16[304,128]{1,0:T(8,128)(2,1)S(1)}, u32[]{:S(2)}, u32[]{:S(2)}) collective-permute-start(bf16[304,128]{1,0:T(8,128)(2,1)S(1)} %get-tuple-element.78), channel_id=1, source_target_pairs={{0,4},{1,29},{4,8},{5,1},{8,12},{9,5},{12,16},{13,9},{16,20},{17,1... | collective-permute-start | bytes 233480 | tf_op jit(solution)/shard_map/ppermute | solution.py:379
  10.6 8.9 %collective-permute-start.3 = (bf16[304,128]{1,0:T(8,128)(2,1)S(1)}, bf16[304,128]{1,0:T(8,128)(2,1)S(1)}, u32[]{:S(2)}, u32[]{:S(2)}) collective-permute-start(bf16[304,128]{1,0:T(8,128)(2,1)S(1)} %get-tuple-element.80), channel_id=1, source_target_pairs={{0,12},{1,21},{4,16},{5,25},{8,20},{9,29},{12,24},{13,1},{16,28},{... | collective-permute-start | bytes 233480 | tf_op jit(solution)/shard_map/ppermute | solution.py:379
  11.1 9.6 %collective-permute-start.5 = (bf16[304,128]{1,0:T(8,128)(2,1)S(1)}, bf16[304,128]{1,0:T(8,128)(2,1)S(1)}, u32[]{:S(2)}, u32[]{:S(2)}) collective-permute-start(bf16[304,128]{1,0:T(8,128)(2,1)S(1)} %get-tuple-element.81), channel_id=1, source_target_pairs={{0,20},{1,13},{4,24},{5,17},{8,28},{9,21},{12,0},{13,25},{16,4},{1... | collective-permute-start | bytes 233480 | tf_op jit(solution)/shard_map/ppermute | solution.py:379
  13.8 8.6 %collective-permute-start.6 = (bf16[304,128]{1,0:T(8,128)(2,1)S(1)}, bf16[304,128]{1,0:T(8,128)(2,1)S(1)}, u32[]{:S(2)}, u32[]{:S(2)}) collective-permute-start(bf16[304,128]{1,0:T(8,128)(2,1)S(1)} %get-tuple-element.82), channel_id=1, source_target_pairs={{0,24},{1,9},{4,28},{5,13},{8,0},{9,17},{12,4},{13,21},{16,8},{17,... | collective-permute-start | bytes 233480 | tf_op jit(solution)/shard_map/ppermute | solution.py:379
  16.2 9.4 %collective-permute-start.7 = (bf16[304,128]{1,0:T(8,128)(2,1)S(1)}, bf16[304,128]{1,0:T(8,128)(2,1)S(1)}, u32[]{:S(2)}, u32[]{:S(2)}) collective-permute-start(bf16[304,128]{1,0:T(8,128)(2,1)S(1)} %get-tuple-element.83), channel_id=1, source_target_pairs={{0,28},{1,5},{4,0},{5,9},{8,4},{9,13},{12,8},{13,17},{16,12},{17,2... | collective-permute-start | bytes 233480 | tf_op jit(solution)/shard_map/ppermute | solution.py:379
  16.3 9.3 %collective-permute-start.4 = (bf16[304,128]{1,0:T(8,128)(2,1)S(1)}, bf16[304,128]{1,0:T(8,128)(2,1)S(1)}, u32[]{:S(2)}, u32[]{:S(2)}) collective-permute-start(bf16[304,128]{1,0:T(8,128)(2,1)S(1)} %slice.65), channel_id=1, source_target_pairs={{0,8},{1,25},{4,12},{5,29},{8,16},{9,1},{12,20},{13,5},{16,24},{17... | collective-permute-start | bytes 233480 | tf_op jit(solution)/shard_map/ppermute | solution.py:379
  25.7 2.9 %collective-permute-start.8 = (bf16[416,768]{1,0:T(8,128)(2,1)S(1)}, bf16[416,768]{1,0:T(8,128)(2,1)S(1)}, u32[]{:S(2)}, u32[]{:S(2)}) collective-permute-start(bf16[416,768]{1,0:T(8,128)(2,1)S(1)} %shard_map.49.own_ref), channel_id=1, source_target_pairs={{0,1},{1,0},{2,3},{3,2},{4,5},{5,4},{6,7},{7,6},{8,9},{9,8},{10,11... | collective-permute-start | bytes 1916936 | tf_op jit(solution)/shard_map/ppermute | solution.py:396
  29.5 9.0 %collective-permute-start.9 = (bf16[304,768]{1,0:T(8,128)(2,1)S(1)}, bf16[304,768]{1,0:T(8,128)(2,1)S(1)}, u32[]{:S(2)}, u32[]{:S(2)}) collective-permute-start(bf16[304,768]{1,0:T(8,128)(2,1)S(1)} %shard_map.51.own), channel_id=1, source_target_pairs={{32,0},{96,64},{160,128},{224,192},{2,32},{66,96},{130,160},{194,2... | collective-permute-start | bytes 1400840 | tf_op jit(solution)/shard_map/ppermute | solution.py:408
  30.7 9.8 %collective-permute-start.11 = (bf16[304,768]{1,0:T(8,128)(2,1)S(1)}, bf16[304,768]{1,0:T(8,128)(2,1)S(1)}, u32[]{:S(2)}, u32[]{:S(2)}) collective-permute-start(bf16[304,768]{1,0:T(8,128)(2,1)S(1)} %shard_map.51.own), channel_id=1, source_target_pairs={{192,0},{0,64},{64,128},{128,192},{224,32},{32,96},{96,160},{160,2... | collective-permute-start | bytes 1400840 | tf_op jit(solution)/shard_map/ppermute | solution.py:408
  34.0 10.0 %collective-permute-start.10 = (bf16[304,768]{1,0:T(8,128)(2,1)S(1)}, bf16[304,768]{1,0:T(8,128)(2,1)S(1)}, u32[]{:S(2)}, u32[]{:S(2)}) collective-permute-start(bf16[304,768]{1,0:T(8,128)(2,1)S(1)} %shard_map.51.own), channel_id=1, source_target_pairs={{34,0},{98,64},{162,128},{226,192},{0,32},{64,96},{128,160},{192,2... | collective-permute-start | bytes 1400840 | tf_op jit(solution)/shard_map/ppermute | solution.py:408
  35.6 11.2 %collective-permute-start.12 = (bf16[304,768]{1,0:T(8,128)(2,1)S(1)}, bf16[304,768]{1,0:T(8,128)(2,1)S(1)}, u32[]{:S(2)}, u32[]{:S(2)}) collective-permute-start(bf16[304,768]{1,0:T(8,128)(2,1)S(1)} %shard_map.51.own), channel_id=1, source_target_pairs={{64,0},{128,64},{192,128},{0,192},{96,32},{160,96},{224,160},{32,2... | collective-permute-start | bytes 1400840 | tf_op jit(solution)/shard_map/ppermute | solution.py:408
  38.5 10.8 %collective-permute-start.13 = (bf16[304,768]{1,0:T(8,128)(2,1)S(1)}, bf16[304,768]{1,0:T(8,128)(2,1)S(1)}, u32[]{:S(2)}, u32[]{:S(2)}) collective-permute-start(bf16[304,768]{1,0:T(8,128)(2,1)S(1)} %collective-permute-done.9.x_first), channel_id=1, source_target_pairs={{32,0},{96,64},{160,128},{224,192},{2,32},{66,96},{130,160},{194,2... | collective-permute-start | bytes 1400840 | tf_op jit(solution)/shard_map/ppermute | solution.py:408
  40.6 9.6 %collective-permute-start.14 = (bf16[304,768]{1,0:T(8,128)(2,1)S(1)}, bf16[304,768]{1,0:T(8,128)(2,1)S(1)}, u32[]{:S(2)}, u32[]{:S(2)}) collective-permute-start(bf16[304,768]{1,0:T(8,128)(2,1)S(1)} %collective-permute-done.11.y_first), channel_id=1, source_target_pairs={{192,0},{0,64},{64,128},{128,192},{224,32},{32,96},{96,160},{160,2... | collective-permute-start | bytes 1400840 | tf_op jit(solution)/shard_map/ppermute | solution.py:408
  52.4 20.9 %all-to-all-start.1 = ((f32[64,1,128]{2,1,0:T(1,128)}), f32[64,1,128]{2,1,0:T(1,128)S(1)}, u32[]{:S(2)}, u32[]{:S(2)}) async-start(f32[64,1,128]{2,1,0:T(1,128)} %shard_map.55), calls=%async_computation.1 | async-start | bytes 65536 | tf_op jit(solution)/shard_map/all_to_all | solution.py:450
  74.6 0.6 copy-start.3

commit v3 on v2

--- a/solution.py
+++ b/solution.py
@@ -74,32 +74,42 @@
     return jnp.where(core == 0, value, -value)
 
 
-def prep_kernel(count_ref, emb_ref, id_ref, rank_ref, *out_refs):
-    slot_ref = out_refs[-1]
-    x = emb_ref[...].astype(jnp.float32)
-    unit = (x * lax.rsqrt(jnp.sum(x * x, axis=1, keepdims=True) + norm_eps)).astype(jnp.bfloat16)
-    ids = id_ref[...]
-    ranks = rank_ref[...]
-    live = iota((1, ROWS), 1) < count_ref[0]
+def slot_kernel(both_ref, where_ref, marks_ref, slot_ref):
+    ids, ranks = both_ref[...] & 15, both_ref[...] >> 4
     target = ids & (GROUPS - 1)
-    chosen = jnp.where((iota((GROUPS, ROWS), 0) == target) & live, 1.0, 0.0)
+    chosen = jnp.where(iota((GROUPS, ROWS), 0) == target, 1.0, 0.0)
     upper = jnp.where(iota((ROWS, ROWS), 0) < iota((ROWS, ROWS), 1), 1.0, 0.0).astype(jnp.bfloat16)
     before = dot(chosen.astype(jnp.bfloat16), upper, ((1,), (0,)))
     within = jnp.sum(before * chosen, axis=0, keepdims=True).astype(jnp.int32)
     steps = signed(lax.axis_index("core"), target - lax.axis_index("z")) & (GROUPS - 1)
     at = jnp.where(steps == 3, 4, jnp.where(steps == 4, 3, steps))
-    slot = jnp.where(live, at * SLOTS + within, -1)
-    where_to = jnp.where(iota((ROUTED, ROWS), 0) == slot, 1.0, 0.0).astype(jnp.bfloat16)
+    slot = jnp.where(within < SLOTS, at * SLOTS + within, -1)
+    where_ref[...] = jnp.where(iota((ROUTED, ROWS), 0) == slot, 1.0, 0.0).astype(jnp.bfloat16)
     high = ranks >> 8
     row = iota((16, ROWS), 0)
     meta = jnp.where(
         row == 0, ids + 1, jnp.where(row == 1, high, jnp.where(row == 2, ranks - (high << 8), 0))
     )
-    meta = meta.astype(jnp.float32).astype(jnp.bfloat16)
+    marks_ref[...] = meta.astype(jnp.float32).astype(jnp.bfloat16)
+    slot_ref[0:1, :] = target
+    slot_ref[1:2, :] = within
+    slot_ref[2:8, :] = jnp.zeros((6, ROWS), jnp.int32)
+
+
+def piece_kernel(count_ref, emb_ref, where_ref, marks_ref, slot_ref, *refs):
+    *out_refs, live_slot_ref = refs
+    live = iota((1, ROWS), 1) < count_ref[0]
+    live_slot_ref[0:1, :] = jnp.where(live, slot_ref[0:1, :], -1)
+    live_slot_ref[1:8, :] = slot_ref[1:8, :]
+    x = emb_ref[...].astype(jnp.float32)
+    unit = x * lax.rsqrt(jnp.sum(x * x, axis=1, keepdims=True) + norm_eps)
+    unit = jnp.where(iota((ROWS, 1), 0) < count_ref[0], unit, 0.0).astype(jnp.bfloat16)
+    where_to = where_ref[...]
     rows = dot(where_to, unit, ((1,), (0,))).astype(jnp.bfloat16)
+    meta = jnp.where(live, marks_ref[...].astype(jnp.float32), 0.0).astype(jnp.bfloat16)
     marks = dot(meta, where_to, ((1,), (1,)))
     at = 0
-    for ref in out_refs[:-1]:
+    for ref in out_refs:
         for first in range(0, ref.shape[0], PIECE):
             for i in range(CHUNKS):
                 ref[first + i * SLOTS : first + (i + 1) * SLOTS, :] = rows[
@@ -110,9 +120,6 @@
             )
             ref[first + CHUNKS * SLOTS : first + PIECE, :] = tail.astype(jnp.bfloat16)
             at += SLOTS
-    slot_ref[0:1, :] = jnp.where(live, target, -1)
-    slot_ref[1:2, :] = within
-    slot_ref[2:8, :] = jnp.zeros((6, ROWS), jnp.int32)
 
 
 def collect_kernel(*refs):
@@ -367,13 +374,20 @@
 def body(embeddings, cluster_id, order_rank, row_count):
     f32, bf16, i32 = jnp.float32, jnp.bfloat16, jnp.int32
     shape = jax.ShapeDtypeStruct
+    slots_shape = shape((8, ROWS), i32)
+    where_to, marks, slots = call(
+        slot_kernel,
+        (shape((ROUTED, ROWS), bf16), shape((16, ROWS), bf16), slots_shape),
+        (cluster_id + 16 * order_rank).reshape(1, ROWS),
+    )
     *pieces, slots = call(
-        prep_kernel,
-        tuple(shape((n * PIECE, META), bf16) for n in PIECES) + (shape((8, ROWS), i32),),
+        piece_kernel,
+        tuple(shape((n * PIECE, META), bf16) for n in PIECES) + (slots_shape,),
         row_count,
         embeddings,
-        cluster_id.reshape(1, ROWS),
-        order_rank.reshape(1, ROWS),
+        where_to,
+        marks,
+        slots,
         smem=(0,),
     )
     send = lambda v, steps: lax.ppermute(v, COLUMN, column_shift(steps))

time: 75.4 us -> 74.6 us (0.989)
  local copies, waits for them, and re-layouts: 2.24 us -> 0.57 us
    unnamed x8 -> x4, local copies, waits for them, and re-layouts: 2.23 us -> 0.56 us
    pallas_call x9 -> x10, Pallas kernels: 9.02 us -> 9.25 us  [call(): pl.pallas_call(kernel, out_shape=out, in_specs=[space(i, smem) for i in r...]
where the time goes in v3:
time: 74.6 us; the launch traced here: 74.5 us
  starting transfers between devices  39 us (52%)
  waiting for transfers between devices  23.4 us (31%)
  Pallas kernels  9.25 us (12%)
  between operations  1.41 us (2%)
  other arithmetic  0.75 us (1%)
    ppermute x7, starting transfers between devices, body(): send = lambda v, steps: lax.ppermute(v, COLUMN, column_shift(steps))  16.5 us
    all_to_all x1, starting transfers between devices, body(): lax.all_to_all(message, RETURN, split_axis=0, concat_axis=0, tiled=True)  11.7 us
    ppermute x6, starting transfers between devices, body(): bring = lambda v, dx, dy: lax.ppermute(v, PLANE, plane_shift(dx, dy))  9.6 us
    pallas_call x10, Pallas kernels, call(): pl.pallas_call(kernel, out_shape=out, in_specs=[space(i, smem) for i in r...  9.25 us
    all_to_all x1, waiting for transfers between devices, body(): lax.all_to_all(message, RETURN, split_axis=0, concat_axis=0, tiled=True)  9.17 us
    ppermute x6, waiting for transfers between devices, body(): bring = lambda v, dx, dy: lax.ppermute(v, PLANE, plane_shift(dx, dy))  7.15 us
    ppermute x7, waiting for transfers between devices, body(): send = lambda v, steps: lax.ppermute(v, COLUMN, column_shift(steps))  6.21 us
  transfers between devices with their start and end apart: 15, of which 9 were waited for; matrix products, arithmetic and copies ran while one was open for 0% of the time, Pallas kernels for 6%

profile of v3, /device:TPU:1, one launch (start us, length us, event | category | flops | bytes accessed | tf_op | source)
XLA Modules:
  0.0 74.5 jit_solution(6429470801506807213)
XLA Ops:
  0.0 0.0 copy-start
  0.0 0.7 %multiply_add_fusion = s32[256]{0:T(256)S(1)} fusion(s32[256]{0:T(256)} %param.9, s32[256]{0:T(256)} %param.10), kind=kLoop, calls=%fused_computation.24 | loop fusion | flops 512 | bytes 3072 | tf_op jit(solution)/shard_map/add | solution.py:381
  0.8 0.2 shard_map.48
  1.6 0.0 copy-done
  1.7 0.5 shard_map.49
  2.2 6.9 %collective-permute-start.2 = (bf16[608,128]{1,0:T(8,128)(2,1)S(1)}, bf16[608,128]{1,0:T(8,128)(2,1)S(1)}, u32[]{:S(2)}, u32[]{:S(2)}) collective-permute-start(bf16[608,128]{1,0:T(8,128)(2,1)S(1)} %get-tuple-element.85), channel_id=1, source_target_pairs={{0,8},{1,25},{4,12},{5,29},{8,16},{9,1},{12,20},{13,5},{16,24},{17... | collective-permute-start | bytes 466952 | tf_op jit(solution)/shard_map/ppermute | solution.py:393
  9.1 0.7 collective-permute-start.1
  9.8 0.5 collective-permute-start.3
  10.4 2.7 %collective-permute-start.5 = (bf16[304,128]{1,0:T(8,128)(2,1)S(1)}, bf16[304,128]{1,0:T(8,128)(2,1)S(1)}, u32[]{:S(2)}, u32[]{:S(2)}) collective-permute-start(bf16[304,128]{1,0:T(8,128)(2,1)S(1)} %get-tuple-element.87), channel_id=1, source_target_pairs={{0,20},{1,13},{4,24},{5,17},{8,28},{9,21},{12,0},{13,25},{16,4},{1... | collective-permute-start | bytes 233480 | tf_op jit(solution)/shard_map/ppermute | solution.py:393
  13.1 2.4 %collective-permute-start.6 = (bf16[304,128]{1,0:T(8,128)(2,1)S(1)}, bf16[304,128]{1,0:T(8,128)(2,1)S(1)}, u32[]{:S(2)}, u32[]{:S(2)}) collective-permute-start(bf16[304,128]{1,0:T(8,128)(2,1)S(1)} %get-tuple-element.88), channel_id=1, source_target_pairs={{0,24},{1,9},{4,28},{5,13},{8,0},{9,17},{12,4},{13,21},{16,8},{17,... | collective-permute-start | bytes 233480 | tf_op jit(solution)/shard_map/ppermute | solution.py:393
  15.5 0.0 collective-permute-done.2.refs_2_
  15.5 0.0 collective-permute-start.7
  15.5 0.1 collective-permute-done.1.refs_1_
  15.6 3.1 %collective-permute-start.4 = (bf16[304,128]{1,0:T(8,128)(2,1)S(1)}, bf16[304,128]{1,0:T(8,128)(2,1)S(1)}, u32[]{:S(2)}, u32[]{:S(2)}) collective-permute-start(bf16[304,128]{1,0:T(8,128)(2,1)S(1)} %slice.65), channel_id=1, source_target_pairs={{0,8},{1,25},{4,12},{5,29},{8,16},{9,1},{12,20},{13,5},{16,24},{17... | collective-permute-start | bytes 233480 | tf_op jit(solution)/shard_map/ppermute | solution.py:393
  18.7 0.0 collective-permute-done.3.refs_3_
  18.7 1.3 %collective-permute-done.5.refs_5_ = bf16[304,128]{1,0:T(8,128)(2,1)S(1)} collective-permute-done((bf16[304,128]{1,0:T(8,128)(2,1)S(1)}, bf16[304,128]{1,0:T(8,128)(2,1)S(1)}, u32[]{:S(2)}, u32[]{:S(2)}) %collective-permute-start.5) | collective-permute-done | bytes 77856 | tf_op jit(solution)/shard_map/ppermute | solution.py:393
  20.0 1.7 %collective-permute-done.6.refs_6_ = bf16[304,128]{1,0:T(8,128)(2,1)S(1)} collective-permute-done((bf16[304,128]{1,0:T(8,128)(2,1)S(1)}, bf16[304,128]{1,0:T(8,128)(2,1)S(1)}, u32[]{:S(2)}, u32[]{:S(2)}) %collective-permute-start.6) | collective-permute-done | bytes 77856 | tf_op jit(solution)/shard_map/ppermute | solution.py:393
  21.7 3.1 %collective-permute-done.7.refs_7_ = bf16[304,128]{1,0:T(8,128)(2,1)S(1)} collective-permute-done((bf16[304,128]{1,0:T(8,128)(2,1)S(1)}, bf16[304,128]{1,0:T(8,128)(2,1)S(1)}, u32[]{:S(2)}, u32[]{:S(2)}) %collective-permute-start.7) | collective-permute-done | bytes 77856 | tf_op jit(solution)/shard_map/ppermute | solution.py:393
  24.9 0.0 collective-permute-done.4.refs_4_
  24.9 0.1 shard_map.50.own_ref
  25.0 1.2 %collective-permute-start.8 = (bf16[416,768]{1,0:T(8,128)(2,1)S(1)}, bf16[416,768]{1,0:T(8,128)(2,1)S(1)}, u32[]{:S(2)}, u32[]{:S(2)}) collective-permute-start(bf16[416,768]{1,0:T(8,128)(2,1)S(1)} %shard_map.50.own_ref), channel_id=1, source_target_pairs={{0,1},{1,0},{2,3},{3,2},{4,5},{5,4},{6,7},{7,6},{8,9},{9,8},{10,11... | collective-permute-start | bytes 1916936 | tf_op jit(solution)/shard_map/ppermute | solution.py:410
  26.2 0.8 %shard_map.51 = (bf16[304,768]{1,0:T(8,128)(2,1)S(1)}, s32[8,384]{1,0:T(8,128)S(1)}, f32[8,384]{1,0:T(8,128)S(1)}, f32[8,128]{1,0:T(8,128)S(1)}) custom-call(bf16[416,768]{1,0:T(8,128)(2,1)S(1)} %shard_map.50.own_ref), custom_call_target="tpu_custom_call" | custom-call | flops 141950976 | bytes 933888 | tf_op jit(solution)/shard_map/pallas_call | solution.py:60
  27.0 0.9 %collective-permute-done.8.other_ref = bf16[416,768]{1,0:T(8,128)(2,1)S(1)} collective-permute-done((bf16[416,768]{1,0:T(8,128)(2,1)S(1)}, bf16[416,768]{1,0:T(8,128)(2,1)S(1)}, u32[]{:S(2)}, u32[]{:S(2)}) %collective-permute-start.8) | collective-permute-done | bytes 639008 | tf_op jit(solution)/shard_map/ppermute | solution.py:410
  27.9 0.8 %shard_map.52.own = bf16[304,768]{1,0:T(8,128)(2,1)S(1)} custom-call(bf16[416,768]{1,0:T(8,128)(2,1)S(1)} %collective-permute-done.8.other_ref, bf16[304,768]{1,0:T(8,128)(2,1)S(1)} %get-tuple-element.90.rows_ref, s32[8,384]{1,0:T(8,128)S(1)} %get-tuple-element.91.pos_ref, f32[8,384]{1,0:T(8,128)S(1)} %get-tuple-element.92.ranks_ref, ...), custom_call_target="tpu_custom_call" | custom-call | flops 141950976 | bytes 933888 | tf_op jit(solution)/shard_map/pallas_call | solution.py:60
  28.7 1.3 %collective-permute-start.9 = (bf16[304,768]{1,0:T(8,128)(2,1)S(1)}, bf16[304,768]{1,0:T(8,128)(2,1)S(1)}, u32[]{:S(2)}, u32[]{:S(2)}) collective-permute-start(bf16[304,768]{1,0:T(8,128)(2,1)S(1)} %shard_map.52.own), channel_id=1, source_target_pairs={{32,0},{96,64},{160,128},{224,192},{2,32},{66,96},{130,160},{194,2... | collective-permute-start | bytes 1400840 | tf_op jit(solution)/shard_map/ppermute | solution.py:422
  30.0 2.7 %collective-permute-start.11 = (bf16[304,768]{1,0:T(8,128)(2,1)S(1)}, bf16[304,768]{1,0:T(8,128)(2,1)S(1)}, u32[]{:S(2)}, u32[]{:S(2)}) collective-permute-start(bf16[304,768]{1,0:T(8,128)(2,1)S(1)} %shard_map.52.own), channel_id=1, source_target_pairs={{192,0},{0,64},{64,128},{128,192},{224,32},{32,96},{96,160},{160,2... | collective-permute-start | bytes 1400840 | tf_op jit(solution)/shard_map/ppermute | solution.py:422
  32.8 0.6 shard_map.53
  33.3 1.6 %collective-permute-start.10 = (bf16[304,768]{1,0:T(8,128)(2,1)S(1)}, bf16[304,768]{1,0:T(8,128)(2,1)S(1)}, u32[]{:S(2)}, u32[]{:S(2)}) collective-permute-start(bf16[304,768]{1,0:T(8,128)(2,1)S(1)} %shard_map.52.own), channel_id=1, source_target_pairs={{34,0},{98,64},{162,128},{226,192},{0,32},{64,96},{128,160},{192,2... | collective-permute-start | bytes 1400840 | tf_op jit(solution)/shard_map/ppermute | solution.py:422
  34.9 0.0 collective-permute-start.12
  34.9 2.9 %collective-permute-done.9.x_first = bf16[304,768]{1,0:T(8,128)(2,1)S(1)} collective-permute-done((bf16[304,768]{1,0:T(8,128)(2,1)S(1)}, bf16[304,768]{1,0:T(8,128)(2,1)S(1)}, u32[]{:S(2)}, u32[]{:S(2)}) %collective-permute-start.9) | collective-permute-done | bytes 466976 | tf_op jit(solution)/shard_map/ppermute | solution.py:422
  37.7 0.6 collective-permute-start.13
  38.4 1.5 %collective-permute-done.11.y_first = bf16[304,768]{1,0:T(8,128)(2,1)S(1)} collective-permute-done((bf16[304,768]{1,0:T(8,128)(2,1)S(1)}, bf16[304,768]{1,0:T(8,128)(2,1)S(1)}, u32[]{:S(2)}, u32[]{:S(2)}) %collective-permute-start.11) | collective-permute-done | bytes 466976 | tf_op jit(solution)/shard_map/ppermute | solution.py:422
  39.9 3.4 %collective-permute-start.14 = (bf16[304,768]{1,0:T(8,128)(2,1)S(1)}, bf16[304,768]{1,0:T(8,128)(2,1)S(1)}, u32[]{:S(2)}, u32[]{:S(2)}) collective-permute-start(bf16[304,768]{1,0:T(8,128)(2,1)S(1)} %collective-permute-done.11.y_first), channel_id=1, source_target_pairs={{192,0},{0,64},{64,128},{128,192},{224,32},{32,96},{96,160},{160,2... | collective-permute-start | bytes 1400840 | tf_op jit(solution)/shard_map/ppermute | solution.py:422
  43.3 0.0 collective-permute-done.10.x_second
  43.3 2.8 %collective-permute-done.12.y_second = bf16[304,768]{1,0:T(8,128)(2,1)S(1)} collective-permute-done((bf16[304,768]{1,0:T(8,128)(2,1)S(1)}, bf16[304,768]{1,0:T(8,128)(2,1)S(1)}, u32[]{:S(2)}, u32[]{:S(2)}) %collective-permute-start.12) | collective-permute-done | bytes 466976 | tf_op jit(solution)/shard_map/ppermute | solution.py:422
  46.0 2.5 %shard_map.54 = (f32[8,384]{1,0:T(8,128)S(1)}, f32[2,304,128]{2,1,0:T(8,128)S(1)}, s32[32,128]{1,0:T(8,128)S(1)}) custom-call(bf16[304,768]{1,0:T(8,128)(2,1)S(1)} %shard_map.52.own, bf16[304,768]{1,0:T(8,128)(2,1)S(1)} %collective-permute-done.9.x_first, bf16[304,768]{1,0:T(8,128)(2,1)S(1)} %collective-permute-done.10.x_second, ...), custom_call_target="tpu_custom_call" | custom-call | flops 1135607808 | bytes 933888 | tf_op jit(solution)/shard_map/pallas_call | solution.py:60
  48.6 0.0 collective-permute-done.13.x_far
  48.6 0.9 %shard_map.55 = (f32[8,384]{1,0:T(8,128)S(1)}, s32[16,128]{1,0:T(8,128)S(1)}) custom-call(bf16[304,768]{1,0:T(8,128)(2,1)S(1)} %shard_map.52.own, bf16[304,768]{1,0:T(8,128)(2,1)S(1)} %collective-permute-done.11.y_first, bf16[304,768]{1,0:T(8,128)(2,1)S(1)} %collective-permute-done.12.y_second, bf16[304,768]{1,0:T(8,128)(2,1)S(1)} %collective-permute-done.13.x_far, ...), custom_call_target="tpu_custom_call" | custom-call | flops 425852928 | bytes 933888 | tf_op jit(solution)/shard_map/pallas_call | solution.py:60
  49.5 0.0 collective-permute-done.14.y_far
  49.5 2.1 %shard_map.56 = f32[64,1,128]{2,1,0:T(1,128)} custom-call(bf16[304,768]{1,0:T(8,128)(2,1)S(1)} %shard_map.52.own, bf16[304,768]{1,0:T(8,128)(2,1)S(1)} %collective-permute-done.9.x_first, bf16[304,768]{1,0:T(8,128)(2,1)S(1)} %collective-permute-done.10.x_second, bf16[304,768]{1,0:T(8,128)(2,1)S(1)} %collective-permute-done.11.y_first, ...), custom_call_target="tpu_custom_call" | custom-call | flops 567803904 | bytes 933888 | tf_op jit(solution)/shard_map/pallas_call | solution.py:60
  51.7 11.7 %all-to-all-start.1 = ((f32[64,1,128]{2,1,0:T(1,128)}), f32[64,1,128]{2,1,0:T(1,128)S(1)}, u32[]{:S(2)}, u32[]{:S(2)}) async-start(f32[64,1,128]{2,1,0:T(1,128)} %shard_map.56), calls=%async_computation.1 | async-start | bytes 65536 | tf_op jit(solution)/shard_map/all_to_all | solution.py:464
  63.4 9.2 %all-to-all-done.1.ans_ref = f32[64,1,128]{2,1,0:T(1,128)S(1)} async-done(((f32[64,1,128]{2,1,0:T(1,128)}), f32[64,1,128]{2,1,0:T(1,128)S(1)}, u32[]{:S(2)}, u32[]{:S(2)}) %all-to-all-start.1) | async-done | bytes 32800 | tf_op jit(solution)/shard_map/all_to_all | solution.py:464
  72.6 0.7 shard_map.57
  73.9 0.0 copy-start.1
  73.9 0.6 copy-done.1
  (2 shorter events, 0.0 us)
Async XLA Ops:
  0.0 1.6 %copy-start = (bf16[256,768]{1,0:T(8,128)(2,1)S(1)}, bf16[256,768]{1,0:T(8,128)(2,1)}, u32[]{:S(2)}) copy-start(bf16[256,768]{1,0:T(8,128)(2,1)} %emb_ref.1) | copy-start | bytes 1179652
  2.2 13.3 %collective-permute-start.2 = (bf16[608,128]{1,0:T(8,128)(2,1)S(1)}, bf16[608,128]{1,0:T(8,128)(2,1)S(1)}, u32[]{:S(2)}, u32[]{:S(2)}) collective-permute-start(bf16[608,128]{1,0:T(8,128)(2,1)S(1)} %get-tuple-element.85), channel_id=1, source_target_pairs={{0,8},{1,25},{4,12},{5,29},{8,16},{9,1},{12,20},{13,5},{16,24},{17... | collective-permute-start | bytes 466952 | tf_op jit(solution)/shard_map/ppermute | solution.py:393
  9.1 6.5 %collective-permute-start.1 = (bf16[304,128]{1,0:T(8,128)(2,1)S(1)}, bf16[304,128]{1,0:T(8,128)(2,1)S(1)}, u32[]{:S(2)}, u32[]{:S(2)}) collective-permute-start(bf16[304,128]{1,0:T(8,128)(2,1)S(1)} %get-tuple-element.84), channel_id=1, source_target_pairs={{0,4},{1,29},{4,8},{5,1},{8,12},{9,5},{12,16},{13,9},{16,20},{17,1... | collective-permute-start | bytes 233480 | tf_op jit(solution)/shard_map/ppermute | solution.py:393
  9.8 8.9 %collective-permute-start.3 = (bf16[304,128]{1,0:T(8,128)(2,1)S(1)}, bf16[304,128]{1,0:T(8,128)(2,1)S(1)}, u32[]{:S(2)}, u32[]{:S(2)}) collective-permute-start(bf16[304,128]{1,0:T(8,128)(2,1)S(1)} %get-tuple-element.86), channel_id=1, source_target_pairs={{0,12},{1,21},{4,16},{5,25},{8,20},{9,29},{12,24},{13,1},{16,28},{... | collective-permute-start | bytes 233480 | tf_op jit(solution)/shard_map/ppermute | solution.py:393
  10.4 9.6 %collective-permute-start.5 = (bf16[304,128]{1,0:T(8,128)(2,1)S(1)}, bf16[304,128]{1,0:T(8,128)(2,1)S(1)}, u32[]{:S(2)}, u32[]{:S(2)}) collective-permute-start(bf16[304,128]{1,0:T(8,128)(2,1)S(1)} %get-tuple-element.87), channel_id=1, source_target_pairs={{0,20},{1,13},{4,24},{5,17},{8,28},{9,21},{12,0},{13,25},{16,4},{1... | collective-permute-start | bytes 233480 | tf_op jit(solution)/shard_map/ppermute | solution.py:393
  13.1 8.6 %collective-permute-start.6 = (bf16[304,128]{1,0:T(8,128)(2,1)S(1)}, bf16[304,128]{1,0:T(8,128)(2,1)S(1)}, u32[]{:S(2)}, u32[]{:S(2)}) collective-permute-start(bf16[304,128]{1,0:T(8,128)(2,1)S(1)} %get-tuple-element.88), channel_id=1, source_target_pairs={{0,24},{1,9},{4,28},{5,13},{8,0},{9,17},{12,4},{13,21},{16,8},{17,... | collective-permute-start | bytes 233480 | tf_op jit(solution)/shard_map/ppermute | solution.py:393
  15.5 9.4 %collective-permute-start.7 = (bf16[304,128]{1,0:T(8,128)(2,1)S(1)}, bf16[304,128]{1,0:T(8,128)(2,1)S(1)}, u32[]{:S(2)}, u32[]{:S(2)}) collective-permute-start(bf16[304,128]{1,0:T(8,128)(2,1)S(1)} %get-tuple-element.89), channel_id=1, source_target_pairs={{0,28},{1,5},{4,0},{5,9},{8,4},{9,13},{12,8},{13,17},{16,12},{17,2... | collective-permute-start | bytes 233480 | tf_op jit(solution)/shard_map/ppermute | solution.py:393
  15.6 9.3 %collective-permute-start.4 = (bf16[304,128]{1,0:T(8,128)(2,1)S(1)}, bf16[304,128]{1,0:T(8,128)(2,1)S(1)}, u32[]{:S(2)}, u32[]{:S(2)}) collective-permute-start(bf16[304,128]{1,0:T(8,128)(2,1)S(1)} %slice.65), channel_id=1, source_target_pairs={{0,8},{1,25},{4,12},{5,29},{8,16},{9,1},{12,20},{13,5},{16,24},{17... | collective-permute-start | bytes 233480 | tf_op jit(solution)/shard_map/ppermute | solution.py:393
  25.0 2.9 %collective-permute-start.8 = (bf16[416,768]{1,0:T(8,128)(2,1)S(1)}, bf16[416,768]{1,0:T(8,128)(2,1)S(1)}, u32[]{:S(2)}, u32[]{:S(2)}) collective-permute-start(bf16[416,768]{1,0:T(8,128)(2,1)S(1)} %shard_map.50.own_ref), channel_id=1, source_target_pairs={{0,1},{1,0},{2,3},{3,2},{4,5},{5,4},{6,7},{7,6},{8,9},{9,8},{10,11... | collective-permute-start | bytes 1916936 | tf_op jit(solution)/shard_map/ppermute | solution.py:410
  28.7 9.0 %collective-permute-start.9 = (bf16[304,768]{1,0:T(8,128)(2,1)S(1)}, bf16[304,768]{1,0:T(8,128)(2,1)S(1)}, u32[]{:S(2)}, u32[]{:S(2)}) collective-permute-start(bf16[304,768]{1,0:T(8,128)(2,1)S(1)} %shard_map.52.own), channel_id=1, source_target_pairs={{32,0},{96,64},{160,128},{224,192},{2,32},{66,96},{130,160},{194,2... | collective-permute-start | bytes 1400840 | tf_op jit(solution)/shard_map/ppermute | solution.py:422
  30.0 9.8 %collective-permute-start.11 = (bf16[304,768]{1,0:T(8,128)(2,1)S(1)}, bf16[304,768]{1,0:T(8,128)(2,1)S(1)}, u32[]{:S(2)}, u32[]{:S(2)}) collective-permute-start(bf16[304,768]{1,0:T(8,128)(2,1)S(1)} %shard_map.52.own), channel_id=1, source_target_pairs={{192,0},{0,64},{64,128},{128,192},{224,32},{32,96},{96,160},{160,2... | collective-permute-start | bytes 1400840 | tf_op jit(solution)/shard_map/ppermute | solution.py:422
  33.3 10.0 %collective-permute-start.10 = (bf16[304,768]{1,0:T(8,128)(2,1)S(1)}, bf16[304,768]{1,0:T(8,128)(2,1)S(1)}, u32[]{:S(2)}, u32[]{:S(2)}) collective-permute-start(bf16[304,768]{1,0:T(8,128)(2,1)S(1)} %shard_map.52.own), channel_id=1, source_target_pairs={{34,0},{98,64},{162,128},{226,192},{0,32},{64,96},{128,160},{192,2... | collective-permute-start | bytes 1400840 | tf_op jit(solution)/shard_map/ppermute | solution.py:422
  34.9 11.2 %collective-permute-start.12 = (bf16[304,768]{1,0:T(8,128)(2,1)S(1)}, bf16[304,768]{1,0:T(8,128)(2,1)S(1)}, u32[]{:S(2)}, u32[]{:S(2)}) collective-permute-start(bf16[304,768]{1,0:T(8,128)(2,1)S(1)} %shard_map.52.own), channel_id=1, source_target_pairs={{64,0},{128,64},{192,128},{0,192},{96,32},{160,96},{224,160},{32,2... | collective-permute-start | bytes 1400840 | tf_op jit(solution)/shard_map/ppermute | solution.py:422
  37.7 10.8 %collective-permute-start.13 = (bf16[304,768]{1,0:T(8,128)(2,1)S(1)}, bf16[304,768]{1,0:T(8,128)(2,1)S(1)}, u32[]{:S(2)}, u32[]{:S(2)}) collective-permute-start(bf16[304,768]{1,0:T(8,128)(2,1)S(1)} %collective-permute-done.9.x_first), channel_id=1, source_target_pairs={{32,0},{96,64},{160,128},{224,192},{2,32},{66,96},{130,160},{194,2... | collective-permute-start | bytes 1400840 | tf_op jit(solution)/shard_map/ppermute | solution.py:422
  39.9 9.6 %collective-permute-start.14 = (bf16[304,768]{1,0:T(8,128)(2,1)S(1)}, bf16[304,768]{1,0:T(8,128)(2,1)S(1)}, u32[]{:S(2)}, u32[]{:S(2)}) collective-permute-start(bf16[304,768]{1,0:T(8,128)(2,1)S(1)} %collective-permute-done.11.y_first), channel_id=1, source_target_pairs={{192,0},{0,64},{64,128},{128,192},{224,32},{32,96},{96,160},{160,2... | collective-permute-start | bytes 1400840 | tf_op jit(solution)/shard_map/ppermute | solution.py:422
  51.7 20.9 %all-to-all-start.1 = ((f32[64,1,128]{2,1,0:T(1,128)}), f32[64,1,128]{2,1,0:T(1,128)S(1)}, u32[]{:S(2)}, u32[]{:S(2)}) async-start(f32[64,1,128]{2,1,0:T(1,128)} %shard_map.56), calls=%async_computation.1 | async-start | bytes 65536 | tf_op jit(solution)/shard_map/all_to_all | solution.py:464
  73.9 0.6 copy-start.1

commit v4 on v3

--- a/solution.py
+++ b/solution.py
@@ -256,43 +256,17 @@
         best_ref[i : i + 1, :CAP] = best
 
 
-def mid_kernel(own, y_first, y_second, x_far, own_columns, columns_ref, out_ref, places_ref):
-    ranks = row_ranks(x_far)
-    best = earlier_best(x_far, ranks, own, own_columns[:, 0:1])
-    for i, key in enumerate((y_first, y_second)):
-        best = jnp.maximum(best, earlier_best(x_far, ranks, key, columns_ref[i, :, 0:1]))
-    out_ref[...] = jnp.full((8, CAPL), -1.0, jnp.float32)
-    out_ref[0:1, :CAP] = best
-    places_ref[...] = slot_places(x_far)
-
-
-def far_kernel(
-    own, x_first, x_second, y_first, y_second, x_far, y_far,
-    own_places, near_ref, near_places, mid_ref, mid_places, out_ref,
-):
-    queries, keys = (own, x_first, x_second, x_far), (y_first, y_second, y_far)
-    far_columns = column_ranks(y_far, make_eye())
-    over = 0.0
-    for block in queries + keys:
+def overflow(blocks):
+    over = jnp.zeros((1, 1), jnp.float32)
+    for block in blocks:
         tail = block[LAST:, CAPL - META : CAPL].astype(jnp.float32)
         over = jnp.maximum(over, tail[13:14, META - 1 :])
-    over = jnp.where(over > NEVER, 1.0, 0.0)
+    return jnp.where(over > NEVER, OVER, 0.0)
+
+
+def message_order():
     my_core, my_z = lax.axis_index("core"), lax.axis_index("z")
     my_x = 2 * lax.axis_index("xh") + lax.axis_index("xl")
-    rows = []
-    for i, query in enumerate(queries):
-        best = earlier_best(query, row_ranks(query), y_far, far_columns)
-        best = jnp.maximum(best, near_ref[i : i + 1, :CAP] if i < 3 else mid_ref[0:1, :CAP])
-        best = jnp.concatenate([best, jnp.full((1, CAPL - CAP), -1.0, jnp.float32)], axis=1)
-        rows.append(jnp.broadcast_to(best, (16, CAPL)))
-    rows = jnp.concatenate(rows, axis=0)
-    places = jnp.concatenate([own_places[...], near_places[...], mid_places[...]], axis=0)
-    found = jnp.full((64, META), -1.0, jnp.float32)
-    for part in range(CAPL // META):
-        values = rows[:, part * META : (part + 1) * META]
-        picked = jnp.take_along_axis(values, places & (META - 1), axis=1, mode="promise_in_bounds")
-        found = jnp.where((places >> 7) == part, picked, found)
-    found = found + OVER * over
     messages = GROUPS * 8
     row, column = iota((messages, messages), 0), iota((messages, messages), 1)
     core = row & 1
@@ -301,9 +275,47 @@
     x_away = signed(my_core, (row >> 5) + (row & 2) - my_x) & 3
     block = jnp.where(x_away == 2, 3, jnp.where(x_away == 3, 2, x_away))
     wanted = block * 16 + (core ^ my_core) * GROUPS + steps
-    order = jnp.where(column == wanted, 1.0, 0.0).astype(jnp.bfloat16)
-    out = dot(jnp.concatenate([order] * 3, axis=1), jnp.concatenate(split3(found), axis=0), ((1,), (0,)))
-    for i in range(messages):
+    return jnp.where(column == wanted, 1.0, 0.0).astype(jnp.bfloat16)
+
+
+def mid_kernel(
+    own, x_first, x_second, y_first, y_second, x_far, own_columns, columns_ref, own_places, near_places,
+    out_ref, places_ref, order_ref, over_ref,
+):
+    ranks = row_ranks(x_far)
+    best = earlier_best(x_far, ranks, own, own_columns[:, 0:1])
+    for i, key in enumerate((y_first, y_second)):
+        best = jnp.maximum(best, earlier_best(x_far, ranks, key, columns_ref[i, :, 0:1]))
+    out_ref[...] = jnp.full((8, CAPL), -1.0, jnp.float32)
+    out_ref[0:1, :CAP] = best
+    places_ref[:16, :] = own_places[...]
+    places_ref[16:48, :] = near_places[...]
+    places_ref[48:, :] = slot_places(x_far)
+    order_ref[...] = jnp.concatenate([message_order()] * 3, axis=1)
+    over = overflow((own, x_first, x_second, y_first, y_second, x_far))
+    over_ref[...] = jnp.broadcast_to(over, (8, META))
+
+
+def far_kernel(
+    own, x_first, x_second, x_far, y_far, near_ref, mid_ref, places_ref, order_ref, over_ref, out_ref
+):
+    far_columns = column_ranks(y_far, make_eye())
+    over = jnp.maximum(overflow((y_far,)), over_ref[0:1, 0:1])
+    rows = []
+    for i, query in enumerate((own, x_first, x_second, x_far)):
+        best = earlier_best(query, row_ranks(query), y_far, far_columns)
+        best = jnp.maximum(best, near_ref[i : i + 1, :CAP] if i < 3 else mid_ref[0:1, :CAP])
+        best = jnp.concatenate([best, jnp.full((1, CAPL - CAP), -1.0, jnp.float32)], axis=1)
+        rows.append(jnp.broadcast_to(best, (16, CAPL)))
+    rows = jnp.concatenate(rows, axis=0)
+    places = places_ref[...]
+    found = jnp.full((64, META), -1.0, jnp.float32)
+    for part in range(CAPL // META):
+        values = rows[:, part * META : (part + 1) * META]
+        picked = jnp.take_along_axis(values, places & (META - 1), axis=1, mode="promise_in_bounds")
+        found = jnp.where((places >> 7) == part, picked, found)
+    out = dot(order_ref[...], jnp.concatenate(split3(found + over), axis=0), ((1,), (0,)))
+    for i in range(GROUPS * 8):
         out_ref[i] = out[i : i + 1, :]
 
 
@@ -437,28 +449,28 @@
         own_columns,
         cost=8,
     )
-    mid, mid_places = call(
+    mid, places, order, over = call(
         mid_kernel,
-        (best_shape, places_shape),
-        block,
-        y_first,
-        y_second,
+        (best_shape, shape((64, META), i32), shape((64, 192), bf16), shape((8, META), f32)),
+        *near_blocks,
         x_far,
         own_columns,
         columns,
+        own_places,
+        near_places,
         cost=3,
     )
     message = call(
         far_kernel,
         shape((64, 1, META), f32),
-        *near_blocks,
+        *near_blocks[:3],
         x_far,
         y_far,
-        own_places,
         near,
-        near_places,
         mid,
-        mid_places,
+        places,
+        order,
+        over,
         cost=4,
     )
     answer = lax.all_to_all(message, RETURN, split_axis=0, concat_axis=0, tiled=True)

time: 74.6 us -> 74.7 us (level)
  no operation moved by 1% of the time
where the time goes in v4:
time: 74.7 us; the launch traced here: 74.5 us
  starting transfers between devices  39 us (52%)
  waiting for transfers between devices  23.4 us (31%)
  Pallas kernels  9.27 us (12%)
  between operations  1.41 us (2%)
  other arithmetic  0.75 us (1%)
    ppermute x7, starting transfers between devices, body(): send = lambda v, steps: lax.ppermute(v, COLUMN, column_shift(steps))  16.5 us
    all_to_all x1, starting transfers between devices, body(): lax.all_to_all(message, RETURN, split_axis=0, concat_axis=0, tiled=True)  11.7 us
    ppermute x6, starting transfers between devices, body(): bring = lambda v, dx, dy: lax.ppermute(v, PLANE, plane_shift(dx, dy))  9.6 us
    pallas_call x10, Pallas kernels, call(): pl.pallas_call(kernel, out_shape=out, in_specs=[space(i, smem) for i in r...  9.27 us
    all_to_all x1, waiting for transfers between devices, body(): lax.all_to_all(message, RETURN, split_axis=0, concat_axis=0, tiled=True)  9.17 us
    ppermute x6, waiting for transfers between devices, body(): bring = lambda v, dx, dy: lax.ppermute(v, PLANE, plane_shift(dx, dy))  7.15 us
    ppermute x7, waiting for transfers between devices, body(): send = lambda v, steps: lax.ppermute(v, COLUMN, column_shift(steps))  6.21 us
  transfers between devices with their start and end apart: 15, of which 9 were waited for; matrix products, arithmetic and copies ran while one was open for 0% of the time, Pallas kernels for 6%

profile of v4, /device:TPU:1, one launch (start us, length us, event | category | flops | bytes accessed | tf_op | source)
XLA Modules:
  0.0 74.5 jit_solution(14418373572381444924)
XLA Ops:
  0.0 0.0 copy-start
  0.0 0.7 %multiply_add_fusion = s32[256]{0:T(256)S(1)} fusion(s32[256]{0:T(256)} %param.9, s32[256]{0:T(256)} %param.10), kind=kLoop, calls=%fused_computation.24 | loop fusion | flops 512 | bytes 3072 | tf_op jit(solution)/shard_map/add | solution.py:393
  0.8 0.2 shard_map.48
  1.6 0.0 copy-done
  1.7 0.5 shard_map.49
  2.2 6.9 %collective-permute-start.2 = (bf16[608,128]{1,0:T(8,128)(2,1)S(1)}, bf16[608,128]{1,0:T(8,128)(2,1)S(1)}, u32[]{:S(2)}, u32[]{:S(2)}) collective-permute-start(bf16[608,128]{1,0:T(8,128)(2,1)S(1)} %get-tuple-element.87), channel_id=1, source_target_pairs={{0,8},{1,25},{4,12},{5,29},{8,16},{9,1},{12,20},{13,5},{16,24},{17... | collective-permute-start | bytes 466952 | tf_op jit(solution)/shard_map/ppermute | solution.py:405
  9.1 0.7 collective-permute-start.1
  9.8 0.5 collective-permute-start.3
  10.4 2.7 %collective-permute-start.5 = (bf16[304,128]{1,0:T(8,128)(2,1)S(1)}, bf16[304,128]{1,0:T(8,128)(2,1)S(1)}, u32[]{:S(2)}, u32[]{:S(2)}) collective-permute-start(bf16[304,128]{1,0:T(8,128)(2,1)S(1)} %get-tuple-element.89), channel_id=1, source_target_pairs={{0,20},{1,13},{4,24},{5,17},{8,28},{9,21},{12,0},{13,25},{16,4},{1... | collective-permute-start | bytes 233480 | tf_op jit(solution)/shard_map/ppermute | solution.py:405
  13.1 2.4 %collective-permute-start.6 = (bf16[304,128]{1,0:T(8,128)(2,1)S(1)}, bf16[304,128]{1,0:T(8,128)(2,1)S(1)}, u32[]{:S(2)}, u32[]{:S(2)}) collective-permute-start(bf16[304,128]{1,0:T(8,128)(2,1)S(1)} %get-tuple-element.90), channel_id=1, source_target_pairs={{0,24},{1,9},{4,28},{5,13},{8,0},{9,17},{12,4},{13,21},{16,8},{17,... | collective-permute-start | bytes 233480 | tf_op jit(solution)/shard_map/ppermute | solution.py:405
  15.5 0.0 collective-permute-done.2.refs_2_
  15.5 0.0 collective-permute-start.7
  15.5 0.1 collective-permute-done.1.refs_1_
  15.6 3.1 %collective-permute-start.4 = (bf16[304,128]{1,0:T(8,128)(2,1)S(1)}, bf16[304,128]{1,0:T(8,128)(2,1)S(1)}, u32[]{:S(2)}, u32[]{:S(2)}) collective-permute-start(bf16[304,128]{1,0:T(8,128)(2,1)S(1)} %slice.65), channel_id=1, source_target_pairs={{0,8},{1,25},{4,12},{5,29},{8,16},{9,1},{12,20},{13,5},{16,24},{17... | collective-permute-start | bytes 233480 | tf_op jit(solution)/shard_map/ppermute | solution.py:405
  18.7 0.0 collective-permute-done.3.refs_3_
  18.7 1.3 %collective-permute-done.5.refs_5_ = bf16[304,128]{1,0:T(8,128)(2,1)S(1)} collective-permute-done((bf16[304,128]{1,0:T(8,128)(2,1)S(1)}, bf16[304,128]{1,0:T(8,128)(2,1)S(1)}, u32[]{:S(2)}, u32[]{:S(2)}) %collective-permute-start.5) | collective-permute-done | bytes 77856 | tf_op jit(solution)/shard_map/ppermute | solution.py:405
  20.0 1.7 %collective-permute-done.6.refs_6_ = bf16[304,128]{1,0:T(8,128)(2,1)S(1)} collective-permute-done((bf16[304,128]{1,0:T(8,128)(2,1)S(1)}, bf16[304,128]{1,0:T(8,128)(2,1)S(1)}, u32[]{:S(2)}, u32[]{:S(2)}) %collective-permute-start.6) | collective-permute-done | bytes 77856 | tf_op jit(solution)/shard_map/ppermute | solution.py:405
  21.7 3.1 %collective-permute-done.7.refs_7_ = bf16[304,128]{1,0:T(8,128)(2,1)S(1)} collective-permute-done((bf16[304,128]{1,0:T(8,128)(2,1)S(1)}, bf16[304,128]{1,0:T(8,128)(2,1)S(1)}, u32[]{:S(2)}, u32[]{:S(2)}) %collective-permute-start.7) | collective-permute-done | bytes 77856 | tf_op jit(solution)/shard_map/ppermute | solution.py:405
  24.9 0.0 collective-permute-done.4.refs_4_
  24.9 0.1 shard_map.50.own_ref
  25.0 1.2 %collective-permute-start.8 = (bf16[416,768]{1,0:T(8,128)(2,1)S(1)}, bf16[416,768]{1,0:T(8,128)(2,1)S(1)}, u32[]{:S(2)}, u32[]{:S(2)}) collective-permute-start(bf16[416,768]{1,0:T(8,128)(2,1)S(1)} %shard_map.50.own_ref), channel_id=1, source_target_pairs={{0,1},{1,0},{2,3},{3,2},{4,5},{5,4},{6,7},{7,6},{8,9},{9,8},{10,11... | collective-permute-start | bytes 1916936 | tf_op jit(solution)/shard_map/ppermute | solution.py:422
  26.2 0.8 %shard_map.51 = (bf16[304,768]{1,0:T(8,128)(2,1)S(1)}, s32[8,384]{1,0:T(8,128)S(1)}, f32[8,384]{1,0:T(8,128)S(1)}, f32[8,128]{1,0:T(8,128)S(1)}) custom-call(bf16[416,768]{1,0:T(8,128)(2,1)S(1)} %shard_map.50.own_ref), custom_call_target="tpu_custom_call" | custom-call | flops 141950976 | bytes 933888 | tf_op jit(solution)/shard_map/pallas_call | solution.py:60
  27.0 0.9 %collective-permute-done.8.other_ref = bf16[416,768]{1,0:T(8,128)(2,1)S(1)} collective-permute-done((bf16[416,768]{1,0:T(8,128)(2,1)S(1)}, bf16[416,768]{1,0:T(8,128)(2,1)S(1)}, u32[]{:S(2)}, u32[]{:S(2)}) %collective-permute-start.8) | collective-permute-done | bytes 639008 | tf_op jit(solution)/shard_map/ppermute | solution.py:422
  27.9 0.8 %shard_map.52.own = bf16[304,768]{1,0:T(8,128)(2,1)S(1)} custom-call(bf16[416,768]{1,0:T(8,128)(2,1)S(1)} %collective-permute-done.8.other_ref, bf16[304,768]{1,0:T(8,128)(2,1)S(1)} %get-tuple-element.92.rows_ref, s32[8,384]{1,0:T(8,128)S(1)} %get-tuple-element.93.pos_ref, f32[8,384]{1,0:T(8,128)S(1)} %get-tuple-element.94.ranks_ref, ...), custom_call_target="tpu_custom_call" | custom-call | flops 141950976 | bytes 933888 | tf_op jit(solution)/shard_map/pallas_call | solution.py:60
  28.7 1.3 %collective-permute-start.9 = (bf16[304,768]{1,0:T(8,128)(2,1)S(1)}, bf16[304,768]{1,0:T(8,128)(2,1)S(1)}, u32[]{:S(2)}, u32[]{:S(2)}) collective-permute-start(bf16[304,768]{1,0:T(8,128)(2,1)S(1)} %shard_map.52.own), channel_id=1, source_target_pairs={{32,0},{96,64},{160,128},{224,192},{2,32},{66,96},{130,160},{194,2... | collective-permute-start | bytes 1400840 | tf_op jit(solution)/shard_map/ppermute | solution.py:434
  30.0 2.7 %collective-permute-start.12 = (bf16[304,768]{1,0:T(8,128)(2,1)S(1)}, bf16[304,768]{1,0:T(8,128)(2,1)S(1)}, u32[]{:S(2)}, u32[]{:S(2)}) collective-permute-start(bf16[304,768]{1,0:T(8,128)(2,1)S(1)} %shard_map.52.own), channel_id=1, source_target_pairs={{192,0},{0,64},{64,128},{128,192},{224,32},{32,96},{96,160},{160,2... | collective-permute-start | bytes 1400840 | tf_op jit(solution)/shard_map/ppermute | solution.py:434
  32.8 0.6 shard_map.53
  33.3 1.6 %collective-permute-start.10 = (bf16[304,768]{1,0:T(8,128)(2,1)S(1)}, bf16[304,768]{1,0:T(8,128)(2,1)S(1)}, u32[]{:S(2)}, u32[]{:S(2)}) collective-permute-start(bf16[304,768]{1,0:T(8,128)(2,1)S(1)} %shard_map.52.own), channel_id=1, source_target_pairs={{34,0},{98,64},{162,128},{226,192},{0,32},{64,96},{128,160},{192,2... | collective-permute-start | bytes 1400840 | tf_op jit(solution)/shard_map/ppermute | solution.py:434
  34.9 0.0 collective-permute-start.14
  34.9 2.9 %collective-permute-done.9.x_first = bf16[304,768]{1,0:T(8,128)(2,1)S(1)} collective-permute-done((bf16[304,768]{1,0:T(8,128)(2,1)S(1)}, bf16[304,768]{1,0:T(8,128)(2,1)S(1)}, u32[]{:S(2)}, u32[]{:S(2)}) %collective-permute-start.9) | collective-permute-done | bytes 466976 | tf_op jit(solution)/shard_map/ppermute | solution.py:434
  37.7 0.6 collective-permute-start.11
  38.4 1.5 %collective-permute-done.12.y_first = bf16[304,768]{1,0:T(8,128)(2,1)S(1)} collective-permute-done((bf16[304,768]{1,0:T(8,128)(2,1)S(1)}, bf16[304,768]{1,0:T(8,128)(2,1)S(1)}, u32[]{:S(2)}, u32[]{:S(2)}) %collective-permute-start.12) | collective-permute-done | bytes 466976 | tf_op jit(solution)/shard_map/ppermute | solution.py:434
  39.9 3.4 %collective-permute-start.13 = (bf16[304,768]{1,0:T(8,128)(2,1)S(1)}, bf16[304,768]{1,0:T(8,128)(2,1)S(1)}, u32[]{:S(2)}, u32[]{:S(2)}) collective-permute-start(bf16[304,768]{1,0:T(8,128)(2,1)S(1)} %collective-permute-done.12.y_first), channel_id=1, source_target_pairs={{192,0},{0,64},{64,128},{128,192},{224,32},{32,96},{96,160},{160,2... | collective-permute-start | bytes 1400840 | tf_op jit(solution)/shard_map/ppermute | solution.py:434
  43.3 0.0 collective-permute-done.10.x_second
  43.3 2.8 %collective-permute-done.14.y_second = bf16[304,768]{1,0:T(8,128)(2,1)S(1)} collective-permute-done((bf16[304,768]{1,0:T(8,128)(2,1)S(1)}, bf16[304,768]{1,0:T(8,128)(2,1)S(1)}, u32[]{:S(2)}, u32[]{:S(2)}) %collective-permute-start.14) | collective-permute-done | bytes 466976 | tf_op jit(solution)/shard_map/ppermute | solution.py:434
  46.0 2.5 %shard_map.54 = (f32[8,384]{1,0:T(8,128)S(1)}, f32[2,304,128]{2,1,0:T(8,128)S(1)}, s32[32,128]{1,0:T(8,128)S(1)}) custom-call(bf16[304,768]{1,0:T(8,128)(2,1)S(1)} %shard_map.52.own, bf16[304,768]{1,0:T(8,128)(2,1)S(1)} %collective-permute-done.9.x_first, bf16[304,768]{1,0:T(8,128)(2,1)S(1)} %collective-permute-done.10.x_second, ...), custom_call_target="tpu_custom_call" | custom-call | flops 1135607808 | bytes 933888 | tf_op jit(solution)/shard_map/pallas_call | solution.py:60
  48.6 0.0 collective-permute-done.11.x_far
  48.6 1.0 %shard_map.55 = (f32[8,384]{1,0:T(8,128)S(1)}, s32[64,128]{1,0:T(8,128)S(1)}, bf16[64,192]{1,0:T(8,128)(2,1)S(1)}, f32[8,128]{1,0:T(8,128)S(1)}) custom-call(bf16[304,768]{1,0:T(8,128)(2,1)S(1)} %shard_map.52.own, bf16[304,768]{1,0:T(8,128)(2,1)S(1)} %collective-permute-done.9.x_first, bf16[304,768]{1,0:T(8,128)(2,1)S(1)} %collective-permute-done.10.x_second, ...), custom_call_target="tpu_custom_call" | custom-call | flops 425852928 | bytes 933888 | tf_op jit(solution)/shard_map/pallas_call | solution.py:60
  49.5 0.0 collective-permute-done.13.y_far
  49.5 2.1 %shard_map.56 = f32[64,1,128]{2,1,0:T(1,128)} custom-call(bf16[304,768]{1,0:T(8,128)(2,1)S(1)} %shard_map.52.own, bf16[304,768]{1,0:T(8,128)(2,1)S(1)} %collective-permute-done.9.x_first, bf16[304,768]{1,0:T(8,128)(2,1)S(1)} %collective-permute-done.10.x_second, bf16[304,768]{1,0:T(8,128)(2,1)S(1)} %collective-permute-done.11.x_far, ...), custom_call_target="tpu_custom_call" | custom-call | flops 567803904 | bytes 933888 | tf_op jit(solution)/shard_map/pallas_call | solution.py:60
  51.7 11.7 %all-to-all-start.1 = ((f32[64,1,128]{2,1,0:T(1,128)}), f32[64,1,128]{2,1,0:T(1,128)S(1)}, u32[]{:S(2)}, u32[]{:S(2)}) async-start(f32[64,1,128]{2,1,0:T(1,128)} %shard_map.56), calls=%async_computation.1 | async-start | bytes 65536 | tf_op jit(solution)/shard_map/all_to_all | solution.py:476
  63.4 9.2 %all-to-all-done.1.ans_ref = f32[64,1,128]{2,1,0:T(1,128)S(1)} async-done(((f32[64,1,128]{2,1,0:T(1,128)}), f32[64,1,128]{2,1,0:T(1,128)S(1)}, u32[]{:S(2)}, u32[]{:S(2)}) %all-to-all-start.1) | async-done | bytes 32800 | tf_op jit(solution)/shard_map/all_to_all | solution.py:476
  72.6 0.7 shard_map.57
  73.9 0.0 copy-start.1
  73.9 0.6 copy-done.1
  (2 shorter events, 0.0 us)
Async XLA Ops:
  0.0 1.6 %copy-start = (bf16[256,768]{1,0:T(8,128)(2,1)S(1)}, bf16[256,768]{1,0:T(8,128)(2,1)}, u32[]{:S(2)}) copy-start(bf16[256,768]{1,0:T(8,128)(2,1)} %emb_ref.1) | copy-start | bytes 1179652
  2.2 13.3 %collective-permute-start.2 = (bf16[608,128]{1,0:T(8,128)(2,1)S(1)}, bf16[608,128]{1,0:T(8,128)(2,1)S(1)}, u32[]{:S(2)}, u32[]{:S(2)}) collective-permute-start(bf16[608,128]{1,0:T(8,128)(2,1)S(1)} %get-tuple-element.87), channel_id=1, source_target_pairs={{0,8},{1,25},{4,12},{5,29},{8,16},{9,1},{12,20},{13,5},{16,24},{17... | collective-permute-start | bytes 466952 | tf_op jit(solution)/shard_map/ppermute | solution.py:405
  9.1 6.5 %collective-permute-start.1 = (bf16[304,128]{1,0:T(8,128)(2,1)S(1)}, bf16[304,128]{1,0:T(8,128)(2,1)S(1)}, u32[]{:S(2)}, u32[]{:S(2)}) collective-permute-start(bf16[304,128]{1,0:T(8,128)(2,1)S(1)} %get-tuple-element.86), channel_id=1, source_target_pairs={{0,4},{1,29},{4,8},{5,1},{8,12},{9,5},{12,16},{13,9},{16,20},{17,1... | collective-permute-start | bytes 233480 | tf_op jit(solution)/shard_map/ppermute | solution.py:405
  9.8 8.9 %collective-permute-start.3 = (bf16[304,128]{1,0:T(8,128)(2,1)S(1)}, bf16[304,128]{1,0:T(8,128)(2,1)S(1)}, u32[]{:S(2)}, u32[]{:S(2)}) collective-permute-start(bf16[304,128]{1,0:T(8,128)(2,1)S(1)} %get-tuple-element.88), channel_id=1, source_target_pairs={{0,12},{1,21},{4,16},{5,25},{8,20},{9,29},{12,24},{13,1},{16,28},{... | collective-permute-start | bytes 233480 | tf_op jit(solution)/shard_map/ppermute | solution.py:405
  10.4 9.6 %collective-permute-start.5 = (bf16[304,128]{1,0:T(8,128)(2,1)S(1)}, bf16[304,128]{1,0:T(8,128)(2,1)S(1)}, u32[]{:S(2)}, u32[]{:S(2)}) collective-permute-start(bf16[304,128]{1,0:T(8,128)(2,1)S(1)} %get-tuple-element.89), channel_id=1, source_target_pairs={{0,20},{1,13},{4,24},{5,17},{8,28},{9,21},{12,0},{13,25},{16,4},{1... | collective-permute-start | bytes 233480 | tf_op jit(solution)/shard_map/ppermute | solution.py:405
  13.1 8.6 %collective-permute-start.6 = (bf16[304,128]{1,0:T(8,128)(2,1)S(1)}, bf16[304,128]{1,0:T(8,128)(2,1)S(1)}, u32[]{:S(2)}, u32[]{:S(2)}) collective-permute-start(bf16[304,128]{1,0:T(8,128)(2,1)S(1)} %get-tuple-element.90), channel_id=1, source_target_pairs={{0,24},{1,9},{4,28},{5,13},{8,0},{9,17},{12,4},{13,21},{16,8},{17,... | collective-permute-start | bytes 233480 | tf_op jit(solution)/shard_map/ppermute | solution.py:405
  15.5 9.4 %collective-permute-start.7 = (bf16[304,128]{1,0:T(8,128)(2,1)S(1)}, bf16[304,128]{1,0:T(8,128)(2,1)S(1)}, u32[]{:S(2)}, u32[]{:S(2)}) collective-permute-start(bf16[304,128]{1,0:T(8,128)(2,1)S(1)} %get-tuple-element.91), channel_id=1, source_target_pairs={{0,28},{1,5},{4,0},{5,9},{8,4},{9,13},{12,8},{13,17},{16,12},{17,2... | collective-permute-start | bytes 233480 | tf_op jit(solution)/shard_map/ppermute | solution.py:405
  15.6 9.3 %collective-permute-start.4 = (bf16[304,128]{1,0:T(8,128)(2,1)S(1)}, bf16[304,128]{1,0:T(8,128)(2,1)S(1)}, u32[]{:S(2)}, u32[]{:S(2)}) collective-permute-start(bf16[304,128]{1,0:T(8,128)(2,1)S(1)} %slice.65), channel_id=1, source_target_pairs={{0,8},{1,25},{4,12},{5,29},{8,16},{9,1},{12,20},{13,5},{16,24},{17... | collective-permute-start | bytes 233480 | tf_op jit(solution)/shard_map/ppermute | solution.py:405
  25.0 2.9 %collective-permute-start.8 = (bf16[416,768]{1,0:T(8,128)(2,1)S(1)}, bf16[416,768]{1,0:T(8,128)(2,1)S(1)}, u32[]{:S(2)}, u32[]{:S(2)}) collective-permute-start(bf16[416,768]{1,0:T(8,128)(2,1)S(1)} %shard_map.50.own_ref), channel_id=1, source_target_pairs={{0,1},{1,0},{2,3},{3,2},{4,5},{5,4},{6,7},{7,6},{8,9},{9,8},{10,11... | collective-permute-start | bytes 1916936 | tf_op jit(solution)/shard_map/ppermute | solution.py:422
  28.7 9.0 %collective-permute-start.9 = (bf16[304,768]{1,0:T(8,128)(2,1)S(1)}, bf16[304,768]{1,0:T(8,128)(2,1)S(1)}, u32[]{:S(2)}, u32[]{:S(2)}) collective-permute-start(bf16[304,768]{1,0:T(8,128)(2,1)S(1)} %shard_map.52.own), channel_id=1, source_target_pairs={{32,0},{96,64},{160,128},{224,192},{2,32},{66,96},{130,160},{194,2... | collective-permute-start | bytes 1400840 | tf_op jit(solution)/shard_map/ppermute | solution.py:434
  30.0 9.8 %collective-permute-start.12 = (bf16[304,768]{1,0:T(8,128)(2,1)S(1)}, bf16[304,768]{1,0:T(8,128)(2,1)S(1)}, u32[]{:S(2)}, u32[]{:S(2)}) collective-permute-start(bf16[304,768]{1,0:T(8,128)(2,1)S(1)} %shard_map.52.own), channel_id=1, source_target_pairs={{192,0},{0,64},{64,128},{128,192},{224,32},{32,96},{96,160},{160,2... | collective-permute-start | bytes 1400840 | tf_op jit(solution)/shard_map/ppermute | solution.py:434
  33.3 10.0 %collective-permute-start.10 = (bf16[304,768]{1,0:T(8,128)(2,1)S(1)}, bf16[304,768]{1,0:T(8,128)(2,1)S(1)}, u32[]{:S(2)}, u32[]{:S(2)}) collective-permute-start(bf16[304,768]{1,0:T(8,128)(2,1)S(1)} %shard_map.52.own), channel_id=1, source_target_pairs={{34,0},{98,64},{162,128},{226,192},{0,32},{64,96},{128,160},{192,2... | collective-permute-start | bytes 1400840 | tf_op jit(solution)/shard_map/ppermute | solution.py:434
  34.9 11.2 %collective-permute-start.14 = (bf16[304,768]{1,0:T(8,128)(2,1)S(1)}, bf16[304,768]{1,0:T(8,128)(2,1)S(1)}, u32[]{:S(2)}, u32[]{:S(2)}) collective-permute-start(bf16[304,768]{1,0:T(8,128)(2,1)S(1)} %shard_map.52.own), channel_id=1, source_target_pairs={{64,0},{128,64},{192,128},{0,192},{96,32},{160,96},{224,160},{32,2... | collective-permute-start | bytes 1400840 | tf_op jit(solution)/shard_map/ppermute | solution.py:434
  37.7 10.8 %collective-permute-start.11 = (bf16[304,768]{1,0:T(8,128)(2,1)S(1)}, bf16[304,768]{1,0:T(8,128)(2,1)S(1)}, u32[]{:S(2)}, u32[]{:S(2)}) collective-permute-start(bf16[304,768]{1,0:T(8,128)(2,1)S(1)} %collective-permute-done.9.x_first), channel_id=1, source_target_pairs={{32,0},{96,64},{160,128},{224,192},{2,32},{66,96},{130,160},{194,2... | collective-permute-start | bytes 1400840 | tf_op jit(solution)/shard_map/ppermute | solution.py:434
  39.9 9.7 %collective-permute-start.13 = (bf16[304,768]{1,0:T(8,128)(2,1)S(1)}, bf16[304,768]{1,0:T(8,128)(2,1)S(1)}, u32[]{:S(2)}, u32[]{:S(2)}) collective-permute-start(bf16[304,768]{1,0:T(8,128)(2,1)S(1)} %collective-permute-done.12.y_first), channel_id=1, source_target_pairs={{192,0},{0,64},{64,128},{128,192},{224,32},{32,96},{96,160},{160,2... | collective-permute-start | bytes 1400840 | tf_op jit(solution)/shard_map/ppermute | solution.py:434
  51.7 20.9 %all-to-all-start.1 = ((f32[64,1,128]{2,1,0:T(1,128)}), f32[64,1,128]{2,1,0:T(1,128)S(1)}, u32[]{:S(2)}, u32[]{:S(2)}) async-start(f32[64,1,128]{2,1,0:T(1,128)} %shard_map.56), calls=%async_computation.1 | async-start | bytes 65536 | tf_op jit(solution)/shard_map/all_to_all | solution.py:476
  73.9 0.6 copy-start.1

commit v5 on v3

--- a/solution.py
+++ b/solution.py
@@ -298,7 +298,7 @@
     core = row & 1
     away = my_z - ((row >> 2) & 7)
     steps = jnp.where(core == 0, away, -away) & 7
-    x_away = signed(my_core, (row >> 5) + (row & 2) - my_x) & 3
+    x_away = signed(my_core, my_x - (row >> 5) - (row & 2)) & 3
     block = jnp.where(x_away == 2, 3, jnp.where(x_away == 3, 2, x_away))
     wanted = block * 16 + (core ^ my_core) * GROUPS + steps
     order = jnp.where(column == wanted, 1.0, 0.0).astype(jnp.bfloat16)
@@ -420,14 +420,14 @@
     )
     block = call(compact_kernel, shape((CAP, WIDTH), bf16), other, *first)
     bring = lambda v, dx, dy: lax.ppermute(v, PLANE, plane_shift(dx, dy))
-    x_first, y_first = bring(block, 1, 0), bring(block, 0, -1)
+    x_first, y_first = bring(block, -1, 0), bring(block, 0, -1)
     best_shape, places_shape = shape((8, CAPL), f32), shape((16, META), i32)
     own_best, own_columns, own_places = call(
         own_kernel, (best_shape, shape((CAP, META), f32), places_shape), block
     )
     own, own_best = lax.optimization_barrier((block, own_best))
-    x_second, y_second = bring(own, -1, 0), bring(own, 0, 1)
-    x_far, y_far = bring(x_first, 1, 0), bring(y_first, 0, -1)
+    x_second, y_second = bring(own, 1, 0), bring(own, 0, 1)
+    x_far, y_far = bring(x_first, -1, 0), bring(y_first, 0, -1)
     near_blocks = (block, x_first, x_second, y_first, y_second)
     near, columns, near_places = call(
         near_kernel,

time: 74.6 us -> 74.2 us (level)
  waiting for transfers between devices: 23.4 us -> 22.2 us
  starting transfers between devices: 39 us -> 39.9 us
    ppermute x6, starting transfers between devices: 9.6 us -> 12.6 us  [body(): bring = lambda v, dx, dy: lax.ppermute(v, PLANE, plane_shift(dx, dy))]
    all_to_all x1, starting transfers between devices: 11.7 us -> 9.64 us  [body(): lax.all_to_all(message, RETURN, split_axis=0, concat_axis=0, tiled=True)]
    ppermute x6, waiting for transfers between devices: 7.15 us -> 5.87 us  [body(): bring = lambda v, dx, dy: lax.ppermute(v, PLANE, plane_shift(dx, dy))]
where the time goes in v5:
time: 74.2 us; the launch traced here: 74.1 us
  starting transfers between devices  39.9 us (54%)
  waiting for transfers between devices  22.2 us (30%)
  Pallas kernels  9.25 us (12%)
  between operations  1.42 us (2%)
  other arithmetic  0.75 us (1%)
    ppermute x7, starting transfers between devices, body(): send = lambda v, steps: lax.ppermute(v, COLUMN, column_shift(steps))  16.5 us
    ppermute x6, starting transfers between devices, body(): bring = lambda v, dx, dy: lax.ppermute(v, PLANE, plane_shift(dx, dy))  12.6 us
    all_to_all x1, starting transfers between devices, body(): lax.all_to_all(message, RETURN, split_axis=0, concat_axis=0, tiled=True)  9.64 us
    pallas_call x10, Pallas kernels, call(): pl.pallas_call(kernel, out_shape=out, in_specs=[space(i, smem) for i in r...  9.25 us
    all_to_all x1, waiting for transfers between devices, body(): lax.all_to_all(message, RETURN, split_axis=0, concat_axis=0, tiled=True)  9.17 us
    ppermute x7, waiting for transfers between devices, body(): send = lambda v, steps: lax.ppermute(v, COLUMN, column_shift(steps))  6.21 us
    ppermute x6, waiting for transfers between devices, body(): bring = lambda v, dx, dy: lax.ppermute(v, PLANE, plane_shift(dx, dy))  5.87 us
  transfers between devices with their start and end apart: 15, of which 9 were waited for; matrix products, arithmetic and copies ran while one was open for 0% of the time, Pallas kernels for 6%

profile of v5, /device:TPU:1, one launch (start us, length us, event | category | flops | bytes accessed | tf_op | source)
XLA Modules:
  0.0 74.1 jit_solution(3922965029488302584)
XLA Ops:
  0.0 0.0 copy-start
  0.0 0.7 %multiply_add_fusion = s32[256]{0:T(256)S(1)} fusion(s32[256]{0:T(256)} %param.9, s32[256]{0:T(256)} %param.10), kind=kLoop, calls=%fused_computation.24 | loop fusion | flops 512 | bytes 3072 | tf_op jit(solution)/shard_map/add | solution.py:381
  0.8 0.2 shard_map.48
  1.6 0.0 copy-done
  1.7 0.5 shard_map.49
  2.2 6.9 %collective-permute-start.2 = (bf16[608,128]{1,0:T(8,128)(2,1)S(1)}, bf16[608,128]{1,0:T(8,128)(2,1)S(1)}, u32[]{:S(2)}, u32[]{:S(2)}) collective-permute-start(bf16[608,128]{1,0:T(8,128)(2,1)S(1)} %get-tuple-element.85), channel_id=1, source_target_pairs={{0,8},{1,25},{4,12},{5,29},{8,16},{9,1},{12,20},{13,5},{16,24},{17... | collective-permute-start | bytes 466952 | tf_op jit(solution)/shard_map/ppermute | solution.py:393
  9.1 0.7 collective-permute-start.1
  9.8 0.5 collective-permute-start.3
  10.4 2.7 %collective-permute-start.5 = (bf16[304,128]{1,0:T(8,128)(2,1)S(1)}, bf16[304,128]{1,0:T(8,128)(2,1)S(1)}, u32[]{:S(2)}, u32[]{:S(2)}) collective-permute-start(bf16[304,128]{1,0:T(8,128)(2,1)S(1)} %get-tuple-element.87), channel_id=1, source_target_pairs={{0,20},{1,13},{4,24},{5,17},{8,28},{9,21},{12,0},{13,25},{16,4},{1... | collective-permute-start | bytes 233480 | tf_op jit(solution)/shard_map/ppermute | solution.py:393
  13.1 2.4 %collective-permute-start.6 = (bf16[304,128]{1,0:T(8,128)(2,1)S(1)}, bf16[304,128]{1,0:T(8,128)(2,1)S(1)}, u32[]{:S(2)}, u32[]{:S(2)}) collective-permute-start(bf16[304,128]{1,0:T(8,128)(2,1)S(1)} %get-tuple-element.88), channel_id=1, source_target_pairs={{0,24},{1,9},{4,28},{5,13},{8,0},{9,17},{12,4},{13,21},{16,8},{17,... | collective-permute-start | bytes 233480 | tf_op jit(solution)/shard_map/ppermute | solution.py:393
  15.5 0.0 collective-permute-done.2.refs_2_
  15.5 0.0 collective-permute-start.7
  15.5 0.1 collective-permute-done.1.refs_1_
  15.6 3.1 %collective-permute-start.4 = (bf16[304,128]{1,0:T(8,128)(2,1)S(1)}, bf16[304,128]{1,0:T(8,128)(2,1)S(1)}, u32[]{:S(2)}, u32[]{:S(2)}) collective-permute-start(bf16[304,128]{1,0:T(8,128)(2,1)S(1)} %slice.65), channel_id=1, source_target_pairs={{0,8},{1,25},{4,12},{5,29},{8,16},{9,1},{12,20},{13,5},{16,24},{17... | collective-permute-start | bytes 233480 | tf_op jit(solution)/shard_map/ppermute | solution.py:393
  18.7 0.0 collective-permute-done.3.refs_3_
  18.7 1.3 %collective-permute-done.5.refs_5_ = bf16[304,128]{1,0:T(8,128)(2,1)S(1)} collective-permute-done((bf16[304,128]{1,0:T(8,128)(2,1)S(1)}, bf16[304,128]{1,0:T(8,128)(2,1)S(1)}, u32[]{:S(2)}, u32[]{:S(2)}) %collective-permute-start.5) | collective-permute-done | bytes 77856 | tf_op jit(solution)/shard_map/ppermute | solution.py:393
  20.0 1.7 %collective-permute-done.6.refs_6_ = bf16[304,128]{1,0:T(8,128)(2,1)S(1)} collective-permute-done((bf16[304,128]{1,0:T(8,128)(2,1)S(1)}, bf16[304,128]{1,0:T(8,128)(2,1)S(1)}, u32[]{:S(2)}, u32[]{:S(2)}) %collective-permute-start.6) | collective-permute-done | bytes 77856 | tf_op jit(solution)/shard_map/ppermute | solution.py:393
  21.7 3.1 %collective-permute-done.7.refs_7_ = bf16[304,128]{1,0:T(8,128)(2,1)S(1)} collective-permute-done((bf16[304,128]{1,0:T(8,128)(2,1)S(1)}, bf16[304,128]{1,0:T(8,128)(2,1)S(1)}, u32[]{:S(2)}, u32[]{:S(2)}) %collective-permute-start.7) | collective-permute-done | bytes 77856 | tf_op jit(solution)/shard_map/ppermute | solution.py:393
  24.9 0.0 collective-permute-done.4.refs_4_
  24.9 0.1 shard_map.50.own_ref
  25.0 1.2 %collective-permute-start.8 = (bf16[416,768]{1,0:T(8,128)(2,1)S(1)}, bf16[416,768]{1,0:T(8,128)(2,1)S(1)}, u32[]{:S(2)}, u32[]{:S(2)}) collective-permute-start(bf16[416,768]{1,0:T(8,128)(2,1)S(1)} %shard_map.50.own_ref), channel_id=1, source_target_pairs={{0,1},{1,0},{2,3},{3,2},{4,5},{5,4},{6,7},{7,6},{8,9},{9,8},{10,11... | collective-permute-start | bytes 1916936 | tf_op jit(solution)/shard_map/ppermute | solution.py:410
  26.2 0.8 %shard_map.51 = (bf16[304,768]{1,0:T(8,128)(2,1)S(1)}, s32[8,384]{1,0:T(8,128)S(1)}, f32[8,384]{1,0:T(8,128)S(1)}, f32[8,128]{1,0:T(8,128)S(1)}) custom-call(bf16[416,768]{1,0:T(8,128)(2,1)S(1)} %shard_map.50.own_ref), custom_call_target="tpu_custom_call" | custom-call | flops 141950976 | bytes 933888 | tf_op jit(solution)/shard_map/pallas_call | solution.py:60
  27.0 0.9 %collective-permute-done.8.other_ref = bf16[416,768]{1,0:T(8,128)(2,1)S(1)} collective-permute-done((bf16[416,768]{1,0:T(8,128)(2,1)S(1)}, bf16[416,768]{1,0:T(8,128)(2,1)S(1)}, u32[]{:S(2)}, u32[]{:S(2)}) %collective-permute-start.8) | collective-permute-done | bytes 639008 | tf_op jit(solution)/shard_map/ppermute | solution.py:410
  27.9 0.8 %shard_map.52.own = bf16[304,768]{1,0:T(8,128)(2,1)S(1)} custom-call(bf16[416,768]{1,0:T(8,128)(2,1)S(1)} %collective-permute-done.8.other_ref, bf16[304,768]{1,0:T(8,128)(2,1)S(1)} %get-tuple-element.90.rows_ref, s32[8,384]{1,0:T(8,128)S(1)} %get-tuple-element.91.pos_ref, f32[8,384]{1,0:T(8,128)S(1)} %get-tuple-element.92.ranks_ref, ...), custom_call_target="tpu_custom_call" | custom-call | flops 141950976 | bytes 933888 | tf_op jit(solution)/shard_map/pallas_call | solution.py:60
  28.7 2.6 %collective-permute-start.9 = (bf16[304,768]{1,0:T(8,128)(2,1)S(1)}, bf16[304,768]{1,0:T(8,128)(2,1)S(1)}, u32[]{:S(2)}, u32[]{:S(2)}) collective-permute-start(bf16[304,768]{1,0:T(8,128)(2,1)S(1)} %shard_map.52.own), channel_id=1, source_target_pairs={{34,0},{98,64},{162,128},{226,192},{0,32},{64,96},{128,160},{192,2... | collective-permute-start | bytes 1400840 | tf_op jit(solution)/shard_map/ppermute | solution.py:422
  31.3 2.7 %collective-permute-start.11 = (bf16[304,768]{1,0:T(8,128)(2,1)S(1)}, bf16[304,768]{1,0:T(8,128)(2,1)S(1)}, u32[]{:S(2)}, u32[]{:S(2)}) collective-permute-start(bf16[304,768]{1,0:T(8,128)(2,1)S(1)} %shard_map.52.own), channel_id=1, source_target_pairs={{192,0},{0,64},{64,128},{128,192},{224,32},{32,96},{96,160},{160,2... | collective-permute-start | bytes 1400840 | tf_op jit(solution)/shard_map/ppermute | solution.py:422
  34.0 0.6 shard_map.53
  34.6 0.1 collective-permute-start.10
  34.7 0.1 collective-permute-start.12
  34.8 3.4 %collective-permute-done.9.x_first = bf16[304,768]{1,0:T(8,128)(2,1)S(1)} collective-permute-done((bf16[304,768]{1,0:T(8,128)(2,1)S(1)}, bf16[304,768]{1,0:T(8,128)(2,1)S(1)}, u32[]{:S(2)}, u32[]{:S(2)}) %collective-permute-start.9) | collective-permute-done | bytes 466976 | tf_op jit(solution)/shard_map/ppermute | solution.py:422
  38.2 3.4 %collective-permute-start.13 = (bf16[304,768]{1,0:T(8,128)(2,1)S(1)}, bf16[304,768]{1,0:T(8,128)(2,1)S(1)}, u32[]{:S(2)}, u32[]{:S(2)}) collective-permute-start(bf16[304,768]{1,0:T(8,128)(2,1)S(1)} %collective-permute-done.9.x_first), channel_id=1, source_target_pairs={{34,0},{98,64},{162,128},{226,192},{0,32},{64,96},{128,160},{192,2... | collective-permute-start | bytes 1400840 | tf_op jit(solution)/shard_map/ppermute | solution.py:422
  41.6 0.4 collective-permute-done.11.y_first
  42.0 3.7 %collective-permute-start.14 = (bf16[304,768]{1,0:T(8,128)(2,1)S(1)}, bf16[304,768]{1,0:T(8,128)(2,1)S(1)}, u32[]{:S(2)}, u32[]{:S(2)}) collective-permute-start(bf16[304,768]{1,0:T(8,128)(2,1)S(1)} %collective-permute-done.11.y_first), channel_id=1, source_target_pairs={{192,0},{0,64},{64,128},{128,192},{224,32},{32,96},{96,160},{160,2... | collective-permute-start | bytes 1400840 | tf_op jit(solution)/shard_map/ppermute | solution.py:422
  45.7 0.0 collective-permute-done.10.x_second
  45.7 0.0 collective-permute-done.12.y_second
  45.7 2.5 %shard_map.54 = (f32[8,384]{1,0:T(8,128)S(1)}, f32[2,304,128]{2,1,0:T(8,128)S(1)}, s32[32,128]{1,0:T(8,128)S(1)}) custom-call(bf16[304,768]{1,0:T(8,128)(2,1)S(1)} %shard_map.52.own, bf16[304,768]{1,0:T(8,128)(2,1)S(1)} %collective-permute-done.9.x_first, bf16[304,768]{1,0:T(8,128)(2,1)S(1)} %collective-permute-done.10.x_second, ...), custom_call_target="tpu_custom_call" | custom-call | flops 1135607808 | bytes 933888 | tf_op jit(solution)/shard_map/pallas_call | solution.py:60
  48.2 0.0 collective-permute-done.13.x_far
  48.2 0.9 %shard_map.55 = (f32[8,384]{1,0:T(8,128)S(1)}, s32[16,128]{1,0:T(8,128)S(1)}) custom-call(bf16[304,768]{1,0:T(8,128)(2,1)S(1)} %shard_map.52.own, bf16[304,768]{1,0:T(8,128)(2,1)S(1)} %collective-permute-done.11.y_first, bf16[304,768]{1,0:T(8,128)(2,1)S(1)} %collective-permute-done.12.y_second, bf16[304,768]{1,0:T(8,128)(2,1)S(1)} %collective-permute-done.13.x_far, ...), custom_call_target="tpu_custom_call" | custom-call | flops 425852928 | bytes 933888 | tf_op jit(solution)/shard_map/pallas_call | solution.py:60
  49.2 2.0 %collective-permute-done.14.y_far = bf16[304,768]{1,0:T(8,128)(2,1)S(1)} collective-permute-done((bf16[304,768]{1,0:T(8,128)(2,1)S(1)}, bf16[304,768]{1,0:T(8,128)(2,1)S(1)}, u32[]{:S(2)}, u32[]{:S(2)}) %collective-permute-start.14) | collective-permute-done | bytes 466976 | tf_op jit(solution)/shard_map/ppermute | solution.py:422
  51.2 2.1 %shard_map.56 = f32[64,1,128]{2,1,0:T(1,128)} custom-call(bf16[304,768]{1,0:T(8,128)(2,1)S(1)} %shard_map.52.own, bf16[304,768]{1,0:T(8,128)(2,1)S(1)} %collective-permute-done.9.x_first, bf16[304,768]{1,0:T(8,128)(2,1)S(1)} %collective-permute-done.10.x_second, bf16[304,768]{1,0:T(8,128)(2,1)S(1)} %collective-permute-done.11.y_first, ...), custom_call_target="tpu_custom_call" | custom-call | flops 567803904 | bytes 933888 | tf_op jit(solution)/shard_map/pallas_call | solution.py:60
  53.4 9.6 %all-to-all-start.1 = ((f32[64,1,128]{2,1,0:T(1,128)}), f32[64,1,128]{2,1,0:T(1,128)S(1)}, u32[]{:S(2)}, u32[]{:S(2)}) async-start(f32[64,1,128]{2,1,0:T(1,128)} %shard_map.56), calls=%async_computation.1 | async-start | bytes 65536 | tf_op jit(solution)/shard_map/all_to_all | solution.py:464
  63.0 9.2 %all-to-all-done.1.ans_ref = f32[64,1,128]{2,1,0:T(1,128)S(1)} async-done(((f32[64,1,128]{2,1,0:T(1,128)}), f32[64,1,128]{2,1,0:T(1,128)S(1)}, u32[]{:S(2)}, u32[]{:S(2)}) %all-to-all-start.1) | async-done | bytes 32800 | tf_op jit(solution)/shard_map/all_to_all | solution.py:464
  72.2 0.7 shard_map.57
  73.5 0.0 copy-start.1
  73.5 0.6 copy-done.1
  (2 shorter events, 0.0 us)
Async XLA Ops:
  0.0 1.6 %copy-start = (bf16[256,768]{1,0:T(8,128)(2,1)S(1)}, bf16[256,768]{1,0:T(8,128)(2,1)}, u32[]{:S(2)}) copy-start(bf16[256,768]{1,0:T(8,128)(2,1)} %emb_ref.1) | copy-start | bytes 1179652
  2.2 13.3 %collective-permute-start.2 = (bf16[608,128]{1,0:T(8,128)(2,1)S(1)}, bf16[608,128]{1,0:T(8,128)(2,1)S(1)}, u32[]{:S(2)}, u32[]{:S(2)}) collective-permute-start(bf16[608,128]{1,0:T(8,128)(2,1)S(1)} %get-tuple-element.85), channel_id=1, source_target_pairs={{0,8},{1,25},{4,12},{5,29},{8,16},{9,1},{12,20},{13,5},{16,24},{17... | collective-permute-start | bytes 466952 | tf_op jit(solution)/shard_map/ppermute | solution.py:393
  9.1 6.5 %collective-permute-start.1 = (bf16[304,128]{1,0:T(8,128)(2,1)S(1)}, bf16[304,128]{1,0:T(8,128)(2,1)S(1)}, u32[]{:S(2)}, u32[]{:S(2)}) collective-permute-start(bf16[304,128]{1,0:T(8,128)(2,1)S(1)} %get-tuple-element.84), channel_id=1, source_target_pairs={{0,4},{1,29},{4,8},{5,1},{8,12},{9,5},{12,16},{13,9},{16,20},{17,1... | collective-permute-start | bytes 233480 | tf_op jit(solution)/shard_map/ppermute | solution.py:393
  9.8 8.9 %collective-permute-start.3 = (bf16[304,128]{1,0:T(8,128)(2,1)S(1)}, bf16[304,128]{1,0:T(8,128)(2,1)S(1)}, u32[]{:S(2)}, u32[]{:S(2)}) collective-permute-start(bf16[304,128]{1,0:T(8,128)(2,1)S(1)} %get-tuple-element.86), channel_id=1, source_target_pairs={{0,12},{1,21},{4,16},{5,25},{8,20},{9,29},{12,24},{13,1},{16,28},{... | collective-permute-start | bytes 233480 | tf_op jit(solution)/shard_map/ppermute | solution.py:393
  10.4 9.6 %collective-permute-start.5 = (bf16[304,128]{1,0:T(8,128)(2,1)S(1)}, bf16[304,128]{1,0:T(8,128)(2,1)S(1)}, u32[]{:S(2)}, u32[]{:S(2)}) collective-permute-start(bf16[304,128]{1,0:T(8,128)(2,1)S(1)} %get-tuple-element.87), channel_id=1, source_target_pairs={{0,20},{1,13},{4,24},{5,17},{8,28},{9,21},{12,0},{13,25},{16,4},{1... | collective-permute-start | bytes 233480 | tf_op jit(solution)/shard_map/ppermute | solution.py:393
  13.1 8.6 %collective-permute-start.6 = (bf16[304,128]{1,0:T(8,128)(2,1)S(1)}, bf16[304,128]{1,0:T(8,128)(2,1)S(1)}, u32[]{:S(2)}, u32[]{:S(2)}) collective-permute-start(bf16[304,128]{1,0:T(8,128)(2,1)S(1)} %get-tuple-element.88), channel_id=1, source_target_pairs={{0,24},{1,9},{4,28},{5,13},{8,0},{9,17},{12,4},{13,21},{16,8},{17,... | collective-permute-start | bytes 233480 | tf_op jit(solution)/shard_map/ppermute | solution.py:393
  15.5 9.4 %collective-permute-start.7 = (bf16[304,128]{1,0:T(8,128)(2,1)S(1)}, bf16[304,128]{1,0:T(8,128)(2,1)S(1)}, u32[]{:S(2)}, u32[]{:S(2)}) collective-permute-start(bf16[304,128]{1,0:T(8,128)(2,1)S(1)} %get-tuple-element.89), channel_id=1, source_target_pairs={{0,28},{1,5},{4,0},{5,9},{8,4},{9,13},{12,8},{13,17},{16,12},{17,2... | collective-permute-start | bytes 233480 | tf_op jit(solution)/shard_map/ppermute | solution.py:393
  15.6 9.3 %collective-permute-start.4 = (bf16[304,128]{1,0:T(8,128)(2,1)S(1)}, bf16[304,128]{1,0:T(8,128)(2,1)S(1)}, u32[]{:S(2)}, u32[]{:S(2)}) collective-permute-start(bf16[304,128]{1,0:T(8,128)(2,1)S(1)} %slice.65), channel_id=1, source_target_pairs={{0,8},{1,25},{4,12},{5,29},{8,16},{9,1},{12,20},{13,5},{16,24},{17... | collective-permute-start | bytes 233480 | tf_op jit(solution)/shard_map/ppermute | solution.py:393
  25.0 2.9 %collective-permute-start.8 = (bf16[416,768]{1,0:T(8,128)(2,1)S(1)}, bf16[416,768]{1,0:T(8,128)(2,1)S(1)}, u32[]{:S(2)}, u32[]{:S(2)}) collective-permute-start(bf16[416,768]{1,0:T(8,128)(2,1)S(1)} %shard_map.50.own_ref), channel_id=1, source_target_pairs={{0,1},{1,0},{2,3},{3,2},{4,5},{5,4},{6,7},{7,6},{8,9},{9,8},{10,11... | collective-permute-start | bytes 1916936 | tf_op jit(solution)/shard_map/ppermute | solution.py:410
  28.7 9.5 %collective-permute-start.9 = (bf16[304,768]{1,0:T(8,128)(2,1)S(1)}, bf16[304,768]{1,0:T(8,128)(2,1)S(1)}, u32[]{:S(2)}, u32[]{:S(2)}) collective-permute-start(bf16[304,768]{1,0:T(8,128)(2,1)S(1)} %shard_map.52.own), channel_id=1, source_target_pairs={{34,0},{98,64},{162,128},{226,192},{0,32},{64,96},{128,160},{192,2... | collective-permute-start | bytes 1400840 | tf_op jit(solution)/shard_map/ppermute | solution.py:422
  31.3 10.7 %collective-permute-start.11 = (bf16[304,768]{1,0:T(8,128)(2,1)S(1)}, bf16[304,768]{1,0:T(8,128)(2,1)S(1)}, u32[]{:S(2)}, u32[]{:S(2)}) collective-permute-start(bf16[304,768]{1,0:T(8,128)(2,1)S(1)} %shard_map.52.own), channel_id=1, source_target_pairs={{192,0},{0,64},{64,128},{128,192},{224,32},{32,96},{96,160},{160,2... | collective-permute-start | bytes 1400840 | tf_op jit(solution)/shard_map/ppermute | solution.py:422
  34.6 11.1 %collective-permute-start.10 = (bf16[304,768]{1,0:T(8,128)(2,1)S(1)}, bf16[304,768]{1,0:T(8,128)(2,1)S(1)}, u32[]{:S(2)}, u32[]{:S(2)}) collective-permute-start(bf16[304,768]{1,0:T(8,128)(2,1)S(1)} %shard_map.52.own), channel_id=1, source_target_pairs={{32,0},{96,64},{160,128},{224,192},{2,32},{66,96},{130,160},{194,2... | collective-permute-start | bytes 1400840 | tf_op jit(solution)/shard_map/ppermute | solution.py:422
  34.7 11.0 %collective-permute-start.12 = (bf16[304,768]{1,0:T(8,128)(2,1)S(1)}, bf16[304,768]{1,0:T(8,128)(2,1)S(1)}, u32[]{:S(2)}, u32[]{:S(2)}) collective-permute-start(bf16[304,768]{1,0:T(8,128)(2,1)S(1)} %shard_map.52.own), channel_id=1, source_target_pairs={{64,0},{128,64},{192,128},{0,192},{96,32},{160,96},{224,160},{32,2... | collective-permute-start | bytes 1400840 | tf_op jit(solution)/shard_map/ppermute | solution.py:422
  38.2 10.0 %collective-permute-start.13 = (bf16[304,768]{1,0:T(8,128)(2,1)S(1)}, bf16[304,768]{1,0:T(8,128)(2,1)S(1)}, u32[]{:S(2)}, u32[]{:S(2)}) collective-permute-start(bf16[304,768]{1,0:T(8,128)(2,1)S(1)} %collective-permute-done.9.x_first), channel_id=1, source_target_pairs={{34,0},{98,64},{162,128},{226,192},{0,32},{64,96},{128,160},{192,2... | collective-permute-start | bytes 1400840 | tf_op jit(solution)/shard_map/ppermute | solution.py:422
  42.0 9.2 %collective-permute-start.14 = (bf16[304,768]{1,0:T(8,128)(2,1)S(1)}, bf16[304,768]{1,0:T(8,128)(2,1)S(1)}, u32[]{:S(2)}, u32[]{:S(2)}) collective-permute-start(bf16[304,768]{1,0:T(8,128)(2,1)S(1)} %collective-permute-done.11.y_first), channel_id=1, source_target_pairs={{192,0},{0,64},{64,128},{128,192},{224,32},{32,96},{96,160},{160,2... | collective-permute-start | bytes 1400840 | tf_op jit(solution)/shard_map/ppermute | solution.py:422
  53.4 18.8 %all-to-all-start.1 = ((f32[64,1,128]{2,1,0:T(1,128)}), f32[64,1,128]{2,1,0:T(1,128)S(1)}, u32[]{:S(2)}, u32[]{:S(2)}) async-start(f32[64,1,128]{2,1,0:T(1,128)} %shard_map.56), calls=%async_computation.1 | async-start | bytes 65536 | tf_op jit(solution)/shard_map/all_to_all | solution.py:464
  73.5 0.6 copy-start.1

commit v6 on v5

--- a/solution.py
+++ b/solution.py
@@ -392,9 +392,10 @@
     )
     send = lambda v, steps: lax.ppermute(v, COLUMN, column_shift(steps))
     two_four = send(pieces[2], 2)
-    three, five, six = send(pieces[3], 3), send(pieces[4], 5), send(pieces[5], 6)
+    three, five = send(pieces[3], 3), send(pieces[4], 5)
+    two_four, *near_pieces = lax.optimization_barrier((two_four, pieces[5], pieces[1], pieces[6]))
     four = send(two_four[PIECE:], 2)
-    one, seven = send(pieces[1], 1), send(pieces[6], 7)
+    six, one, seven = send(near_pieces[0], 6), send(near_pieces[1], 1), send(near_pieces[2], 7)
     arrived = call(
         collect_kernel,
         shape((ROUTED + MARKS, WIDTH), bf16),

time: 74.2 us -> 77.6 us (1.046)
  waiting for transfers between devices: 22.2 us -> 25.7 us
    ppermute x7, waiting for transfers between devices: 6.21 us -> 9.71 us  [body(): send = lambda v, steps: lax.ppermute(v, COLUMN, column_shift(steps))]
    all_to_all x1, starting transfers between devices: 9.64 us -> 11.1 us  [body(): lax.all_to_all(message, RETURN, split_axis=0, concat_axis=0, tiled=True)]
    ppermute x1, starting transfers between devices: 1.23 us -> 0.43 us  [body(): other = lax.ppermute(arrived, 'core', [(0, 1), (1, 0)])]
where the time goes in v6:
time: 77.6 us; the launch traced here: 77.5 us
  starting transfers between devices  39.8 us (51%)
  waiting for transfers between devices  25.7 us (33%)
  Pallas kernels  9.25 us (12%)
  between operations  1.42 us (2%)
    ppermute x7, starting transfers between devices, body(): send = lambda v, steps: lax.ppermute(v, COLUMN, column_shift(steps))  15.7 us
    ppermute x6, starting transfers between devices, body(): bring = lambda v, dx, dy: lax.ppermute(v, PLANE, plane_shift(dx, dy))  12.6 us
    all_to_all x1, starting transfers between devices, body(): lax.all_to_all(message, RETURN, split_axis=0, concat_axis=0, tiled=True)  11.1 us
    ppermute x7, waiting for transfers between devices, body(): send = lambda v, steps: lax.ppermute(v, COLUMN, column_shift(steps))  9.71 us
    pallas_call x10, Pallas kernels, call(): pl.pallas_call(kernel, out_shape=out, in_specs=[space(i, smem) for i in r...  9.25 us
    all_to_all x1, waiting for transfers between devices, body(): lax.all_to_all(message, RETURN, split_axis=0, concat_axis=0, tiled=True)  9.17 us
    ppermute x6, waiting for transfers between devices, body(): bring = lambda v, dx, dy: lax.ppermute(v, PLANE, plane_shift(dx, dy))  5.89 us
  transfers between devices with their start and end apart: 15, of which 9 were waited for; matrix products, arithmetic and copies ran while one was open for 0% of the time, Pallas kernels for 6%

profile of v6, /device:TPU:1, one launch (start us, length us, event | category | flops | bytes accessed | tf_op | source)
XLA Modules:
  0.0 77.5 jit_solution(18422214171167214335)
XLA Ops:
  0.0 0.0 copy-start
  0.0 0.7 multiply_add_fusion
  0.8 0.2 shard_map.48
  1.6 0.0 copy-done
  1.7 0.5 shard_map.49
  2.2 6.9 %collective-permute-start.1 = (bf16[608,128]{1,0:T(8,128)(2,1)S(1)}, bf16[608,128]{1,0:T(8,128)(2,1)S(1)}, u32[]{:S(2)}, u32[]{:S(2)}) collective-permute-start(bf16[608,128]{1,0:T(8,128)(2,1)S(1)} %get-tuple-element.88), channel_id=1, source_target_pairs={{0,8},{1,25},{4,12},{5,29},{8,16},{9,1},{12,20},{13,5},{16,24},{17... | collective-permute-start | bytes 466952 | tf_op jit(solution)/shard_map/ppermute | solution.py:393
  9.1 0.7 collective-permute-start.3
  9.8 2.5 %collective-permute-start.5 = (bf16[304,128]{1,0:T(8,128)(2,1)S(1)}, bf16[304,128]{1,0:T(8,128)(2,1)S(1)}, u32[]{:S(2)}, u32[]{:S(2)}) collective-permute-start(bf16[304,128]{1,0:T(8,128)(2,1)S(1)} %get-tuple-element.95), channel_id=1, source_target_pairs={{0,20},{1,13},{4,24},{5,17},{8,28},{9,21},{12,0},{13,25},{16,4},{1... | collective-permute-start | bytes 233480 | tf_op jit(solution)/shard_map/ppermute | solution.py:393
  12.4 4.0 %collective-permute-done.1.refs_2_ = bf16[608,128]{1,0:T(8,128)(2,1)S(1)} collective-permute-done((bf16[608,128]{1,0:T(8,128)(2,1)S(1)}, bf16[608,128]{1,0:T(8,128)(2,1)S(1)}, u32[]{:S(2)}, u32[]{:S(2)}) %collective-permute-start.1) | collective-permute-done | bytes 155680 | tf_op jit(solution)/shard_map/ppermute | solution.py:393
  16.3 4.1 %collective-permute-start.4 = (bf16[304,128]{1,0:T(8,128)(2,1)S(1)}, bf16[304,128]{1,0:T(8,128)(2,1)S(1)}, u32[]{:S(2)}, u32[]{:S(2)}) collective-permute-start(bf16[304,128]{1,0:T(8,128)(2,1)S(1)} %slice.49), channel_id=1, source_target_pairs={{0,8},{1,25},{4,12},{5,29},{8,16},{9,1},{12,20},{13,5},{16,24},{17... | collective-permute-start | bytes 233480 | tf_op jit(solution)/shard_map/ppermute | solution.py:393
  20.4 0.0 collective-permute-start.2
  20.4 0.0 collective-permute-start.6
  20.4 0.0 collective-permute-done.3.refs_3_
  20.4 1.5 %collective-permute-start.7 = (bf16[304,128]{1,0:T(8,128)(2,1)S(1)}, bf16[304,128]{1,0:T(8,128)(2,1)S(1)}, u32[]{:S(2)}, u32[]{:S(2)}) collective-permute-start(bf16[304,128]{1,0:T(8,128)(2,1)S(1)} %get-tuple-element.97), channel_id=1, source_target_pairs={{0,28},{1,5},{4,0},{5,9},{8,4},{9,13},{12,8},{13,17},{16,12},{17,2... | collective-permute-start | bytes 233480 | tf_op jit(solution)/shard_map/ppermute | solution.py:393
  21.9 0.0 collective-permute-done.5.refs_5_
  21.9 0.0 collective-permute-done.4.refs_4_
  21.9 2.1 %collective-permute-done.2.refs_1_ = bf16[304,128]{1,0:T(8,128)(2,1)S(1)} collective-permute-done((bf16[304,128]{1,0:T(8,128)(2,1)S(1)}, bf16[304,128]{1,0:T(8,128)(2,1)S(1)}, u32[]{:S(2)}, u32[]{:S(2)}) %collective-permute-start.2) | collective-permute-done | bytes 77856 | tf_op jit(solution)/shard_map/ppermute | solution.py:393
  24.0 2.1 %collective-permute-done.6.refs_6_ = bf16[304,128]{1,0:T(8,128)(2,1)S(1)} collective-permute-done((bf16[304,128]{1,0:T(8,128)(2,1)S(1)}, bf16[304,128]{1,0:T(8,128)(2,1)S(1)}, u32[]{:S(2)}, u32[]{:S(2)}) %collective-permute-start.6) | collective-permute-done | bytes 77856 | tf_op jit(solution)/shard_map/ppermute | solution.py:393
  26.1 1.6 %collective-permute-done.7.refs_7_ = bf16[304,128]{1,0:T(8,128)(2,1)S(1)} collective-permute-done((bf16[304,128]{1,0:T(8,128)(2,1)S(1)}, bf16[304,128]{1,0:T(8,128)(2,1)S(1)}, u32[]{:S(2)}, u32[]{:S(2)}) %collective-permute-start.7) | collective-permute-done | bytes 77856 | tf_op jit(solution)/shard_map/ppermute | solution.py:393
  27.6 0.1 shard_map.50.own_ref
  27.8 0.4 collective-permute-start.8
  28.2 0.8 %shard_map.51 = (bf16[304,768]{1,0:T(8,128)(2,1)S(1)}, s32[8,384]{1,0:T(8,128)S(1)}, f32[8,384]{1,0:T(8,128)S(1)}, f32[8,128]{1,0:T(8,128)S(1)}) custom-call(bf16[416,768]{1,0:T(8,128)(2,1)S(1)} %shard_map.50.own_ref), custom_call_target="tpu_custom_call" | custom-call | flops 141950976 | bytes 933888 | tf_op jit(solution)/shard_map/pallas_call | solution.py:60
  29.0 0.9 %collective-permute-done.8.other_ref = bf16[416,768]{1,0:T(8,128)(2,1)S(1)} collective-permute-done((bf16[416,768]{1,0:T(8,128)(2,1)S(1)}, bf16[416,768]{1,0:T(8,128)(2,1)S(1)}, u32[]{:S(2)}, u32[]{:S(2)}) %collective-permute-start.8) | collective-permute-done | bytes 639008 | tf_op jit(solution)/shard_map/ppermute | solution.py:411
  29.9 0.8 %shard_map.52.own = bf16[304,768]{1,0:T(8,128)(2,1)S(1)} custom-call(bf16[416,768]{1,0:T(8,128)(2,1)S(1)} %collective-permute-done.8.other_ref, bf16[304,768]{1,0:T(8,128)(2,1)S(1)} %get-tuple-element.98.rows_ref, s32[8,384]{1,0:T(8,128)S(1)} %get-tuple-element.99.pos_ref, f32[8,384]{1,0:T(8,128)S(1)} %get-tuple-element.100.ranks_ref, ...), custom_call_target="tpu_custom_call" | custom-call | flops 141950976 | bytes 933888 | tf_op jit(solution)/shard_map/pallas_call | solution.py:60
  30.7 2.6 %collective-permute-start.9 = (bf16[304,768]{1,0:T(8,128)(2,1)S(1)}, bf16[304,768]{1,0:T(8,128)(2,1)S(1)}, u32[]{:S(2)}, u32[]{:S(2)}) collective-permute-start(bf16[304,768]{1,0:T(8,128)(2,1)S(1)} %shard_map.52.own), channel_id=1, source_target_pairs={{34,0},{98,64},{162,128},{226,192},{0,32},{64,96},{128,160},{192,2... | collective-permute-start | bytes 1400840 | tf_op jit(solution)/shard_map/ppermute | solution.py:423
  33.3 2.7 %collective-permute-start.11 = (bf16[304,768]{1,0:T(8,128)(2,1)S(1)}, bf16[304,768]{1,0:T(8,128)(2,1)S(1)}, u32[]{:S(2)}, u32[]{:S(2)}) collective-permute-start(bf16[304,768]{1,0:T(8,128)(2,1)S(1)} %shard_map.52.own), channel_id=1, source_target_pairs={{192,0},{0,64},{64,128},{128,192},{224,32},{32,96},{96,160},{160,2... | collective-permute-start | bytes 1400840 | tf_op jit(solution)/shard_map/ppermute | solution.py:423
  36.0 0.6 shard_map.53
  36.6 0.1 collective-permute-start.10
  36.7 0.1 collective-permute-start.12
  36.8 3.5 %collective-permute-done.9.x_first = bf16[304,768]{1,0:T(8,128)(2,1)S(1)} collective-permute-done((bf16[304,768]{1,0:T(8,128)(2,1)S(1)}, bf16[304,768]{1,0:T(8,128)(2,1)S(1)}, u32[]{:S(2)}, u32[]{:S(2)}) %collective-permute-start.9) | collective-permute-done | bytes 466976 | tf_op jit(solution)/shard_map/ppermute | solution.py:423
  40.2 3.4 %collective-permute-start.13 = (bf16[304,768]{1,0:T(8,128)(2,1)S(1)}, bf16[304,768]{1,0:T(8,128)(2,1)S(1)}, u32[]{:S(2)}, u32[]{:S(2)}) collective-permute-start(bf16[304,768]{1,0:T(8,128)(2,1)S(1)} %collective-permute-done.9.x_first), channel_id=1, source_target_pairs={{34,0},{98,64},{162,128},{226,192},{0,32},{64,96},{128,160},{192,2... | collective-permute-start | bytes 1400840 | tf_op jit(solution)/shard_map/ppermute | solution.py:423
  43.6 0.4 collective-permute-done.11.y_first
  44.0 3.7 %collective-permute-start.14 = (bf16[304,768]{1,0:T(8,128)(2,1)S(1)}, bf16[304,768]{1,0:T(8,128)(2,1)S(1)}, u32[]{:S(2)}, u32[]{:S(2)}) collective-permute-start(bf16[304,768]{1,0:T(8,128)(2,1)S(1)} %collective-permute-done.11.y_first), channel_id=1, source_target_pairs={{192,0},{0,64},{64,128},{128,192},{224,32},{32,96},{96,160},{160,2... | collective-permute-start | bytes 1400840 | tf_op jit(solution)/shard_map/ppermute | solution.py:423
  47.7 0.0 collective-permute-done.10.x_second
  47.7 0.0 collective-permute-done.12.y_second
  47.7 2.5 %shard_map.54 = (f32[8,384]{1,0:T(8,128)S(1)}, f32[2,304,128]{2,1,0:T(8,128)S(1)}, s32[32,128]{1,0:T(8,128)S(1)}) custom-call(bf16[304,768]{1,0:T(8,128)(2,1)S(1)} %shard_map.52.own, bf16[304,768]{1,0:T(8,128)(2,1)S(1)} %collective-permute-done.9.x_first, bf16[304,768]{1,0:T(8,128)(2,1)S(1)} %collective-permute-done.10.x_second, ...), custom_call_target="tpu_custom_call" | custom-call | flops 1135607808 | bytes 933888 | tf_op jit(solution)/shard_map/pallas_call | solution.py:60
  50.2 0.0 collective-permute-done.13.x_far
  50.2 0.9 %shard_map.55 = (f32[8,384]{1,0:T(8,128)S(1)}, s32[16,128]{1,0:T(8,128)S(1)}) custom-call(bf16[304,768]{1,0:T(8,128)(2,1)S(1)} %shard_map.52.own, bf16[304,768]{1,0:T(8,128)(2,1)S(1)} %collective-permute-done.11.y_first, bf16[304,768]{1,0:T(8,128)(2,1)S(1)} %collective-permute-done.12.y_second, bf16[304,768]{1,0:T(8,128)(2,1)S(1)} %collective-permute-done.13.x_far, ...), custom_call_target="tpu_custom_call" | custom-call | flops 425852928 | bytes 933888 | tf_op jit(solution)/shard_map/pallas_call | solution.py:60
  51.2 2.0 %collective-permute-done.14.y_far = bf16[304,768]{1,0:T(8,128)(2,1)S(1)} collective-permute-done((bf16[304,768]{1,0:T(8,128)(2,1)S(1)}, bf16[304,768]{1,0:T(8,128)(2,1)S(1)}, u32[]{:S(2)}, u32[]{:S(2)}) %collective-permute-start.14) | collective-permute-done | bytes 466976 | tf_op jit(solution)/shard_map/ppermute | solution.py:423
  53.2 2.1 %shard_map.56 = f32[64,1,128]{2,1,0:T(1,128)} custom-call(bf16[304,768]{1,0:T(8,128)(2,1)S(1)} %shard_map.52.own, bf16[304,768]{1,0:T(8,128)(2,1)S(1)} %collective-permute-done.9.x_first, bf16[304,768]{1,0:T(8,128)(2,1)S(1)} %collective-permute-done.10.x_second, bf16[304,768]{1,0:T(8,128)(2,1)S(1)} %collective-permute-done.11.y_first, ...), custom_call_target="tpu_custom_call" | custom-call | flops 567803904 | bytes 933888 | tf_op jit(solution)/shard_map/pallas_call | solution.py:60
  55.4 11.1 %all-to-all-start.1 = ((f32[64,1,128]{2,1,0:T(1,128)}), f32[64,1,128]{2,1,0:T(1,128)S(1)}, u32[]{:S(2)}, u32[]{:S(2)}) async-start(f32[64,1,128]{2,1,0:T(1,128)} %shard_map.56), calls=%async_computation.1 | async-start | bytes 65536 | tf_op jit(solution)/shard_map/all_to_all | solution.py:465
  66.4 9.2 %all-to-all-done.1.ans_ref = f32[64,1,128]{2,1,0:T(1,128)S(1)} async-done(((f32[64,1,128]{2,1,0:T(1,128)}), f32[64,1,128]{2,1,0:T(1,128)S(1)}, u32[]{:S(2)}, u32[]{:S(2)}) %all-to-all-start.1) | async-done | bytes 32800 | tf_op jit(solution)/shard_map/all_to_all | solution.py:465
  75.6 0.7 shard_map.57
  76.9 0.0 copy-start.1
  76.9 0.6 copy-done.1
  (2 shorter events, 0.0 us)
Async XLA Ops:
  0.0 1.6 %copy-start = (bf16[256,768]{1,0:T(8,128)(2,1)S(1)}, bf16[256,768]{1,0:T(8,128)(2,1)}, u32[]{:S(2)}) copy-start(bf16[256,768]{1,0:T(8,128)(2,1)} %emb_ref.1) | copy-start | bytes 1179652
  2.2 14.2 %collective-permute-start.1 = (bf16[608,128]{1,0:T(8,128)(2,1)S(1)}, bf16[608,128]{1,0:T(8,128)(2,1)S(1)}, u32[]{:S(2)}, u32[]{:S(2)}) collective-permute-start(bf16[608,128]{1,0:T(8,128)(2,1)S(1)} %get-tuple-element.88), channel_id=1, source_target_pairs={{0,8},{1,25},{4,12},{5,29},{8,16},{9,1},{12,20},{13,5},{16,24},{17... | collective-permute-start | bytes 466952 | tf_op jit(solution)/shard_map/ppermute | solution.py:393
  9.1 11.3 %collective-permute-start.3 = (bf16[304,128]{1,0:T(8,128)(2,1)S(1)}, bf16[304,128]{1,0:T(8,128)(2,1)S(1)}, u32[]{:S(2)}, u32[]{:S(2)}) collective-permute-start(bf16[304,128]{1,0:T(8,128)(2,1)S(1)} %get-tuple-element.94), channel_id=1, source_target_pairs={{0,12},{1,21},{4,16},{5,25},{8,20},{9,29},{12,24},{13,1},{16,28},{... | collective-permute-start | bytes 233480 | tf_op jit(solution)/shard_map/ppermute | solution.py:393
  9.8 12.1 %collective-permute-start.5 = (bf16[304,128]{1,0:T(8,128)(2,1)S(1)}, bf16[304,128]{1,0:T(8,128)(2,1)S(1)}, u32[]{:S(2)}, u32[]{:S(2)}) collective-permute-start(bf16[304,128]{1,0:T(8,128)(2,1)S(1)} %get-tuple-element.95), channel_id=1, source_target_pairs={{0,20},{1,13},{4,24},{5,17},{8,28},{9,21},{12,0},{13,25},{16,4},{1... | collective-permute-start | bytes 233480 | tf_op jit(solution)/shard_map/ppermute | solution.py:393
  16.3 5.6 %collective-permute-start.4 = (bf16[304,128]{1,0:T(8,128)(2,1)S(1)}, bf16[304,128]{1,0:T(8,128)(2,1)S(1)}, u32[]{:S(2)}, u32[]{:S(2)}) collective-permute-start(bf16[304,128]{1,0:T(8,128)(2,1)S(1)} %slice.49), channel_id=1, source_target_pairs={{0,8},{1,25},{4,12},{5,29},{8,16},{9,1},{12,20},{13,5},{16,24},{17... | collective-permute-start | bytes 233480 | tf_op jit(solution)/shard_map/ppermute | solution.py:393
  20.4 3.5 %collective-permute-start.2 = (bf16[304,128]{1,0:T(8,128)(2,1)S(1)}, bf16[304,128]{1,0:T(8,128)(2,1)S(1)}, u32[]{:S(2)}, u32[]{:S(2)}) collective-permute-start(bf16[304,128]{1,0:T(8,128)(2,1)S(1)} %get-tuple-element.92), channel_id=1, source_target_pairs={{0,4},{1,29},{4,8},{5,1},{8,12},{9,5},{12,16},{13,9},{16,20},{17,1... | collective-permute-start | bytes 233480 | tf_op jit(solution)/shard_map/ppermute | solution.py:393
  20.4 5.6 %collective-permute-start.6 = (bf16[304,128]{1,0:T(8,128)(2,1)S(1)}, bf16[304,128]{1,0:T(8,128)(2,1)S(1)}, u32[]{:S(2)}, u32[]{:S(2)}) collective-permute-start(bf16[304,128]{1,0:T(8,128)(2,1)S(1)} %get-tuple-element.96), channel_id=1, source_target_pairs={{0,24},{1,9},{4,28},{5,13},{8,0},{9,17},{12,4},{13,21},{16,8},{17,... | collective-permute-start | bytes 233480 | tf_op jit(solution)/shard_map/ppermute | solution.py:393
  20.4 7.2 %collective-permute-start.7 = (bf16[304,128]{1,0:T(8,128)(2,1)S(1)}, bf16[304,128]{1,0:T(8,128)(2,1)S(1)}, u32[]{:S(2)}, u32[]{:S(2)}) collective-permute-start(bf16[304,128]{1,0:T(8,128)(2,1)S(1)} %get-tuple-element.97), channel_id=1, source_target_pairs={{0,28},{1,5},{4,0},{5,9},{8,4},{9,13},{12,8},{13,17},{16,12},{17,2... | collective-permute-start | bytes 233480 | tf_op jit(solution)/shard_map/ppermute | solution.py:393
  27.8 2.2 %collective-permute-start.8 = (bf16[416,768]{1,0:T(8,128)(2,1)S(1)}, bf16[416,768]{1,0:T(8,128)(2,1)S(1)}, u32[]{:S(2)}, u32[]{:S(2)}) collective-permute-start(bf16[416,768]{1,0:T(8,128)(2,1)S(1)} %shard_map.50.own_ref), channel_id=1, source_target_pairs={{0,1},{1,0},{2,3},{3,2},{4,5},{5,4},{6,7},{7,6},{8,9},{9,8},{10,11... | collective-permute-start | bytes 1916936 | tf_op jit(solution)/shard_map/ppermute | solution.py:411
  30.7 9.5 %collective-permute-start.9 = (bf16[304,768]{1,0:T(8,128)(2,1)S(1)}, bf16[304,768]{1,0:T(8,128)(2,1)S(1)}, u32[]{:S(2)}, u32[]{:S(2)}) collective-permute-start(bf16[304,768]{1,0:T(8,128)(2,1)S(1)} %shard_map.52.own), channel_id=1, source_target_pairs={{34,0},{98,64},{162,128},{226,192},{0,32},{64,96},{128,160},{192,2... | collective-permute-start | bytes 1400840 | tf_op jit(solution)/shard_map/ppermute | solution.py:423
  33.3 10.7 %collective-permute-start.11 = (bf16[304,768]{1,0:T(8,128)(2,1)S(1)}, bf16[304,768]{1,0:T(8,128)(2,1)S(1)}, u32[]{:S(2)}, u32[]{:S(2)}) collective-permute-start(bf16[304,768]{1,0:T(8,128)(2,1)S(1)} %shard_map.52.own), channel_id=1, source_target_pairs={{192,0},{0,64},{64,128},{128,192},{224,32},{32,96},{96,160},{160,2... | collective-permute-start | bytes 1400840 | tf_op jit(solution)/shard_map/ppermute | solution.py:423
  36.6 11.1 %collective-permute-start.10 = (bf16[304,768]{1,0:T(8,128)(2,1)S(1)}, bf16[304,768]{1,0:T(8,128)(2,1)S(1)}, u32[]{:S(2)}, u32[]{:S(2)}) collective-permute-start(bf16[304,768]{1,0:T(8,128)(2,1)S(1)} %shard_map.52.own), channel_id=1, source_target_pairs={{32,0},{96,64},{160,128},{224,192},{2,32},{66,96},{130,160},{194,2... | collective-permute-start | bytes 1400840 | tf_op jit(solution)/shard_map/ppermute | solution.py:423
  36.7 11.1 %collective-permute-start.12 = (bf16[304,768]{1,0:T(8,128)(2,1)S(1)}, bf16[304,768]{1,0:T(8,128)(2,1)S(1)}, u32[]{:S(2)}, u32[]{:S(2)}) collective-permute-start(bf16[304,768]{1,0:T(8,128)(2,1)S(1)} %shard_map.52.own), channel_id=1, source_target_pairs={{64,0},{128,64},{192,128},{0,192},{96,32},{160,96},{224,160},{32,2... | collective-permute-start | bytes 1400840 | tf_op jit(solution)/shard_map/ppermute | solution.py:423
  40.2 10.0 %collective-permute-start.13 = (bf16[304,768]{1,0:T(8,128)(2,1)S(1)}, bf16[304,768]{1,0:T(8,128)(2,1)S(1)}, u32[]{:S(2)}, u32[]{:S(2)}) collective-permute-start(bf16[304,768]{1,0:T(8,128)(2,1)S(1)} %collective-permute-done.9.x_first), channel_id=1, source_target_pairs={{34,0},{98,64},{162,128},{226,192},{0,32},{64,96},{128,160},{192,2... | collective-permute-start | bytes 1400840 | tf_op jit(solution)/shard_map/ppermute | solution.py:423
  44.0 9.2 %collective-permute-start.14 = (bf16[304,768]{1,0:T(8,128)(2,1)S(1)}, bf16[304,768]{1,0:T(8,128)(2,1)S(1)}, u32[]{:S(2)}, u32[]{:S(2)}) collective-permute-start(bf16[304,768]{1,0:T(8,128)(2,1)S(1)} %collective-permute-done.11.y_first), channel_id=1, source_target_pairs={{192,0},{0,64},{64,128},{128,192},{224,32},{32,96},{96,160},{160,2... | collective-permute-start | bytes 1400840 | tf_op jit(solution)/shard_map/ppermute | solution.py:423
  55.4 20.2 %all-to-all-start.1 = ((f32[64,1,128]{2,1,0:T(1,128)}), f32[64,1,128]{2,1,0:T(1,128)S(1)}, u32[]{:S(2)}, u32[]{:S(2)}) async-start(f32[64,1,128]{2,1,0:T(1,128)} %shard_map.56), calls=%async_computation.1 | async-start | bytes 65536 | tf_op jit(solution)/shard_map/all_to_all | solution.py:465
  76.9 0.6 copy-start.1

commit v7 on v5

--- a/solution.py
+++ b/solution.py
@@ -75,15 +75,17 @@
 
 
 def slot_kernel(both_ref, where_ref, marks_ref, slot_ref):
-    ids, ranks = both_ref[...] & 15, both_ref[...] >> 4
+    both = both_ref[...]
+    live = both >= 0
+    ids, ranks = both & 15, both >> 4
     target = ids & (GROUPS - 1)
-    chosen = jnp.where(iota((GROUPS, ROWS), 0) == target, 1.0, 0.0)
+    chosen = jnp.where((iota((GROUPS, ROWS), 0) == target) & live, 1.0, 0.0)
     upper = jnp.where(iota((ROWS, ROWS), 0) < iota((ROWS, ROWS), 1), 1.0, 0.0).astype(jnp.bfloat16)
     before = dot(chosen.astype(jnp.bfloat16), upper, ((1,), (0,)))
     within = jnp.sum(before * chosen, axis=0, keepdims=True).astype(jnp.int32)
     steps = signed(lax.axis_index("core"), target - lax.axis_index("z")) & (GROUPS - 1)
     at = jnp.where(steps == 3, 4, jnp.where(steps == 4, 3, steps))
-    slot = jnp.where(within < SLOTS, at * SLOTS + within, -1)
+    slot = jnp.where(live, at * SLOTS + within, -1)
     where_ref[...] = jnp.where(iota((ROUTED, ROWS), 0) == slot, 1.0, 0.0).astype(jnp.bfloat16)
     high = ranks >> 8
     row = iota((16, ROWS), 0)
@@ -91,23 +93,17 @@
         row == 0, ids + 1, jnp.where(row == 1, high, jnp.where(row == 2, ranks - (high << 8), 0))
     )
     marks_ref[...] = meta.astype(jnp.float32).astype(jnp.bfloat16)
-    slot_ref[0:1, :] = target
+    slot_ref[0:1, :] = jnp.where(live, target, -1)
     slot_ref[1:2, :] = within
     slot_ref[2:8, :] = jnp.zeros((6, ROWS), jnp.int32)
 
 
-def piece_kernel(count_ref, emb_ref, where_ref, marks_ref, slot_ref, *refs):
-    *out_refs, live_slot_ref = refs
-    live = iota((1, ROWS), 1) < count_ref[0]
-    live_slot_ref[0:1, :] = jnp.where(live, slot_ref[0:1, :], -1)
-    live_slot_ref[1:8, :] = slot_ref[1:8, :]
+def piece_kernel(emb_ref, where_ref, marks_ref, *out_refs):
     x = emb_ref[...].astype(jnp.float32)
-    unit = x * lax.rsqrt(jnp.sum(x * x, axis=1, keepdims=True) + norm_eps)
-    unit = jnp.where(iota((ROWS, 1), 0) < count_ref[0], unit, 0.0).astype(jnp.bfloat16)
+    unit = (x * lax.rsqrt(jnp.sum(x * x, axis=1, keepdims=True) + norm_eps)).astype(jnp.bfloat16)
     where_to = where_ref[...]
     rows = dot(where_to, unit, ((1,), (0,))).astype(jnp.bfloat16)
-    meta = jnp.where(live, marks_ref[...].astype(jnp.float32), 0.0).astype(jnp.bfloat16)
-    marks = dot(meta, where_to, ((1,), (1,)))
+    marks = dot(marks_ref[...], where_to, ((1,), (1,)))
     at = 0
     for ref in out_refs:
         for first in range(0, ref.shape[0], PIECE):
@@ -374,21 +370,19 @@
 def body(embeddings, cluster_id, order_rank, row_count):
     f32, bf16, i32 = jnp.float32, jnp.bfloat16, jnp.int32
     shape = jax.ShapeDtypeStruct
-    slots_shape = shape((8, ROWS), i32)
+    live = jnp.arange(ROWS, dtype=i32) < row_count[0]
+    both = jnp.where(live, cluster_id + 16 * order_rank, -1)
     where_to, marks, slots = call(
         slot_kernel,
-        (shape((ROUTED, ROWS), bf16), shape((16, ROWS), bf16), slots_shape),
-        (cluster_id + 16 * order_rank).reshape(1, ROWS),
-    )
-    *pieces, slots = call(
+        (shape((ROUTED, ROWS), bf16), shape((16, ROWS), bf16), shape((8, ROWS), i32)),
+        both.reshape(1, ROWS),
+    )
+    pieces = call(
         piece_kernel,
-        tuple(shape((n * PIECE, META), bf16) for n in PIECES) + (slots_shape,),
-        row_count,
+        tuple(shape((n * PIECE, META), bf16) for n in PIECES),
         embeddings,
         where_to,
         marks,
-        slots,
-        smem=(0,),
     )
     send = lambda v, steps: lax.ppermute(v, COLUMN, column_shift(steps))
     two_four = send(pieces[2], 2)

time: 74.2 us -> 74.3 us (level)
    add x1 -> x0, other arithmetic: 0.75 us -> none  [body(): cluster_id + 16 * order_rank]
where the time goes in v7:
time: 74.3 us; the launch traced here: 74.1 us
  starting transfers between devices  39.9 us (54%)
  waiting for transfers between devices  22.2 us (30%)
  Pallas kernels  9.26 us (12%)
  between operations  1.48 us (2%)
    ppermute x7, starting transfers between devices, body(): send = lambda v, steps: lax.ppermute(v, COLUMN, column_shift(steps))  16.5 us
    ppermute x6, starting transfers between devices, body(): bring = lambda v, dx, dy: lax.ppermute(v, PLANE, plane_shift(dx, dy))  12.6 us
    all_to_all x1, starting transfers between devices, body(): lax.all_to_all(message, RETURN, split_axis=0, concat_axis=0, tiled=True)  9.63 us
    pallas_call x10, Pallas kernels, call(): pl.pallas_call(kernel, out_shape=out, in_specs=[space(i, smem) for i in r...  9.26 us
    all_to_all x1, waiting for transfers between devices, body(): lax.all_to_all(message, RETURN, split_axis=0, concat_axis=0, tiled=True)  9.17 us
    ppermute x7, waiting for transfers between devices, body(): send = lambda v, steps: lax.ppermute(v, COLUMN, column_shift(steps))  6.21 us
    ppermute x6, waiting for transfers between devices, body(): bring = lambda v, dx, dy: lax.ppermute(v, PLANE, plane_shift(dx, dy))  5.88 us
  transfers between devices with their start and end apart: 15, of which 9 were waited for; matrix products, arithmetic and copies ran while one was open for 0% of the time, Pallas kernels for 6%

profile of v7, /device:TPU:1, one launch (start us, length us, event | category | flops | bytes accessed | tf_op | source)
XLA Modules:
  0.0 74.1 jit_solution(10985739968183083889)
XLA Ops:
  0.0 0.0 copy-start
  0.7 0.7 compare_select_fusion.2
  1.4 0.2 shard_map.48
  1.7 0.0 copy-done
  1.7 0.5 shard_map.49
  2.2 6.9 %collective-permute-start.2 = (bf16[608,128]{1,0:T(8,128)(2,1)S(1)}, bf16[608,128]{1,0:T(8,128)(2,1)S(1)}, u32[]{:S(2)}, u32[]{:S(2)}) collective-permute-start(bf16[608,128]{1,0:T(8,128)(2,1)S(1)} %get-tuple-element.83), channel_id=1, source_target_pairs={{0,8},{1,25},{4,12},{5,29},{8,16},{9,1},{12,20},{13,5},{16,24},{17... | collective-permute-start | bytes 466952 | tf_op jit(solution)/shard_map/ppermute | solution.py:387
  9.1 0.7 collective-permute-start.1
  9.8 0.5 collective-permute-start.3
  10.4 2.7 %collective-permute-start.5 = (bf16[304,128]{1,0:T(8,128)(2,1)S(1)}, bf16[304,128]{1,0:T(8,128)(2,1)S(1)}, u32[]{:S(2)}, u32[]{:S(2)}) collective-permute-start(bf16[304,128]{1,0:T(8,128)(2,1)S(1)} %get-tuple-element.85), channel_id=1, source_target_pairs={{0,20},{1,13},{4,24},{5,17},{8,28},{9,21},{12,0},{13,25},{16,4},{1... | collective-permute-start | bytes 233480 | tf_op jit(solution)/shard_map/ppermute | solution.py:387
  13.1 2.4 %collective-permute-start.6 = (bf16[304,128]{1,0:T(8,128)(2,1)S(1)}, bf16[304,128]{1,0:T(8,128)(2,1)S(1)}, u32[]{:S(2)}, u32[]{:S(2)}) collective-permute-start(bf16[304,128]{1,0:T(8,128)(2,1)S(1)} %get-tuple-element.86), channel_id=1, source_target_pairs={{0,24},{1,9},{4,28},{5,13},{8,0},{9,17},{12,4},{13,21},{16,8},{17,... | collective-permute-start | bytes 233480 | tf_op jit(solution)/shard_map/ppermute | solution.py:387
  15.5 0.0 collective-permute-done.2.refs_2_
  15.5 0.0 collective-permute-start.7
  15.5 0.1 collective-permute-done.1.refs_1_
  15.6 3.1 %collective-permute-start.4 = (bf16[304,128]{1,0:T(8,128)(2,1)S(1)}, bf16[304,128]{1,0:T(8,128)(2,1)S(1)}, u32[]{:S(2)}, u32[]{:S(2)}) collective-permute-start(bf16[304,128]{1,0:T(8,128)(2,1)S(1)} %slice.65), channel_id=1, source_target_pairs={{0,8},{1,25},{4,12},{5,29},{8,16},{9,1},{12,20},{13,5},{16,24},{17... | collective-permute-start | bytes 233480 | tf_op jit(solution)/shard_map/ppermute | solution.py:387
  18.7 0.0 collective-permute-done.3.refs_3_
  18.7 1.3 %collective-permute-done.5.refs_5_ = bf16[304,128]{1,0:T(8,128)(2,1)S(1)} collective-permute-done((bf16[304,128]{1,0:T(8,128)(2,1)S(1)}, bf16[304,128]{1,0:T(8,128)(2,1)S(1)}, u32[]{:S(2)}, u32[]{:S(2)}) %collective-permute-start.5) | collective-permute-done | bytes 77856 | tf_op jit(solution)/shard_map/ppermute | solution.py:387
  20.0 1.8 %collective-permute-done.6.refs_6_ = bf16[304,128]{1,0:T(8,128)(2,1)S(1)} collective-permute-done((bf16[304,128]{1,0:T(8,128)(2,1)S(1)}, bf16[304,128]{1,0:T(8,128)(2,1)S(1)}, u32[]{:S(2)}, u32[]{:S(2)}) %collective-permute-start.6) | collective-permute-done | bytes 77856 | tf_op jit(solution)/shard_map/ppermute | solution.py:387
  21.7 3.1 %collective-permute-done.7.refs_7_ = bf16[304,128]{1,0:T(8,128)(2,1)S(1)} collective-permute-done((bf16[304,128]{1,0:T(8,128)(2,1)S(1)}, bf16[304,128]{1,0:T(8,128)(2,1)S(1)}, u32[]{:S(2)}, u32[]{:S(2)}) %collective-permute-start.7) | collective-permute-done | bytes 77856 | tf_op jit(solution)/shard_map/ppermute | solution.py:387
  24.9 0.0 collective-permute-done.4.refs_4_
  24.9 0.1 shard_map.50.own_ref
  25.0 1.2 %collective-permute-start.8 = (bf16[416,768]{1,0:T(8,128)(2,1)S(1)}, bf16[416,768]{1,0:T(8,128)(2,1)S(1)}, u32[]{:S(2)}, u32[]{:S(2)}) collective-permute-start(bf16[416,768]{1,0:T(8,128)(2,1)S(1)} %shard_map.50.own_ref), channel_id=1, source_target_pairs={{0,1},{1,0},{2,3},{3,2},{4,5},{5,4},{6,7},{7,6},{8,9},{9,8},{10,11... | collective-permute-start | bytes 1916936 | tf_op jit(solution)/shard_map/ppermute | solution.py:404
  26.2 0.8 %shard_map.51 = (bf16[304,768]{1,0:T(8,128)(2,1)S(1)}, s32[8,384]{1,0:T(8,128)S(1)}, f32[8,384]{1,0:T(8,128)S(1)}, f32[8,128]{1,0:T(8,128)S(1)}) custom-call(bf16[416,768]{1,0:T(8,128)(2,1)S(1)} %shard_map.50.own_ref), custom_call_target="tpu_custom_call" | custom-call | flops 141950976 | bytes 933888 | tf_op jit(solution)/shard_map/pallas_call | solution.py:60
  27.0 0.9 %collective-permute-done.8.other_ref = bf16[416,768]{1,0:T(8,128)(2,1)S(1)} collective-permute-done((bf16[416,768]{1,0:T(8,128)(2,1)S(1)}, bf16[416,768]{1,0:T(8,128)(2,1)S(1)}, u32[]{:S(2)}, u32[]{:S(2)}) %collective-permute-start.8) | collective-permute-done | bytes 639008 | tf_op jit(solution)/shard_map/ppermute | solution.py:404
  27.9 0.8 %shard_map.52.own = bf16[304,768]{1,0:T(8,128)(2,1)S(1)} custom-call(bf16[416,768]{1,0:T(8,128)(2,1)S(1)} %collective-permute-done.8.other_ref, bf16[304,768]{1,0:T(8,128)(2,1)S(1)} %get-tuple-element.88.rows_ref, s32[8,384]{1,0:T(8,128)S(1)} %get-tuple-element.89.pos_ref, f32[8,384]{1,0:T(8,128)S(1)} %get-tuple-element.90.ranks_ref, ...), custom_call_target="tpu_custom_call" | custom-call | flops 141950976 | bytes 933888 | tf_op jit(solution)/shard_map/pallas_call | solution.py:60
  28.7 2.6 %collective-permute-start.9 = (bf16[304,768]{1,0:T(8,128)(2,1)S(1)}, bf16[304,768]{1,0:T(8,128)(2,1)S(1)}, u32[]{:S(2)}, u32[]{:S(2)}) collective-permute-start(bf16[304,768]{1,0:T(8,128)(2,1)S(1)} %shard_map.52.own), channel_id=1, source_target_pairs={{34,0},{98,64},{162,128},{226,192},{0,32},{64,96},{128,160},{192,2... | collective-permute-start | bytes 1400840 | tf_op jit(solution)/shard_map/ppermute | solution.py:416
  31.3 2.7 %collective-permute-start.11 = (bf16[304,768]{1,0:T(8,128)(2,1)S(1)}, bf16[304,768]{1,0:T(8,128)(2,1)S(1)}, u32[]{:S(2)}, u32[]{:S(2)}) collective-permute-start(bf16[304,768]{1,0:T(8,128)(2,1)S(1)} %shard_map.52.own), channel_id=1, source_target_pairs={{192,0},{0,64},{64,128},{128,192},{224,32},{32,96},{96,160},{160,2... | collective-permute-start | bytes 1400840 | tf_op jit(solution)/shard_map/ppermute | solution.py:416
  34.0 0.6 shard_map.53
  34.6 0.1 collective-permute-start.10
  34.7 0.1 collective-permute-start.12
  34.8 3.5 %collective-permute-done.9.x_first = bf16[304,768]{1,0:T(8,128)(2,1)S(1)} collective-permute-done((bf16[304,768]{1,0:T(8,128)(2,1)S(1)}, bf16[304,768]{1,0:T(8,128)(2,1)S(1)}, u32[]{:S(2)}, u32[]{:S(2)}) %collective-permute-start.9) | collective-permute-done | bytes 466976 | tf_op jit(solution)/shard_map/ppermute | solution.py:416
  38.2 3.4 %collective-permute-start.13 = (bf16[304,768]{1,0:T(8,128)(2,1)S(1)}, bf16[304,768]{1,0:T(8,128)(2,1)S(1)}, u32[]{:S(2)}, u32[]{:S(2)}) collective-permute-start(bf16[304,768]{1,0:T(8,128)(2,1)S(1)} %collective-permute-done.9.x_first), channel_id=1, source_target_pairs={{34,0},{98,64},{162,128},{226,192},{0,32},{64,96},{128,160},{192,2... | collective-permute-start | bytes 1400840 | tf_op jit(solution)/shard_map/ppermute | solution.py:416
  41.6 0.4 collective-permute-done.11.y_first
  42.0 3.7 %collective-permute-start.14 = (bf16[304,768]{1,0:T(8,128)(2,1)S(1)}, bf16[304,768]{1,0:T(8,128)(2,1)S(1)}, u32[]{:S(2)}, u32[]{:S(2)}) collective-permute-start(bf16[304,768]{1,0:T(8,128)(2,1)S(1)} %collective-permute-done.11.y_first), channel_id=1, source_target_pairs={{192,0},{0,64},{64,128},{128,192},{224,32},{32,96},{96,160},{160,2... | collective-permute-start | bytes 1400840 | tf_op jit(solution)/shard_map/ppermute | solution.py:416
  45.7 0.0 collective-permute-done.10.x_second
  45.7 0.0 collective-permute-done.12.y_second
  45.7 2.5 %shard_map.54 = (f32[8,384]{1,0:T(8,128)S(1)}, f32[2,304,128]{2,1,0:T(8,128)S(1)}, s32[32,128]{1,0:T(8,128)S(1)}) custom-call(bf16[304,768]{1,0:T(8,128)(2,1)S(1)} %shard_map.52.own, bf16[304,768]{1,0:T(8,128)(2,1)S(1)} %collective-permute-done.9.x_first, bf16[304,768]{1,0:T(8,128)(2,1)S(1)} %collective-permute-done.10.x_second, ...), custom_call_target="tpu_custom_call" | custom-call | flops 1135607808 | bytes 933888 | tf_op jit(solution)/shard_map/pallas_call | solution.py:60
  48.3 0.0 collective-permute-done.13.x_far
  48.3 0.9 %shard_map.55 = (f32[8,384]{1,0:T(8,128)S(1)}, s32[16,128]{1,0:T(8,128)S(1)}) custom-call(bf16[304,768]{1,0:T(8,128)(2,1)S(1)} %shard_map.52.own, bf16[304,768]{1,0:T(8,128)(2,1)S(1)} %collective-permute-done.11.y_first, bf16[304,768]{1,0:T(8,128)(2,1)S(1)} %collective-permute-done.12.y_second, bf16[304,768]{1,0:T(8,128)(2,1)S(1)} %collective-permute-done.13.x_far, ...), custom_call_target="tpu_custom_call" | custom-call | flops 425852928 | bytes 933888 | tf_op jit(solution)/shard_map/pallas_call | solution.py:60
  49.2 2.0 %collective-permute-done.14.y_far = bf16[304,768]{1,0:T(8,128)(2,1)S(1)} collective-permute-done((bf16[304,768]{1,0:T(8,128)(2,1)S(1)}, bf16[304,768]{1,0:T(8,128)(2,1)S(1)}, u32[]{:S(2)}, u32[]{:S(2)}) %collective-permute-start.14) | collective-permute-done | bytes 466976 | tf_op jit(solution)/shard_map/ppermute | solution.py:416
  51.2 2.1 %shard_map.56 = f32[64,1,128]{2,1,0:T(1,128)} custom-call(bf16[304,768]{1,0:T(8,128)(2,1)S(1)} %shard_map.52.own, bf16[304,768]{1,0:T(8,128)(2,1)S(1)} %collective-permute-done.9.x_first, bf16[304,768]{1,0:T(8,128)(2,1)S(1)} %collective-permute-done.10.x_second, bf16[304,768]{1,0:T(8,128)(2,1)S(1)} %collective-permute-done.11.y_first, ...), custom_call_target="tpu_custom_call" | custom-call | flops 567803904 | bytes 933888 | tf_op jit(solution)/shard_map/pallas_call | solution.py:60
  53.4 9.6 %all-to-all-start.1 = ((f32[64,1,128]{2,1,0:T(1,128)}), f32[64,1,128]{2,1,0:T(1,128)S(1)}, u32[]{:S(2)}, u32[]{:S(2)}) async-start(f32[64,1,128]{2,1,0:T(1,128)} %shard_map.56), calls=%async_computation.1 | async-start | bytes 65536 | tf_op jit(solution)/shard_map/all_to_all | solution.py:458
  63.0 9.2 %all-to-all-done.1.ans_ref = f32[64,1,128]{2,1,0:T(1,128)S(1)} async-done(((f32[64,1,128]{2,1,0:T(1,128)}), f32[64,1,128]{2,1,0:T(1,128)S(1)}, u32[]{:S(2)}, u32[]{:S(2)}) %all-to-all-start.1) | async-done | bytes 32800 | tf_op jit(solution)/shard_map/all_to_all | solution.py:458
  72.2 0.7 shard_map.57
  73.5 0.0 copy-start.1
  73.5 0.6 copy-done.1
  (2 shorter events, 0.0 us)
Async XLA Ops:
  0.0 1.7 %copy-start = (bf16[256,768]{1,0:T(8,128)(2,1)S(1)}, bf16[256,768]{1,0:T(8,128)(2,1)}, u32[]{:S(2)}) copy-start(bf16[256,768]{1,0:T(8,128)(2,1)} %emb_ref.1) | copy-start | bytes 1179652
  2.2 13.3 %collective-permute-start.2 = (bf16[608,128]{1,0:T(8,128)(2,1)S(1)}, bf16[608,128]{1,0:T(8,128)(2,1)S(1)}, u32[]{:S(2)}, u32[]{:S(2)}) collective-permute-start(bf16[608,128]{1,0:T(8,128)(2,1)S(1)} %get-tuple-element.83), channel_id=1, source_target_pairs={{0,8},{1,25},{4,12},{5,29},{8,16},{9,1},{12,20},{13,5},{16,24},{17... | collective-permute-start | bytes 466952 | tf_op jit(solution)/shard_map/ppermute | solution.py:387
  9.1 6.5 %collective-permute-start.1 = (bf16[304,128]{1,0:T(8,128)(2,1)S(1)}, bf16[304,128]{1,0:T(8,128)(2,1)S(1)}, u32[]{:S(2)}, u32[]{:S(2)}) collective-permute-start(bf16[304,128]{1,0:T(8,128)(2,1)S(1)} %get-tuple-element.82), channel_id=1, source_target_pairs={{0,4},{1,29},{4,8},{5,1},{8,12},{9,5},{12,16},{13,9},{16,20},{17,1... | collective-permute-start | bytes 233480 | tf_op jit(solution)/shard_map/ppermute | solution.py:387
  9.8 8.9 %collective-permute-start.3 = (bf16[304,128]{1,0:T(8,128)(2,1)S(1)}, bf16[304,128]{1,0:T(8,128)(2,1)S(1)}, u32[]{:S(2)}, u32[]{:S(2)}) collective-permute-start(bf16[304,128]{1,0:T(8,128)(2,1)S(1)} %get-tuple-element.84), channel_id=1, source_target_pairs={{0,12},{1,21},{4,16},{5,25},{8,20},{9,29},{12,24},{13,1},{16,28},{... | collective-permute-start | bytes 233480 | tf_op jit(solution)/shard_map/ppermute | solution.py:387
  10.4 9.6 %collective-permute-start.5 = (bf16[304,128]{1,0:T(8,128)(2,1)S(1)}, bf16[304,128]{1,0:T(8,128)(2,1)S(1)}, u32[]{:S(2)}, u32[]{:S(2)}) collective-permute-start(bf16[304,128]{1,0:T(8,128)(2,1)S(1)} %get-tuple-element.85), channel_id=1, source_target_pairs={{0,20},{1,13},{4,24},{5,17},{8,28},{9,21},{12,0},{13,25},{16,4},{1... | collective-permute-start | bytes 233480 | tf_op jit(solution)/shard_map/ppermute | solution.py:387
  13.1 8.6 %collective-permute-start.6 = (bf16[304,128]{1,0:T(8,128)(2,1)S(1)}, bf16[304,128]{1,0:T(8,128)(2,1)S(1)}, u32[]{:S(2)}, u32[]{:S(2)}) collective-permute-start(bf16[304,128]{1,0:T(8,128)(2,1)S(1)} %get-tuple-element.86), channel_id=1, source_target_pairs={{0,24},{1,9},{4,28},{5,13},{8,0},{9,17},{12,4},{13,21},{16,8},{17,... | collective-permute-start | bytes 233480 | tf_op jit(solution)/shard_map/ppermute | solution.py:387
  15.5 9.4 %collective-permute-start.7 = (bf16[304,128]{1,0:T(8,128)(2,1)S(1)}, bf16[304,128]{1,0:T(8,128)(2,1)S(1)}, u32[]{:S(2)}, u32[]{:S(2)}) collective-permute-start(bf16[304,128]{1,0:T(8,128)(2,1)S(1)} %get-tuple-element.87), channel_id=1, source_target_pairs={{0,28},{1,5},{4,0},{5,9},{8,4},{9,13},{12,8},{13,17},{16,12},{17,2... | collective-permute-start | bytes 233480 | tf_op jit(solution)/shard_map/ppermute | solution.py:387
  15.6 9.3 %collective-permute-start.4 = (bf16[304,128]{1,0:T(8,128)(2,1)S(1)}, bf16[304,128]{1,0:T(8,128)(2,1)S(1)}, u32[]{:S(2)}, u32[]{:S(2)}) collective-permute-start(bf16[304,128]{1,0:T(8,128)(2,1)S(1)} %slice.65), channel_id=1, source_target_pairs={{0,8},{1,25},{4,12},{5,29},{8,16},{9,1},{12,20},{13,5},{16,24},{17... | collective-permute-start | bytes 233480 | tf_op jit(solution)/shard_map/ppermute | solution.py:387
  25.0 2.9 %collective-permute-start.8 = (bf16[416,768]{1,0:T(8,128)(2,1)S(1)}, bf16[416,768]{1,0:T(8,128)(2,1)S(1)}, u32[]{:S(2)}, u32[]{:S(2)}) collective-permute-start(bf16[416,768]{1,0:T(8,128)(2,1)S(1)} %shard_map.50.own_ref), channel_id=1, source_target_pairs={{0,1},{1,0},{2,3},{3,2},{4,5},{5,4},{6,7},{7,6},{8,9},{9,8},{10,11... | collective-permute-start | bytes 1916936 | tf_op jit(solution)/shard_map/ppermute | solution.py:404
  28.7 9.5 %collective-permute-start.9 = (bf16[304,768]{1,0:T(8,128)(2,1)S(1)}, bf16[304,768]{1,0:T(8,128)(2,1)S(1)}, u32[]{:S(2)}, u32[]{:S(2)}) collective-permute-start(bf16[304,768]{1,0:T(8,128)(2,1)S(1)} %shard_map.52.own), channel_id=1, source_target_pairs={{34,0},{98,64},{162,128},{226,192},{0,32},{64,96},{128,160},{192,2... | collective-permute-start | bytes 1400840 | tf_op jit(solution)/shard_map/ppermute | solution.py:416
  31.3 10.7 %collective-permute-start.11 = (bf16[304,768]{1,0:T(8,128)(2,1)S(1)}, bf16[304,768]{1,0:T(8,128)(2,1)S(1)}, u32[]{:S(2)}, u32[]{:S(2)}) collective-permute-start(bf16[304,768]{1,0:T(8,128)(2,1)S(1)} %shard_map.52.own), channel_id=1, source_target_pairs={{192,0},{0,64},{64,128},{128,192},{224,32},{32,96},{96,160},{160,2... | collective-permute-start | bytes 1400840 | tf_op jit(solution)/shard_map/ppermute | solution.py:416
  34.6 11.1 %collective-permute-start.10 = (bf16[304,768]{1,0:T(8,128)(2,1)S(1)}, bf16[304,768]{1,0:T(8,128)(2,1)S(1)}, u32[]{:S(2)}, u32[]{:S(2)}) collective-permute-start(bf16[304,768]{1,0:T(8,128)(2,1)S(1)} %shard_map.52.own), channel_id=1, source_target_pairs={{32,0},{96,64},{160,128},{224,192},{2,32},{66,96},{130,160},{194,2... | collective-permute-start | bytes 1400840 | tf_op jit(solution)/shard_map/ppermute | solution.py:416
  34.7 11.0 %collective-permute-start.12 = (bf16[304,768]{1,0:T(8,128)(2,1)S(1)}, bf16[304,768]{1,0:T(8,128)(2,1)S(1)}, u32[]{:S(2)}, u32[]{:S(2)}) collective-permute-start(bf16[304,768]{1,0:T(8,128)(2,1)S(1)} %shard_map.52.own), channel_id=1, source_target_pairs={{64,0},{128,64},{192,128},{0,192},{96,32},{160,96},{224,160},{32,2... | collective-permute-start | bytes 1400840 | tf_op jit(solution)/shard_map/ppermute | solution.py:416
  38.2 10.0 %collective-permute-start.13 = (bf16[304,768]{1,0:T(8,128)(2,1)S(1)}, bf16[304,768]{1,0:T(8,128)(2,1)S(1)}, u32[]{:S(2)}, u32[]{:S(2)}) collective-permute-start(bf16[304,768]{1,0:T(8,128)(2,1)S(1)} %collective-permute-done.9.x_first), channel_id=1, source_target_pairs={{34,0},{98,64},{162,128},{226,192},{0,32},{64,96},{128,160},{192,2... | collective-permute-start | bytes 1400840 | tf_op jit(solution)/shard_map/ppermute | solution.py:416
  42.0 9.2 %collective-permute-start.14 = (bf16[304,768]{1,0:T(8,128)(2,1)S(1)}, bf16[304,768]{1,0:T(8,128)(2,1)S(1)}, u32[]{:S(2)}, u32[]{:S(2)}) collective-permute-start(bf16[304,768]{1,0:T(8,128)(2,1)S(1)} %collective-permute-done.11.y_first), channel_id=1, source_target_pairs={{192,0},{0,64},{64,128},{128,192},{224,32},{32,96},{96,160},{160,2... | collective-permute-start | bytes 1400840 | tf_op jit(solution)/shard_map/ppermute | solution.py:416
  53.4 18.8 %all-to-all-start.1 = ((f32[64,1,128]{2,1,0:T(1,128)}), f32[64,1,128]{2,1,0:T(1,128)S(1)}, u32[]{:S(2)}, u32[]{:S(2)}) async-start(f32[64,1,128]{2,1,0:T(1,128)} %shard_map.56), calls=%async_computation.1 | async-start | bytes 65536 | tf_op jit(solution)/shard_map/all_to_all | solution.py:458
  73.5 0.6 copy-start.1

commit v8 on v5

--- a/solution.py
+++ b/solution.py
@@ -303,8 +303,7 @@
     wanted = block * 16 + (core ^ my_core) * GROUPS + steps
     order = jnp.where(column == wanted, 1.0, 0.0).astype(jnp.bfloat16)
     out = dot(jnp.concatenate([order] * 3, axis=1), jnp.concatenate(split3(found), axis=0), ((1,), (0,)))
-    for i in range(messages):
-        out_ref[i] = out[i : i + 1, :]
+    out_ref[...] = out.reshape(messages, 1, META)
 
 
 def final_kernel(slot_ref, ans_ref, out_ref, flag_ref):

time: 74.2 us -> 74.2 us (level)
  no operation moved by 1% of the time
where the time goes in v8:
time: 74.2 us; the launch traced here: 74.1 us
  starting transfers between devices  39.9 us (54%)
  waiting for transfers between devices  22.2 us (30%)
  Pallas kernels  9.26 us (12%)
  between operations  1.42 us (2%)
  other arithmetic  0.75 us (1%)
    ppermute x7, starting transfers between devices, body(): send = lambda v, steps: lax.ppermute(v, COLUMN, column_shift(steps))  16.5 us
    ppermute x6, starting transfers between devices, body(): bring = lambda v, dx, dy: lax.ppermute(v, PLANE, plane_shift(dx, dy))  12.6 us
    all_to_all x1, starting transfers between devices, body(): lax.all_to_all(message, RETURN, split_axis=0, concat_axis=0, tiled=True)  9.64 us
    pallas_call x10, Pallas kernels, call(): pl.pallas_call(kernel, out_shape=out, in_specs=[space(i, smem) for i in r...  9.26 us
    all_to_all x1, waiting for transfers between devices, body(): lax.all_to_all(message, RETURN, split_axis=0, concat_axis=0, tiled=True)  9.17 us
    ppermute x7, waiting for transfers between devices, body(): send = lambda v, steps: lax.ppermute(v, COLUMN, column_shift(steps))  6.21 us
    ppermute x6, waiting for transfers between devices, body(): bring = lambda v, dx, dy: lax.ppermute(v, PLANE, plane_shift(dx, dy))  5.87 us
  transfers between devices with their start and end apart: 15, of which 9 were waited for; matrix products, arithmetic and copies ran while one was open for 0% of the time, Pallas kernels for 6%

profile of v8, /device:TPU:1, one launch (start us, length us, event | category | flops | bytes accessed | tf_op | source)
XLA Modules:
  0.0 74.1 jit_solution(4986412832321157288)
XLA Ops:
  0.0 0.0 copy-start
  0.0 0.7 %multiply_add_fusion = s32[256]{0:T(256)S(1)} fusion(s32[256]{0:T(256)} %param.9, s32[256]{0:T(256)} %param.10), kind=kLoop, calls=%fused_computation.24 | loop fusion | flops 512 | bytes 3072 | tf_op jit(solution)/shard_map/add | solution.py:380
  0.8 0.2 shard_map.48
  1.6 0.0 copy-done
  1.7 0.5 shard_map.49
  2.2 6.9 %collective-permute-start.2 = (bf16[608,128]{1,0:T(8,128)(2,1)S(1)}, bf16[608,128]{1,0:T(8,128)(2,1)S(1)}, u32[]{:S(2)}, u32[]{:S(2)}) collective-permute-start(bf16[608,128]{1,0:T(8,128)(2,1)S(1)} %get-tuple-element.85), channel_id=1, source_target_pairs={{0,8},{1,25},{4,12},{5,29},{8,16},{9,1},{12,20},{13,5},{16,24},{17... | collective-permute-start | bytes 466952 | tf_op jit(solution)/shard_map/ppermute | solution.py:392
  9.1 0.7 collective-permute-start.1
  9.8 0.5 collective-permute-start.3
  10.4 2.7 %collective-permute-start.5 = (bf16[304,128]{1,0:T(8,128)(2,1)S(1)}, bf16[304,128]{1,0:T(8,128)(2,1)S(1)}, u32[]{:S(2)}, u32[]{:S(2)}) collective-permute-start(bf16[304,128]{1,0:T(8,128)(2,1)S(1)} %get-tuple-element.87), channel_id=1, source_target_pairs={{0,20},{1,13},{4,24},{5,17},{8,28},{9,21},{12,0},{13,25},{16,4},{1... | collective-permute-start | bytes 233480 | tf_op jit(solution)/shard_map/ppermute | solution.py:392
  13.1 2.4 %collective-permute-start.6 = (bf16[304,128]{1,0:T(8,128)(2,1)S(1)}, bf16[304,128]{1,0:T(8,128)(2,1)S(1)}, u32[]{:S(2)}, u32[]{:S(2)}) collective-permute-start(bf16[304,128]{1,0:T(8,128)(2,1)S(1)} %get-tuple-element.88), channel_id=1, source_target_pairs={{0,24},{1,9},{4,28},{5,13},{8,0},{9,17},{12,4},{13,21},{16,8},{17,... | collective-permute-start | bytes 233480 | tf_op jit(solution)/shard_map/ppermute | solution.py:392
  15.5 0.0 collective-permute-done.2.refs_2_
  15.5 0.0 collective-permute-start.7
  15.5 0.1 collective-permute-done.1.refs_1_
  15.6 3.1 %collective-permute-start.4 = (bf16[304,128]{1,0:T(8,128)(2,1)S(1)}, bf16[304,128]{1,0:T(8,128)(2,1)S(1)}, u32[]{:S(2)}, u32[]{:S(2)}) collective-permute-start(bf16[304,128]{1,0:T(8,128)(2,1)S(1)} %slice.65), channel_id=1, source_target_pairs={{0,8},{1,25},{4,12},{5,29},{8,16},{9,1},{12,20},{13,5},{16,24},{17... | collective-permute-start | bytes 233480 | tf_op jit(solution)/shard_map/ppermute | solution.py:392
  18.7 0.0 collective-permute-done.3.refs_3_
  18.7 1.3 %collective-permute-done.5.refs_5_ = bf16[304,128]{1,0:T(8,128)(2,1)S(1)} collective-permute-done((bf16[304,128]{1,0:T(8,128)(2,1)S(1)}, bf16[304,128]{1,0:T(8,128)(2,1)S(1)}, u32[]{:S(2)}, u32[]{:S(2)}) %collective-permute-start.5) | collective-permute-done | bytes 77856 | tf_op jit(solution)/shard_map/ppermute | solution.py:392
  20.0 1.7 %collective-permute-done.6.refs_6_ = bf16[304,128]{1,0:T(8,128)(2,1)S(1)} collective-permute-done((bf16[304,128]{1,0:T(8,128)(2,1)S(1)}, bf16[304,128]{1,0:T(8,128)(2,1)S(1)}, u32[]{:S(2)}, u32[]{:S(2)}) %collective-permute-start.6) | collective-permute-done | bytes 77856 | tf_op jit(solution)/shard_map/ppermute | solution.py:392
  21.7 3.1 %collective-permute-done.7.refs_7_ = bf16[304,128]{1,0:T(8,128)(2,1)S(1)} collective-permute-done((bf16[304,128]{1,0:T(8,128)(2,1)S(1)}, bf16[304,128]{1,0:T(8,128)(2,1)S(1)}, u32[]{:S(2)}, u32[]{:S(2)}) %collective-permute-start.7) | collective-permute-done | bytes 77856 | tf_op jit(solution)/shard_map/ppermute | solution.py:392
  24.9 0.0 collective-permute-done.4.refs_4_
  24.9 0.1 shard_map.50.own_ref
  25.0 1.2 %collective-permute-start.8 = (bf16[416,768]{1,0:T(8,128)(2,1)S(1)}, bf16[416,768]{1,0:T(8,128)(2,1)S(1)}, u32[]{:S(2)}, u32[]{:S(2)}) collective-permute-start(bf16[416,768]{1,0:T(8,128)(2,1)S(1)} %shard_map.50.own_ref), channel_id=1, source_target_pairs={{0,1},{1,0},{2,3},{3,2},{4,5},{5,4},{6,7},{7,6},{8,9},{9,8},{10,11... | collective-permute-start | bytes 1916936 | tf_op jit(solution)/shard_map/ppermute | solution.py:409
  26.2 0.8 %shard_map.51 = (bf16[304,768]{1,0:T(8,128)(2,1)S(1)}, s32[8,384]{1,0:T(8,128)S(1)}, f32[8,384]{1,0:T(8,128)S(1)}, f32[8,128]{1,0:T(8,128)S(1)}) custom-call(bf16[416,768]{1,0:T(8,128)(2,1)S(1)} %shard_map.50.own_ref), custom_call_target="tpu_custom_call" | custom-call | flops 141950976 | bytes 933888 | tf_op jit(solution)/shard_map/pallas_call | solution.py:60
  27.0 0.9 %collective-permute-done.8.other_ref = bf16[416,768]{1,0:T(8,128)(2,1)S(1)} collective-permute-done((bf16[416,768]{1,0:T(8,128)(2,1)S(1)}, bf16[416,768]{1,0:T(8,128)(2,1)S(1)}, u32[]{:S(2)}, u32[]{:S(2)}) %collective-permute-start.8) | collective-permute-done | bytes 639008 | tf_op jit(solution)/shard_map/ppermute | solution.py:409
  27.9 0.8 %shard_map.52.own = bf16[304,768]{1,0:T(8,128)(2,1)S(1)} custom-call(bf16[416,768]{1,0:T(8,128)(2,1)S(1)} %collective-permute-done.8.other_ref, bf16[304,768]{1,0:T(8,128)(2,1)S(1)} %get-tuple-element.90.rows_ref, s32[8,384]{1,0:T(8,128)S(1)} %get-tuple-element.91.pos_ref, f32[8,384]{1,0:T(8,128)S(1)} %get-tuple-element.92.ranks_ref, ...), custom_call_target="tpu_custom_call" | custom-call | flops 141950976 | bytes 933888 | tf_op jit(solution)/shard_map/pallas_call | solution.py:60
  28.7 2.6 %collective-permute-start.9 = (bf16[304,768]{1,0:T(8,128)(2,1)S(1)}, bf16[304,768]{1,0:T(8,128)(2,1)S(1)}, u32[]{:S(2)}, u32[]{:S(2)}) collective-permute-start(bf16[304,768]{1,0:T(8,128)(2,1)S(1)} %shard_map.52.own), channel_id=1, source_target_pairs={{34,0},{98,64},{162,128},{226,192},{0,32},{64,96},{128,160},{192,2... | collective-permute-start | bytes 1400840 | tf_op jit(solution)/shard_map/ppermute | solution.py:421
  31.3 2.7 %collective-permute-start.11 = (bf16[304,768]{1,0:T(8,128)(2,1)S(1)}, bf16[304,768]{1,0:T(8,128)(2,1)S(1)}, u32[]{:S(2)}, u32[]{:S(2)}) collective-permute-start(bf16[304,768]{1,0:T(8,128)(2,1)S(1)} %shard_map.52.own), channel_id=1, source_target_pairs={{192,0},{0,64},{64,128},{128,192},{224,32},{32,96},{96,160},{160,2... | collective-permute-start | bytes 1400840 | tf_op jit(solution)/shard_map/ppermute | solution.py:421
  34.0 0.6 shard_map.53
  34.6 0.1 collective-permute-start.10
  34.7 0.1 collective-permute-start.12
  34.8 3.4 %collective-permute-done.9.x_first = bf16[304,768]{1,0:T(8,128)(2,1)S(1)} collective-permute-done((bf16[304,768]{1,0:T(8,128)(2,1)S(1)}, bf16[304,768]{1,0:T(8,128)(2,1)S(1)}, u32[]{:S(2)}, u32[]{:S(2)}) %collective-permute-start.9) | collective-permute-done | bytes 466976 | tf_op jit(solution)/shard_map/ppermute | solution.py:421
  38.2 3.4 %collective-permute-start.13 = (bf16[304,768]{1,0:T(8,128)(2,1)S(1)}, bf16[304,768]{1,0:T(8,128)(2,1)S(1)}, u32[]{:S(2)}, u32[]{:S(2)}) collective-permute-start(bf16[304,768]{1,0:T(8,128)(2,1)S(1)} %collective-permute-done.9.x_first), channel_id=1, source_target_pairs={{34,0},{98,64},{162,128},{226,192},{0,32},{64,96},{128,160},{192,2... | collective-permute-start | bytes 1400840 | tf_op jit(solution)/shard_map/ppermute | solution.py:421
  41.6 0.4 collective-permute-done.11.y_first
  42.0 3.7 %collective-permute-start.14 = (bf16[304,768]{1,0:T(8,128)(2,1)S(1)}, bf16[304,768]{1,0:T(8,128)(2,1)S(1)}, u32[]{:S(2)}, u32[]{:S(2)}) collective-permute-start(bf16[304,768]{1,0:T(8,128)(2,1)S(1)} %collective-permute-done.11.y_first), channel_id=1, source_target_pairs={{192,0},{0,64},{64,128},{128,192},{224,32},{32,96},{96,160},{160,2... | collective-permute-start | bytes 1400840 | tf_op jit(solution)/shard_map/ppermute | solution.py:421
  45.7 0.0 collective-permute-done.10.x_second
  45.7 0.0 collective-permute-done.12.y_second
  45.7 2.5 %shard_map.54 = (f32[8,384]{1,0:T(8,128)S(1)}, f32[2,304,128]{2,1,0:T(8,128)S(1)}, s32[32,128]{1,0:T(8,128)S(1)}) custom-call(bf16[304,768]{1,0:T(8,128)(2,1)S(1)} %shard_map.52.own, bf16[304,768]{1,0:T(8,128)(2,1)S(1)} %collective-permute-done.9.x_first, bf16[304,768]{1,0:T(8,128)(2,1)S(1)} %collective-permute-done.10.x_second, ...), custom_call_target="tpu_custom_call" | custom-call | flops 1135607808 | bytes 933888 | tf_op jit(solution)/shard_map/pallas_call | solution.py:60
  48.2 0.0 collective-permute-done.13.x_far
  48.2 0.9 %shard_map.55 = (f32[8,384]{1,0:T(8,128)S(1)}, s32[16,128]{1,0:T(8,128)S(1)}) custom-call(bf16[304,768]{1,0:T(8,128)(2,1)S(1)} %shard_map.52.own, bf16[304,768]{1,0:T(8,128)(2,1)S(1)} %collective-permute-done.11.y_first, bf16[304,768]{1,0:T(8,128)(2,1)S(1)} %collective-permute-done.12.y_second, bf16[304,768]{1,0:T(8,128)(2,1)S(1)} %collective-permute-done.13.x_far, ...), custom_call_target="tpu_custom_call" | custom-call | flops 425852928 | bytes 933888 | tf_op jit(solution)/shard_map/pallas_call | solution.py:60
  49.2 2.0 %collective-permute-done.14.y_far = bf16[304,768]{1,0:T(8,128)(2,1)S(1)} collective-permute-done((bf16[304,768]{1,0:T(8,128)(2,1)S(1)}, bf16[304,768]{1,0:T(8,128)(2,1)S(1)}, u32[]{:S(2)}, u32[]{:S(2)}) %collective-permute-start.14) | collective-permute-done | bytes 466976 | tf_op jit(solution)/shard_map/ppermute | solution.py:421
  51.2 2.1 %shard_map.56 = f32[64,1,128]{2,1,0:T(1,128)} custom-call(bf16[304,768]{1,0:T(8,128)(2,1)S(1)} %shard_map.52.own, bf16[304,768]{1,0:T(8,128)(2,1)S(1)} %collective-permute-done.9.x_first, bf16[304,768]{1,0:T(8,128)(2,1)S(1)} %collective-permute-done.10.x_second, bf16[304,768]{1,0:T(8,128)(2,1)S(1)} %collective-permute-done.11.y_first, ...), custom_call_target="tpu_custom_call" | custom-call | flops 567803904 | bytes 933888 | tf_op jit(solution)/shard_map/pallas_call | solution.py:60
  53.4 9.6 %all-to-all-start.1 = ((f32[64,1,128]{2,1,0:T(1,128)}), f32[64,1,128]{2,1,0:T(1,128)S(1)}, u32[]{:S(2)}, u32[]{:S(2)}) async-start(f32[64,1,128]{2,1,0:T(1,128)} %shard_map.56), calls=%async_computation.1 | async-start | bytes 65536 | tf_op jit(solution)/shard_map/all_to_all | solution.py:463
  63.0 9.2 %all-to-all-done.1.ans_ref = f32[64,1,128]{2,1,0:T(1,128)S(1)} async-done(((f32[64,1,128]{2,1,0:T(1,128)}), f32[64,1,128]{2,1,0:T(1,128)S(1)}, u32[]{:S(2)}, u32[]{:S(2)}) %all-to-all-start.1) | async-done | bytes 32800 | tf_op jit(solution)/shard_map/all_to_all | solution.py:463
  72.2 0.7 shard_map.57
  73.5 0.0 copy-start.1
  73.5 0.6 copy-done.1
  (2 shorter events, 0.0 us)
Async XLA Ops:
  0.0 1.6 %copy-start = (bf16[256,768]{1,0:T(8,128)(2,1)S(1)}, bf16[256,768]{1,0:T(8,128)(2,1)}, u32[]{:S(2)}) copy-start(bf16[256,768]{1,0:T(8,128)(2,1)} %emb_ref.1) | copy-start | bytes 1179652
  2.2 13.3 %collective-permute-start.2 = (bf16[608,128]{1,0:T(8,128)(2,1)S(1)}, bf16[608,128]{1,0:T(8,128)(2,1)S(1)}, u32[]{:S(2)}, u32[]{:S(2)}) collective-permute-start(bf16[608,128]{1,0:T(8,128)(2,1)S(1)} %get-tuple-element.85), channel_id=1, source_target_pairs={{0,8},{1,25},{4,12},{5,29},{8,16},{9,1},{12,20},{13,5},{16,24},{17... | collective-permute-start | bytes 466952 | tf_op jit(solution)/shard_map/ppermute | solution.py:392
  9.1 6.5 %collective-permute-start.1 = (bf16[304,128]{1,0:T(8,128)(2,1)S(1)}, bf16[304,128]{1,0:T(8,128)(2,1)S(1)}, u32[]{:S(2)}, u32[]{:S(2)}) collective-permute-start(bf16[304,128]{1,0:T(8,128)(2,1)S(1)} %get-tuple-element.84), channel_id=1, source_target_pairs={{0,4},{1,29},{4,8},{5,1},{8,12},{9,5},{12,16},{13,9},{16,20},{17,1... | collective-permute-start | bytes 233480 | tf_op jit(solution)/shard_map/ppermute | solution.py:392
  9.8 8.9 %collective-permute-start.3 = (bf16[304,128]{1,0:T(8,128)(2,1)S(1)}, bf16[304,128]{1,0:T(8,128)(2,1)S(1)}, u32[]{:S(2)}, u32[]{:S(2)}) collective-permute-start(bf16[304,128]{1,0:T(8,128)(2,1)S(1)} %get-tuple-element.86), channel_id=1, source_target_pairs={{0,12},{1,21},{4,16},{5,25},{8,20},{9,29},{12,24},{13,1},{16,28},{... | collective-permute-start | bytes 233480 | tf_op jit(solution)/shard_map/ppermute | solution.py:392
  10.4 9.6 %collective-permute-start.5 = (bf16[304,128]{1,0:T(8,128)(2,1)S(1)}, bf16[304,128]{1,0:T(8,128)(2,1)S(1)}, u32[]{:S(2)}, u32[]{:S(2)}) collective-permute-start(bf16[304,128]{1,0:T(8,128)(2,1)S(1)} %get-tuple-element.87), channel_id=1, source_target_pairs={{0,20},{1,13},{4,24},{5,17},{8,28},{9,21},{12,0},{13,25},{16,4},{1... | collective-permute-start | bytes 233480 | tf_op jit(solution)/shard_map/ppermute | solution.py:392
  13.1 8.6 %collective-permute-start.6 = (bf16[304,128]{1,0:T(8,128)(2,1)S(1)}, bf16[304,128]{1,0:T(8,128)(2,1)S(1)}, u32[]{:S(2)}, u32[]{:S(2)}) collective-permute-start(bf16[304,128]{1,0:T(8,128)(2,1)S(1)} %get-tuple-element.88), channel_id=1, source_target_pairs={{0,24},{1,9},{4,28},{5,13},{8,0},{9,17},{12,4},{13,21},{16,8},{17,... | collective-permute-start | bytes 233480 | tf_op jit(solution)/shard_map/ppermute | solution.py:392
  15.5 9.4 %collective-permute-start.7 = (bf16[304,128]{1,0:T(8,128)(2,1)S(1)}, bf16[304,128]{1,0:T(8,128)(2,1)S(1)}, u32[]{:S(2)}, u32[]{:S(2)}) collective-permute-start(bf16[304,128]{1,0:T(8,128)(2,1)S(1)} %get-tuple-element.89), channel_id=1, source_target_pairs={{0,28},{1,5},{4,0},{5,9},{8,4},{9,13},{12,8},{13,17},{16,12},{17,2... | collective-permute-start | bytes 233480 | tf_op jit(solution)/shard_map/ppermute | solution.py:392
  15.6 9.3 %collective-permute-start.4 = (bf16[304,128]{1,0:T(8,128)(2,1)S(1)}, bf16[304,128]{1,0:T(8,128)(2,1)S(1)}, u32[]{:S(2)}, u32[]{:S(2)}) collective-permute-start(bf16[304,128]{1,0:T(8,128)(2,1)S(1)} %slice.65), channel_id=1, source_target_pairs={{0,8},{1,25},{4,12},{5,29},{8,16},{9,1},{12,20},{13,5},{16,24},{17... | collective-permute-start | bytes 233480 | tf_op jit(solution)/shard_map/ppermute | solution.py:392
  25.0 2.9 %collective-permute-start.8 = (bf16[416,768]{1,0:T(8,128)(2,1)S(1)}, bf16[416,768]{1,0:T(8,128)(2,1)S(1)}, u32[]{:S(2)}, u32[]{:S(2)}) collective-permute-start(bf16[416,768]{1,0:T(8,128)(2,1)S(1)} %shard_map.50.own_ref), channel_id=1, source_target_pairs={{0,1},{1,0},{2,3},{3,2},{4,5},{5,4},{6,7},{7,6},{8,9},{9,8},{10,11... | collective-permute-start | bytes 1916936 | tf_op jit(solution)/shard_map/ppermute | solution.py:409
  28.7 9.5 %collective-permute-start.9 = (bf16[304,768]{1,0:T(8,128)(2,1)S(1)}, bf16[304,768]{1,0:T(8,128)(2,1)S(1)}, u32[]{:S(2)}, u32[]{:S(2)}) collective-permute-start(bf16[304,768]{1,0:T(8,128)(2,1)S(1)} %shard_map.52.own), channel_id=1, source_target_pairs={{34,0},{98,64},{162,128},{226,192},{0,32},{64,96},{128,160},{192,2... | collective-permute-start | bytes 1400840 | tf_op jit(solution)/shard_map/ppermute | solution.py:421
  31.3 10.7 %collective-permute-start.11 = (bf16[304,768]{1,0:T(8,128)(2,1)S(1)}, bf16[304,768]{1,0:T(8,128)(2,1)S(1)}, u32[]{:S(2)}, u32[]{:S(2)}) collective-permute-start(bf16[304,768]{1,0:T(8,128)(2,1)S(1)} %shard_map.52.own), channel_id=1, source_target_pairs={{192,0},{0,64},{64,128},{128,192},{224,32},{32,96},{96,160},{160,2... | collective-permute-start | bytes 1400840 | tf_op jit(solution)/shard_map/ppermute | solution.py:421
  34.6 11.1 %collective-permute-start.10 = (bf16[304,768]{1,0:T(8,128)(2,1)S(1)}, bf16[304,768]{1,0:T(8,128)(2,1)S(1)}, u32[]{:S(2)}, u32[]{:S(2)}) collective-permute-start(bf16[304,768]{1,0:T(8,128)(2,1)S(1)} %shard_map.52.own), channel_id=1, source_target_pairs={{32,0},{96,64},{160,128},{224,192},{2,32},{66,96},{130,160},{194,2... | collective-permute-start | bytes 1400840 | tf_op jit(solution)/shard_map/ppermute | solution.py:421
  34.7 11.0 %collective-permute-start.12 = (bf16[304,768]{1,0:T(8,128)(2,1)S(1)}, bf16[304,768]{1,0:T(8,128)(2,1)S(1)}, u32[]{:S(2)}, u32[]{:S(2)}) collective-permute-start(bf16[304,768]{1,0:T(8,128)(2,1)S(1)} %shard_map.52.own), channel_id=1, source_target_pairs={{64,0},{128,64},{192,128},{0,192},{96,32},{160,96},{224,160},{32,2... | collective-permute-start | bytes 1400840 | tf_op jit(solution)/shard_map/ppermute | solution.py:421
  38.2 10.0 %collective-permute-start.13 = (bf16[304,768]{1,0:T(8,128)(2,1)S(1)}, bf16[304,768]{1,0:T(8,128)(2,1)S(1)}, u32[]{:S(2)}, u32[]{:S(2)}) collective-permute-start(bf16[304,768]{1,0:T(8,128)(2,1)S(1)} %collective-permute-done.9.x_first), channel_id=1, source_target_pairs={{34,0},{98,64},{162,128},{226,192},{0,32},{64,96},{128,160},{192,2... | collective-permute-start | bytes 1400840 | tf_op jit(solution)/shard_map/ppermute | solution.py:421
  42.0 9.2 %collective-permute-start.14 = (bf16[304,768]{1,0:T(8,128)(2,1)S(1)}, bf16[304,768]{1,0:T(8,128)(2,1)S(1)}, u32[]{:S(2)}, u32[]{:S(2)}) collective-permute-start(bf16[304,768]{1,0:T(8,128)(2,1)S(1)} %collective-permute-done.11.y_first), channel_id=1, source_target_pairs={{192,0},{0,64},{64,128},{128,192},{224,32},{32,96},{96,160},{160,2... | collective-permute-start | bytes 1400840 | tf_op jit(solution)/shard_map/ppermute | solution.py:421
  53.4 18.8 %all-to-all-start.1 = ((f32[64,1,128]{2,1,0:T(1,128)}), f32[64,1,128]{2,1,0:T(1,128)S(1)}, u32[]{:S(2)}, u32[]{:S(2)}) async-start(f32[64,1,128]{2,1,0:T(1,128)} %shard_map.56), calls=%async_computation.1 | async-start | bytes 65536 | tf_op jit(solution)/shard_map/all_to_all | solution.py:463
  73.5 0.6 copy-start.1

commit v9 on v5

--- a/solution.py
+++ b/solution.py
@@ -256,19 +256,28 @@
         best_ref[i : i + 1, :CAP] = best
 
 
-def mid_kernel(own, y_first, y_second, x_far, own_columns, columns_ref, out_ref, places_ref):
+def mid_kernel(
+    own, x_first, x_second, y_first, y_second, x_far, own_columns, columns_ref, near_ref,
+    out_ref, places_ref, queries_ref, ranks_ref,
+):
     ranks = row_ranks(x_far)
     best = earlier_best(x_far, ranks, own, own_columns[:, 0:1])
     for i, key in enumerate((y_first, y_second)):
         best = jnp.maximum(best, earlier_best(x_far, ranks, key, columns_ref[i, :, 0:1]))
-    out_ref[...] = jnp.full((8, CAPL), -1.0, jnp.float32)
-    out_ref[0:1, :CAP] = best
+    out_ref[...] = jnp.full((8, 4 * CAPL), -1.0, jnp.float32)
+    ranks_ref[...] = jnp.zeros((8, 4 * CAPL), jnp.float32)
+    for i, query in enumerate((own, x_first, x_second, x_far)):
+        at = i * CAPL
+        out_ref[0:1, at : at + CAP] = best if i == 3 else near_ref[i : i + 1, :CAP]
+        ranks_ref[0:1, at : at + CAP] = row_ranks(query)
+        queries_ref[at : at + CAP, :] = query[...]
+        queries_ref[at + CAP : at + CAPL, :] = jnp.zeros((CAPL - CAP, WIDTH), jnp.bfloat16)
     places_ref[...] = slot_places(x_far)
 
 
 def far_kernel(
     own, x_first, x_second, y_first, y_second, x_far, y_far,
-    own_places, near_ref, near_places, mid_ref, mid_places, out_ref,
+    own_places, near_places, mid_ref, mid_places, queries_ref, ranks_ref, out_ref,
 ):
     queries, keys = (own, x_first, x_second, x_far), (y_first, y_second, y_far)
     far_columns = column_ranks(y_far, make_eye())
@@ -280,11 +289,12 @@
     my_core, my_z = lax.axis_index("core"), lax.axis_index("z")
     my_x = 2 * lax.axis_index("xh") + lax.axis_index("xl")
     rows = []
-    for i, query in enumerate(queries):
-        best = earlier_best(query, row_ranks(query), y_far, far_columns)
-        best = jnp.maximum(best, near_ref[i : i + 1, :CAP] if i < 3 else mid_ref[0:1, :CAP])
-        best = jnp.concatenate([best, jnp.full((1, CAPL - CAP), -1.0, jnp.float32)], axis=1)
-        rows.append(jnp.broadcast_to(best, (16, CAPL)))
+    for first in range(0, 4 * CAPL, 2 * CAPL):
+        two = slice(first, first + 2 * CAPL)
+        scores = dot(y_far[...], queries_ref[two, :], ((1,), (1,)))
+        best = jnp.where(far_columns < ranks_ref[0:1, two], scores, -1.0)
+        best = jnp.maximum(jnp.max(best, axis=0, keepdims=True), mid_ref[0:1, two])
+        rows += [jnp.broadcast_to(best[:, at : at + CAPL], (16, CAPL)) for at in (0, CAPL)]
     rows = jnp.concatenate(rows, axis=0)
     places = jnp.concatenate([own_places[...], near_places[...], mid_places[...]], axis=0)
     found = jnp.full((64, META), -1.0, jnp.float32)
@@ -437,15 +447,15 @@
         own_columns,
         cost=8,
     )
-    mid, mid_places = call(
+    wide = shape((8, 4 * CAPL), f32)
+    mid, mid_places, queries, ranks = call(
         mid_kernel,
-        (best_shape, places_shape),
-        block,
-        y_first,
-        y_second,
+        (wide, places_shape, shape((4 * CAPL, WIDTH), bf16), wide),
+        *near_blocks,
         x_far,
         own_columns,
         columns,
+        near,
         cost=3,
     )
     message = call(
@@ -455,10 +465,11 @@
         x_far,
         y_far,
         own_places,
-        near,
         near_places,
         mid,
         mid_places,
+        queries,
+        ranks,
         cost=4,
     )
     answer = lax.all_to_all(message, RETURN, split_axis=0, concat_axis=0, tiled=True)

time: 74.2 us -> 76.6 us (1.032)
  Pallas kernels: 9.25 us -> 12.2 us
  waiting for transfers between devices: 22.2 us -> 20.7 us
  local copies, waits for them, and re-layouts: 0.57 us -> 1.55 us
    pallas_call x10, Pallas kernels: 9.25 us -> 12.2 us  [call(): pl.pallas_call(kernel, out_shape=out, in_specs=[space(i, smem) for i in r...]
    ppermute x6, waiting for transfers between devices: 5.87 us -> 4.36 us  [body(): bring = lambda v, dx, dy: lax.ppermute(v, PLANE, plane_shift(dx, dy))]
    unnamed x4, local copies, waits for them, and re-layouts: 0.56 us -> 1.55 us
  transfers between devices with their start and end apart: 15 -> 15, of which waited for: 9 -> 9; matrix products, arithmetic and copies ran while one was open for 0% -> 0% of each run, Pallas kernels for 6% -> 8%
where the time goes in v9:
time: 76.6 us; the launch traced here: 76.4 us
  starting transfers between devices  39.9 us (52%)
  waiting for transfers between devices  20.7 us (27%)
  Pallas kernels  12.2 us (16%)
  local copies, waits for them, and re-layouts  1.55 us (2%)
  between operations  1.42 us (2%)
    ppermute x7, starting transfers between devices, body(): send = lambda v, steps: lax.ppermute(v, COLUMN, column_shift(steps))  16.5 us
    ppermute x6, starting transfers between devices, body(): bring = lambda v, dx, dy: lax.ppermute(v, PLANE, plane_shift(dx, dy))  12.6 us
    pallas_call x10, Pallas kernels, call(): pl.pallas_call(kernel, out_shape=out, in_specs=[space(i, smem) for i in r...  12.2 us
    all_to_all x1, starting transfers between devices, body(): lax.all_to_all(message, RETURN, split_axis=0, concat_axis=0, tiled=True)  9.62 us
    all_to_all x1, waiting for transfers between devices, body(): lax.all_to_all(message, RETURN, split_axis=0, concat_axis=0, tiled=True)  9.19 us
    ppermute x7, waiting for transfers between devices, body(): send = lambda v, steps: lax.ppermute(v, COLUMN, column_shift(steps))  6.21 us
    ppermute x6, waiting for transfers between devices, body(): bring = lambda v, dx, dy: lax.ppermute(v, PLANE, plane_shift(dx, dy))  4.36 us
    unnamed x4, local copies, waits for them, and re-layouts  1.55 us
  transfers between devices with their start and end apart: 15, of which 9 were waited for; matrix products, arithmetic and copies ran while one was open for 0% of the time, Pallas kernels for 8%

profile of v9, /device:TPU:1, one launch (start us, length us, event | category | flops | bytes accessed | tf_op | source)
XLA Modules:
  0.0 76.4 jit_solution(14916573124346207028)
XLA Ops:
  0.0 0.7 multiply_add_fusion
  0.7 0.2 shard_map.48
  1.6 0.0 copy-start
  1.6 1.0 %copy-done = bf16[256,768]{1,0:T(8,128)(2,1)S(1)} copy-done((bf16[256,768]{1,0:T(8,128)(2,1)S(1)}, bf16[256,768]{1,0:T(8,128)(2,1)}, u32[]{:S(2)}) %copy-start) | copy-done | bytes 393240
  2.6 0.5 shard_map.49
  3.1 6.9 %collective-permute-start.2 = (bf16[608,128]{1,0:T(8,128)(2,1)S(1)}, bf16[608,128]{1,0:T(8,128)(2,1)S(1)}, u32[]{:S(2)}, u32[]{:S(2)}) collective-permute-start(bf16[608,128]{1,0:T(8,128)(2,1)S(1)} %get-tuple-element.87), channel_id=1, source_target_pairs={{0,8},{1,25},{4,12},{5,29},{8,16},{9,1},{12,20},{13,5},{16,24},{17... | collective-permute-start | bytes 466952 | tf_op jit(solution)/shard_map/ppermute | solution.py:403
  10.0 0.7 collective-permute-start.1
  10.8 0.5 collective-permute-start.3
  11.3 2.7 %collective-permute-start.5 = (bf16[304,128]{1,0:T(8,128)(2,1)S(1)}, bf16[304,128]{1,0:T(8,128)(2,1)S(1)}, u32[]{:S(2)}, u32[]{:S(2)}) collective-permute-start(bf16[304,128]{1,0:T(8,128)(2,1)S(1)} %get-tuple-element.89), channel_id=1, source_target_pairs={{0,20},{1,13},{4,24},{5,17},{8,28},{9,21},{12,0},{13,25},{16,4},{1... | collective-permute-start | bytes 233480 | tf_op jit(solution)/shard_map/ppermute | solution.py:403
  14.0 2.4 %collective-permute-start.6 = (bf16[304,128]{1,0:T(8,128)(2,1)S(1)}, bf16[304,128]{1,0:T(8,128)(2,1)S(1)}, u32[]{:S(2)}, u32[]{:S(2)}) collective-permute-start(bf16[304,128]{1,0:T(8,128)(2,1)S(1)} %get-tuple-element.90), channel_id=1, source_target_pairs={{0,24},{1,9},{4,28},{5,13},{8,0},{9,17},{12,4},{13,21},{16,8},{17,... | collective-permute-start | bytes 233480 | tf_op jit(solution)/shard_map/ppermute | solution.py:403
  16.4 0.0 collective-permute-done.2.refs_2_
  16.4 0.0 collective-permute-start.7
  16.5 0.1 collective-permute-done.1.refs_1_
  16.5 3.1 %collective-permute-start.4 = (bf16[304,128]{1,0:T(8,128)(2,1)S(1)}, bf16[304,128]{1,0:T(8,128)(2,1)S(1)}, u32[]{:S(2)}, u32[]{:S(2)}) collective-permute-start(bf16[304,128]{1,0:T(8,128)(2,1)S(1)} %slice.65), channel_id=1, source_target_pairs={{0,8},{1,25},{4,12},{5,29},{8,16},{9,1},{12,20},{13,5},{16,24},{17... | collective-permute-start | bytes 233480 | tf_op jit(solution)/shard_map/ppermute | solution.py:403
  19.6 0.0 collective-permute-done.3.refs_3_
  19.7 1.3 %collective-permute-done.5.refs_5_ = bf16[304,128]{1,0:T(8,128)(2,1)S(1)} collective-permute-done((bf16[304,128]{1,0:T(8,128)(2,1)S(1)}, bf16[304,128]{1,0:T(8,128)(2,1)S(1)}, u32[]{:S(2)}, u32[]{:S(2)}) %collective-permute-start.5) | collective-permute-done | bytes 77856 | tf_op jit(solution)/shard_map/ppermute | solution.py:403
  20.9 1.8 %collective-permute-done.6.refs_6_ = bf16[304,128]{1,0:T(8,128)(2,1)S(1)} collective-permute-done((bf16[304,128]{1,0:T(8,128)(2,1)S(1)}, bf16[304,128]{1,0:T(8,128)(2,1)S(1)}, u32[]{:S(2)}, u32[]{:S(2)}) %collective-permute-start.6) | collective-permute-done | bytes 77856 | tf_op jit(solution)/shard_map/ppermute | solution.py:403
  22.7 3.1 %collective-permute-done.7.refs_7_ = bf16[304,128]{1,0:T(8,128)(2,1)S(1)} collective-permute-done((bf16[304,128]{1,0:T(8,128)(2,1)S(1)}, bf16[304,128]{1,0:T(8,128)(2,1)S(1)}, u32[]{:S(2)}, u32[]{:S(2)}) %collective-permute-start.7) | collective-permute-done | bytes 77856 | tf_op jit(solution)/shard_map/ppermute | solution.py:403
  25.8 0.0 collective-permute-done.4.refs_4_
  25.8 0.1 shard_map.50.own_ref
  25.9 1.2 %collective-permute-start.8 = (bf16[416,768]{1,0:T(8,128)(2,1)S(1)}, bf16[416,768]{1,0:T(8,128)(2,1)S(1)}, u32[]{:S(2)}, u32[]{:S(2)}) collective-permute-start(bf16[416,768]{1,0:T(8,128)(2,1)S(1)} %shard_map.50.own_ref), channel_id=1, source_target_pairs={{0,1},{1,0},{2,3},{3,2},{4,5},{5,4},{6,7},{7,6},{8,9},{9,8},{10,11... | collective-permute-start | bytes 1916936 | tf_op jit(solution)/shard_map/ppermute | solution.py:420
  27.2 0.8 %shard_map.51 = (bf16[304,768]{1,0:T(8,128)(2,1)S(1)}, s32[8,384]{1,0:T(8,128)S(1)}, f32[8,384]{1,0:T(8,128)S(1)}, f32[8,128]{1,0:T(8,128)S(1)}) custom-call(bf16[416,768]{1,0:T(8,128)(2,1)S(1)} %shard_map.50.own_ref), custom_call_target="tpu_custom_call" | custom-call | flops 141950976 | bytes 933888 | tf_op jit(solution)/shard_map/pallas_call | solution.py:60
  27.9 0.9 %collective-permute-done.8.other_ref = bf16[416,768]{1,0:T(8,128)(2,1)S(1)} collective-permute-done((bf16[416,768]{1,0:T(8,128)(2,1)S(1)}, bf16[416,768]{1,0:T(8,128)(2,1)S(1)}, u32[]{:S(2)}, u32[]{:S(2)}) %collective-permute-start.8) | collective-permute-done | bytes 639008 | tf_op jit(solution)/shard_map/ppermute | solution.py:420
  28.9 0.8 %shard_map.52.own = bf16[304,768]{1,0:T(8,128)(2,1)S(1)} custom-call(bf16[416,768]{1,0:T(8,128)(2,1)S(1)} %collective-permute-done.8.other_ref, bf16[304,768]{1,0:T(8,128)(2,1)S(1)} %get-tuple-element.92.rows_ref, s32[8,384]{1,0:T(8,128)S(1)} %get-tuple-element.93.pos_ref, f32[8,384]{1,0:T(8,128)S(1)} %get-tuple-element.94.ranks_ref, ...), custom_call_target="tpu_custom_call" | custom-call | flops 141950976 | bytes 933888 | tf_op jit(solution)/shard_map/pallas_call | solution.py:60
  29.7 2.6 %collective-permute-start.9 = (bf16[304,768]{1,0:T(8,128)(2,1)S(1)}, bf16[304,768]{1,0:T(8,128)(2,1)S(1)}, u32[]{:S(2)}, u32[]{:S(2)}) collective-permute-start(bf16[304,768]{1,0:T(8,128)(2,1)S(1)} %shard_map.52.own), channel_id=1, source_target_pairs={{34,0},{98,64},{162,128},{226,192},{0,32},{64,96},{128,160},{192,2... | collective-permute-start | bytes 1400840 | tf_op jit(solution)/shard_map/ppermute | solution.py:432
  32.2 2.7 %collective-permute-start.11 = (bf16[304,768]{1,0:T(8,128)(2,1)S(1)}, bf16[304,768]{1,0:T(8,128)(2,1)S(1)}, u32[]{:S(2)}, u32[]{:S(2)}) collective-permute-start(bf16[304,768]{1,0:T(8,128)(2,1)S(1)} %shard_map.52.own), channel_id=1, source_target_pairs={{192,0},{0,64},{64,128},{128,192},{224,32},{32,96},{96,160},{160,2... | collective-permute-start | bytes 1400840 | tf_op jit(solution)/shard_map/ppermute | solution.py:432
  35.0 0.6 shard_map.53
  35.5 0.1 collective-permute-start.10
  35.6 0.1 collective-permute-start.12
  35.7 3.4 %collective-permute-done.9.x_first = bf16[304,768]{1,0:T(8,128)(2,1)S(1)} collective-permute-done((bf16[304,768]{1,0:T(8,128)(2,1)S(1)}, bf16[304,768]{1,0:T(8,128)(2,1)S(1)}, u32[]{:S(2)}, u32[]{:S(2)}) %collective-permute-start.9) | collective-permute-done | bytes 466976 | tf_op jit(solution)/shard_map/ppermute | solution.py:432
  39.1 3.4 %collective-permute-start.13 = (bf16[304,768]{1,0:T(8,128)(2,1)S(1)}, bf16[304,768]{1,0:T(8,128)(2,1)S(1)}, u32[]{:S(2)}, u32[]{:S(2)}) collective-permute-start(bf16[304,768]{1,0:T(8,128)(2,1)S(1)} %collective-permute-done.9.x_first), channel_id=1, source_target_pairs={{34,0},{98,64},{162,128},{226,192},{0,32},{64,96},{128,160},{192,2... | collective-permute-start | bytes 1400840 | tf_op jit(solution)/shard_map/ppermute | solution.py:432
  42.6 0.4 collective-permute-done.11.y_first
  43.0 3.7 %collective-permute-start.14 = (bf16[304,768]{1,0:T(8,128)(2,1)S(1)}, bf16[304,768]{1,0:T(8,128)(2,1)S(1)}, u32[]{:S(2)}, u32[]{:S(2)}) collective-permute-start(bf16[304,768]{1,0:T(8,128)(2,1)S(1)} %collective-permute-done.11.y_first), channel_id=1, source_target_pairs={{192,0},{0,64},{64,128},{128,192},{224,32},{32,96},{96,160},{160,2... | collective-permute-start | bytes 1400840 | tf_op jit(solution)/shard_map/ppermute | solution.py:432
  46.6 0.0 collective-permute-done.10.x_second
  46.7 0.0 collective-permute-done.12.y_second
  46.7 2.5 %shard_map.54 = (f32[8,384]{1,0:T(8,128)S(1)}, f32[2,304,128]{2,1,0:T(8,128)S(1)}, s32[32,128]{1,0:T(8,128)S(1)}) custom-call(bf16[304,768]{1,0:T(8,128)(2,1)S(1)} %shard_map.52.own, bf16[304,768]{1,0:T(8,128)(2,1)S(1)} %collective-permute-done.9.x_first, bf16[304,768]{1,0:T(8,128)(2,1)S(1)} %collective-permute-done.10.x_second, ...), custom_call_target="tpu_custom_call" | custom-call | flops 1135607808 | bytes 933888 | tf_op jit(solution)/shard_map/pallas_call | solution.py:60
  49.2 0.0 collective-permute-done.13.x_far
  49.2 2.4 %shard_map.55 = (f32[8,1536]{1,0:T(8,128)S(1)}, s32[16,128]{1,0:T(8,128)S(1)}, bf16[1536,768]{1,0:T(8,128)(2,1)}, f32[8,1536]{1,0:T(8,128)S(1)}) custom-call(bf16[304,768]{1,0:T(8,128)(2,1)S(1)} %shard_map.52.own, bf16[304,768]{1,0:T(8,128)(2,1)S(1)} %collective-permute-done.9.x_first, bf16[304,768]{1,0:T(8,128)(2,1)S(1)} %collective-permute-done.10.x_second, ...), custom_call_target="tpu_custom_call" | custom-call | flops 425852928 | bytes 933888 | tf_op jit(solution)/shard_map/pallas_call | solution.py:60
  51.6 0.5 collective-permute-done.14.y_far
  52.2 3.6 %shard_map.56 = f32[64,1,128]{2,1,0:T(1,128)} custom-call(bf16[304,768]{1,0:T(8,128)(2,1)S(1)} %shard_map.52.own, bf16[304,768]{1,0:T(8,128)(2,1)S(1)} %collective-permute-done.9.x_first, bf16[304,768]{1,0:T(8,128)(2,1)S(1)} %collective-permute-done.10.x_second, bf16[304,768]{1,0:T(8,128)(2,1)S(1)} %collective-permute-done.11.y_first, ...), custom_call_target="tpu_custom_call" | custom-call | flops 567803904 | bytes 933888 | tf_op jit(solution)/shard_map/pallas_call | solution.py:60
  55.7 9.6 %all-to-all-start.1 = ((f32[64,1,128]{2,1,0:T(1,128)}), f32[64,1,128]{2,1,0:T(1,128)S(1)}, u32[]{:S(2)}, u32[]{:S(2)}) async-start(f32[64,1,128]{2,1,0:T(1,128)} %shard_map.56), calls=%async_computation.1 | async-start | bytes 65536 | tf_op jit(solution)/shard_map/all_to_all | solution.py:475
  65.3 9.2 %all-to-all-done.1.ans_ref = f32[64,1,128]{2,1,0:T(1,128)S(1)} async-done(((f32[64,1,128]{2,1,0:T(1,128)}), f32[64,1,128]{2,1,0:T(1,128)S(1)}, u32[]{:S(2)}, u32[]{:S(2)}) %all-to-all-start.1) | async-done | bytes 32800 | tf_op jit(solution)/shard_map/all_to_all | solution.py:475
  74.5 0.7 shard_map.57
  75.9 0.0 copy-start.1
  75.9 0.6 copy-done.1
  (2 shorter events, 0.0 us)
Async XLA Ops:
  1.6 1.0 %copy-start = (bf16[256,768]{1,0:T(8,128)(2,1)S(1)}, bf16[256,768]{1,0:T(8,128)(2,1)}, u32[]{:S(2)}) copy-start(bf16[256,768]{1,0:T(8,128)(2,1)} %emb_ref.1) | copy-start | bytes 1179652
  3.1 13.3 %collective-permute-start.2 = (bf16[608,128]{1,0:T(8,128)(2,1)S(1)}, bf16[608,128]{1,0:T(8,128)(2,1)S(1)}, u32[]{:S(2)}, u32[]{:S(2)}) collective-permute-start(bf16[608,128]{1,0:T(8,128)(2,1)S(1)} %get-tuple-element.87), channel_id=1, source_target_pairs={{0,8},{1,25},{4,12},{5,29},{8,16},{9,1},{12,20},{13,5},{16,24},{17... | collective-permute-start | bytes 466952 | tf_op jit(solution)/shard_map/ppermute | solution.py:403
  10.0 6.5 %collective-permute-start.1 = (bf16[304,128]{1,0:T(8,128)(2,1)S(1)}, bf16[304,128]{1,0:T(8,128)(2,1)S(1)}, u32[]{:S(2)}, u32[]{:S(2)}) collective-permute-start(bf16[304,128]{1,0:T(8,128)(2,1)S(1)} %get-tuple-element.86), channel_id=1, source_target_pairs={{0,4},{1,29},{4,8},{5,1},{8,12},{9,5},{12,16},{13,9},{16,20},{17,1... | collective-permute-start | bytes 233480 | tf_op jit(solution)/shard_map/ppermute | solution.py:403
  10.8 8.9 %collective-permute-start.3 = (bf16[304,128]{1,0:T(8,128)(2,1)S(1)}, bf16[304,128]{1,0:T(8,128)(2,1)S(1)}, u32[]{:S(2)}, u32[]{:S(2)}) collective-permute-start(bf16[304,128]{1,0:T(8,128)(2,1)S(1)} %get-tuple-element.88), channel_id=1, source_target_pairs={{0,12},{1,21},{4,16},{5,25},{8,20},{9,29},{12,24},{13,1},{16,28},{... | collective-permute-start | bytes 233480 | tf_op jit(solution)/shard_map/ppermute | solution.py:403
  11.3 9.6 %collective-permute-start.5 = (bf16[304,128]{1,0:T(8,128)(2,1)S(1)}, bf16[304,128]{1,0:T(8,128)(2,1)S(1)}, u32[]{:S(2)}, u32[]{:S(2)}) collective-permute-start(bf16[304,128]{1,0:T(8,128)(2,1)S(1)} %get-tuple-element.89), channel_id=1, source_target_pairs={{0,20},{1,13},{4,24},{5,17},{8,28},{9,21},{12,0},{13,25},{16,4},{1... | collective-permute-start | bytes 233480 | tf_op jit(solution)/shard_map/ppermute | solution.py:403
  14.0 8.6 %collective-permute-start.6 = (bf16[304,128]{1,0:T(8,128)(2,1)S(1)}, bf16[304,128]{1,0:T(8,128)(2,1)S(1)}, u32[]{:S(2)}, u32[]{:S(2)}) collective-permute-start(bf16[304,128]{1,0:T(8,128)(2,1)S(1)} %get-tuple-element.90), channel_id=1, source_target_pairs={{0,24},{1,9},{4,28},{5,13},{8,0},{9,17},{12,4},{13,21},{16,8},{17,... | collective-permute-start | bytes 233480 | tf_op jit(solution)/shard_map/ppermute | solution.py:403
  16.4 9.4 %collective-permute-start.7 = (bf16[304,128]{1,0:T(8,128)(2,1)S(1)}, bf16[304,128]{1,0:T(8,128)(2,1)S(1)}, u32[]{:S(2)}, u32[]{:S(2)}) collective-permute-start(bf16[304,128]{1,0:T(8,128)(2,1)S(1)} %get-tuple-element.91), channel_id=1, source_target_pairs={{0,28},{1,5},{4,0},{5,9},{8,4},{9,13},{12,8},{13,17},{16,12},{17,2... | collective-permute-start | bytes 233480 | tf_op jit(solution)/shard_map/ppermute | solution.py:403
  16.5 9.3 %collective-permute-start.4 = (bf16[304,128]{1,0:T(8,128)(2,1)S(1)}, bf16[304,128]{1,0:T(8,128)(2,1)S(1)}, u32[]{:S(2)}, u32[]{:S(2)}) collective-permute-start(bf16[304,128]{1,0:T(8,128)(2,1)S(1)} %slice.65), channel_id=1, source_target_pairs={{0,8},{1,25},{4,12},{5,29},{8,16},{9,1},{12,20},{13,5},{16,24},{17... | collective-permute-start | bytes 233480 | tf_op jit(solution)/shard_map/ppermute | solution.py:403
  25.9 2.9 %collective-permute-start.8 = (bf16[416,768]{1,0:T(8,128)(2,1)S(1)}, bf16[416,768]{1,0:T(8,128)(2,1)S(1)}, u32[]{:S(2)}, u32[]{:S(2)}) collective-permute-start(bf16[416,768]{1,0:T(8,128)(2,1)S(1)} %shard_map.50.own_ref), channel_id=1, source_target_pairs={{0,1},{1,0},{2,3},{3,2},{4,5},{5,4},{6,7},{7,6},{8,9},{9,8},{10,11... | collective-permute-start | bytes 1916936 | tf_op jit(solution)/shard_map/ppermute | solution.py:420
  29.7 9.5 %collective-permute-start.9 = (bf16[304,768]{1,0:T(8,128)(2,1)S(1)}, bf16[304,768]{1,0:T(8,128)(2,1)S(1)}, u32[]{:S(2)}, u32[]{:S(2)}) collective-permute-start(bf16[304,768]{1,0:T(8,128)(2,1)S(1)} %shard_map.52.own), channel_id=1, source_target_pairs={{34,0},{98,64},{162,128},{226,192},{0,32},{64,96},{128,160},{192,2... | collective-permute-start | bytes 1400840 | tf_op jit(solution)/shard_map/ppermute | solution.py:432
  32.2 10.7 %collective-permute-start.11 = (bf16[304,768]{1,0:T(8,128)(2,1)S(1)}, bf16[304,768]{1,0:T(8,128)(2,1)S(1)}, u32[]{:S(2)}, u32[]{:S(2)}) collective-permute-start(bf16[304,768]{1,0:T(8,128)(2,1)S(1)} %shard_map.52.own), channel_id=1, source_target_pairs={{192,0},{0,64},{64,128},{128,192},{224,32},{32,96},{96,160},{160,2... | collective-permute-start | bytes 1400840 | tf_op jit(solution)/shard_map/ppermute | solution.py:432
  35.5 11.1 %collective-permute-start.10 = (bf16[304,768]{1,0:T(8,128)(2,1)S(1)}, bf16[304,768]{1,0:T(8,128)(2,1)S(1)}, u32[]{:S(2)}, u32[]{:S(2)}) collective-permute-start(bf16[304,768]{1,0:T(8,128)(2,1)S(1)} %shard_map.52.own), channel_id=1, source_target_pairs={{32,0},{96,64},{160,128},{224,192},{2,32},{66,96},{130,160},{194,2... | collective-permute-start | bytes 1400840 | tf_op jit(solution)/shard_map/ppermute | solution.py:432
  35.6 11.0 %collective-permute-start.12 = (bf16[304,768]{1,0:T(8,128)(2,1)S(1)}, bf16[304,768]{1,0:T(8,128)(2,1)S(1)}, u32[]{:S(2)}, u32[]{:S(2)}) collective-permute-start(bf16[304,768]{1,0:T(8,128)(2,1)S(1)} %shard_map.52.own), channel_id=1, source_target_pairs={{64,0},{128,64},{192,128},{0,192},{96,32},{160,96},{224,160},{32,2... | collective-permute-start | bytes 1400840 | tf_op jit(solution)/shard_map/ppermute | solution.py:432
  39.1 10.0 %collective-permute-start.13 = (bf16[304,768]{1,0:T(8,128)(2,1)S(1)}, bf16[304,768]{1,0:T(8,128)(2,1)S(1)}, u32[]{:S(2)}, u32[]{:S(2)}) collective-permute-start(bf16[304,768]{1,0:T(8,128)(2,1)S(1)} %collective-permute-done.9.x_first), channel_id=1, source_target_pairs={{34,0},{98,64},{162,128},{226,192},{0,32},{64,96},{128,160},{192,2... | collective-permute-start | bytes 1400840 | tf_op jit(solution)/shard_map/ppermute | solution.py:432
  43.0 9.2 %collective-permute-start.14 = (bf16[304,768]{1,0:T(8,128)(2,1)S(1)}, bf16[304,768]{1,0:T(8,128)(2,1)S(1)}, u32[]{:S(2)}, u32[]{:S(2)}) collective-permute-start(bf16[304,768]{1,0:T(8,128)(2,1)S(1)} %collective-permute-done.11.y_first), channel_id=1, source_target_pairs={{192,0},{0,64},{64,128},{128,192},{224,32},{32,96},{96,160},{160,2... | collective-permute-start | bytes 1400840 | tf_op jit(solution)/shard_map/ppermute | solution.py:432
  55.7 18.8 %all-to-all-start.1 = ((f32[64,1,128]{2,1,0:T(1,128)}), f32[64,1,128]{2,1,0:T(1,128)S(1)}, u32[]{:S(2)}, u32[]{:S(2)}) async-start(f32[64,1,128]{2,1,0:T(1,128)} %shard_map.56), calls=%async_computation.1 | async-start | bytes 65536 | tf_op jit(solution)/shard_map/all_to_all | solution.py:475
  75.9 0.6 copy-start.1

commit v10 on v5

--- a/solution.py
+++ b/solution.py
@@ -420,14 +420,14 @@
     )
     block = call(compact_kernel, shape((CAP, WIDTH), bf16), other, *first)
     bring = lambda v, dx, dy: lax.ppermute(v, PLANE, plane_shift(dx, dy))
-    x_first, y_first = bring(block, -1, 0), bring(block, 0, -1)
+    x_first, y_first = bring(block, -1, 0), bring(block, 0, 1)
     best_shape, places_shape = shape((8, CAPL), f32), shape((16, META), i32)
     own_best, own_columns, own_places = call(
         own_kernel, (best_shape, shape((CAP, META), f32), places_shape), block
     )
     own, own_best = lax.optimization_barrier((block, own_best))
-    x_second, y_second = bring(own, 1, 0), bring(own, 0, 1)
-    x_far, y_far = bring(x_first, -1, 0), bring(y_first, 0, -1)
+    x_second, y_second = bring(own, 1, 0), bring(own, 0, -1)
+    x_far, y_far = bring(x_first, -1, 0), bring(y_first, 0, 1)
     near_blocks = (block, x_first, x_second, y_first, y_second)
     near, columns, near_places = call(
         near_kernel,

time: 74.2 us -> 75.4 us (1.016)
  starting transfers between devices: 39.9 us -> 41.2 us
    all_to_all x1, starting transfers between devices: 9.64 us -> 10.9 us  [body(): lax.all_to_all(message, RETURN, split_axis=0, concat_axis=0, tiled=True)]
  transfers between devices with their start and end apart: 15 -> 15, of which waited for: 9 -> 11; matrix products, arithmetic and copies ran while one was open for 0% -> 0% of each run, Pallas kernels for 6% -> 6%
where the time goes in v10:
time: 75.4 us; the launch traced here: 75.2 us
  starting transfers between devices  41.2 us (55%)
  waiting for transfers between devices  22 us (29%)
  Pallas kernels  9.25 us (12%)
  between operations  1.41 us (2%)
    ppermute x7, starting transfers between devices, body(): send = lambda v, steps: lax.ppermute(v, COLUMN, column_shift(steps))  16.5 us
    ppermute x6, starting transfers between devices, body(): bring = lambda v, dx, dy: lax.ppermute(v, PLANE, plane_shift(dx, dy))  12.6 us
    all_to_all x1, starting transfers between devices, body(): lax.all_to_all(message, RETURN, split_axis=0, concat_axis=0, tiled=True)  10.9 us
    pallas_call x10, Pallas kernels, call(): pl.pallas_call(kernel, out_shape=out, in_specs=[space(i, smem) for i in r...  9.25 us
    all_to_all x1, waiting for transfers between devices, body(): lax.all_to_all(message, RETURN, split_axis=0, concat_axis=0, tiled=True)  9.17 us
    ppermute x7, waiting for transfers between devices, body(): send = lambda v, steps: lax.ppermute(v, COLUMN, column_shift(steps))  6.21 us
    ppermute x6, waiting for transfers between devices, body(): bring = lambda v, dx, dy: lax.ppermute(v, PLANE, plane_shift(dx, dy))  5.74 us
  transfers between devices with their start and end apart: 15, of which 11 were waited for; matrix products, arithmetic and copies ran while one was open for 0% of the time, Pallas kernels for 6%

profile of v10, /device:TPU:1, one launch (start us, length us, event | category | flops | bytes accessed | tf_op | source)
XLA Modules:
  0.0 75.2 jit_solution(13697465111573578912)
XLA Ops:
  0.0 0.0 copy-start
  0.0 0.7 multiply_add_fusion
  0.8 0.2 shard_map.48
  1.6 0.0 copy-done
  1.7 0.5 shard_map.49
  2.2 6.9 %collective-permute-start.2 = (bf16[608,128]{1,0:T(8,128)(2,1)S(1)}, bf16[608,128]{1,0:T(8,128)(2,1)S(1)}, u32[]{:S(2)}, u32[]{:S(2)}) collective-permute-start(bf16[608,128]{1,0:T(8,128)(2,1)S(1)} %get-tuple-element.85), channel_id=1, source_target_pairs={{0,8},{1,25},{4,12},{5,29},{8,16},{9,1},{12,20},{13,5},{16,24},{17... | collective-permute-start | bytes 466952 | tf_op jit(solution)/shard_map/ppermute | solution.py:393
  9.1 0.7 collective-permute-start.1
  9.8 0.5 collective-permute-start.3
  10.4 2.7 %collective-permute-start.5 = (bf16[304,128]{1,0:T(8,128)(2,1)S(1)}, bf16[304,128]{1,0:T(8,128)(2,1)S(1)}, u32[]{:S(2)}, u32[]{:S(2)}) collective-permute-start(bf16[304,128]{1,0:T(8,128)(2,1)S(1)} %get-tuple-element.87), channel_id=1, source_target_pairs={{0,20},{1,13},{4,24},{5,17},{8,28},{9,21},{12,0},{13,25},{16,4},{1... | collective-permute-start | bytes 233480 | tf_op jit(solution)/shard_map/ppermute | solution.py:393
  13.1 2.4 %collective-permute-start.6 = (bf16[304,128]{1,0:T(8,128)(2,1)S(1)}, bf16[304,128]{1,0:T(8,128)(2,1)S(1)}, u32[]{:S(2)}, u32[]{:S(2)}) collective-permute-start(bf16[304,128]{1,0:T(8,128)(2,1)S(1)} %get-tuple-element.88), channel_id=1, source_target_pairs={{0,24},{1,9},{4,28},{5,13},{8,0},{9,17},{12,4},{13,21},{16,8},{17,... | collective-permute-start | bytes 233480 | tf_op jit(solution)/shard_map/ppermute | solution.py:393
  15.5 0.0 collective-permute-done.2.refs_2_
  15.5 0.0 collective-permute-start.7
  15.5 0.1 collective-permute-done.1.refs_1_
  15.6 3.1 %collective-permute-start.4 = (bf16[304,128]{1,0:T(8,128)(2,1)S(1)}, bf16[304,128]{1,0:T(8,128)(2,1)S(1)}, u32[]{:S(2)}, u32[]{:S(2)}) collective-permute-start(bf16[304,128]{1,0:T(8,128)(2,1)S(1)} %slice.65), channel_id=1, source_target_pairs={{0,8},{1,25},{4,12},{5,29},{8,16},{9,1},{12,20},{13,5},{16,24},{17... | collective-permute-start | bytes 233480 | tf_op jit(solution)/shard_map/ppermute | solution.py:393
  18.7 0.0 collective-permute-done.3.refs_3_
  18.7 1.3 %collective-permute-done.5.refs_5_ = bf16[304,128]{1,0:T(8,128)(2,1)S(1)} collective-permute-done((bf16[304,128]{1,0:T(8,128)(2,1)S(1)}, bf16[304,128]{1,0:T(8,128)(2,1)S(1)}, u32[]{:S(2)}, u32[]{:S(2)}) %collective-permute-start.5) | collective-permute-done | bytes 77856 | tf_op jit(solution)/shard_map/ppermute | solution.py:393
  20.0 1.7 %collective-permute-done.6.refs_6_ = bf16[304,128]{1,0:T(8,128)(2,1)S(1)} collective-permute-done((bf16[304,128]{1,0:T(8,128)(2,1)S(1)}, bf16[304,128]{1,0:T(8,128)(2,1)S(1)}, u32[]{:S(2)}, u32[]{:S(2)}) %collective-permute-start.6) | collective-permute-done | bytes 77856 | tf_op jit(solution)/shard_map/ppermute | solution.py:393
  21.7 3.1 %collective-permute-done.7.refs_7_ = bf16[304,128]{1,0:T(8,128)(2,1)S(1)} collective-permute-done((bf16[304,128]{1,0:T(8,128)(2,1)S(1)}, bf16[304,128]{1,0:T(8,128)(2,1)S(1)}, u32[]{:S(2)}, u32[]{:S(2)}) %collective-permute-start.7) | collective-permute-done | bytes 77856 | tf_op jit(solution)/shard_map/ppermute | solution.py:393
  24.9 0.0 collective-permute-done.4.refs_4_
  24.9 0.1 shard_map.50.own_ref
  25.0 1.2 %collective-permute-start.8 = (bf16[416,768]{1,0:T(8,128)(2,1)S(1)}, bf16[416,768]{1,0:T(8,128)(2,1)S(1)}, u32[]{:S(2)}, u32[]{:S(2)}) collective-permute-start(bf16[416,768]{1,0:T(8,128)(2,1)S(1)} %shard_map.50.own_ref), channel_id=1, source_target_pairs={{0,1},{1,0},{2,3},{3,2},{4,5},{5,4},{6,7},{7,6},{8,9},{9,8},{10,11... | collective-permute-start | bytes 1916936 | tf_op jit(solution)/shard_map/ppermute | solution.py:410
  26.2 0.8 %shard_map.51 = (bf16[304,768]{1,0:T(8,128)(2,1)S(1)}, s32[8,384]{1,0:T(8,128)S(1)}, f32[8,384]{1,0:T(8,128)S(1)}, f32[8,128]{1,0:T(8,128)S(1)}) custom-call(bf16[416,768]{1,0:T(8,128)(2,1)S(1)} %shard_map.50.own_ref), custom_call_target="tpu_custom_call" | custom-call | flops 141950976 | bytes 933888 | tf_op jit(solution)/shard_map/pallas_call | solution.py:60
  27.0 0.9 %collective-permute-done.8.other_ref = bf16[416,768]{1,0:T(8,128)(2,1)S(1)} collective-permute-done((bf16[416,768]{1,0:T(8,128)(2,1)S(1)}, bf16[416,768]{1,0:T(8,128)(2,1)S(1)}, u32[]{:S(2)}, u32[]{:S(2)}) %collective-permute-start.8) | collective-permute-done | bytes 639008 | tf_op jit(solution)/shard_map/ppermute | solution.py:410
  27.9 0.8 %shard_map.52.own = bf16[304,768]{1,0:T(8,128)(2,1)S(1)} custom-call(bf16[416,768]{1,0:T(8,128)(2,1)S(1)} %collective-permute-done.8.other_ref, bf16[304,768]{1,0:T(8,128)(2,1)S(1)} %get-tuple-element.90.rows_ref, s32[8,384]{1,0:T(8,128)S(1)} %get-tuple-element.91.pos_ref, f32[8,384]{1,0:T(8,128)S(1)} %get-tuple-element.92.ranks_ref, ...), custom_call_target="tpu_custom_call" | custom-call | flops 141950976 | bytes 933888 | tf_op jit(solution)/shard_map/pallas_call | solution.py:60
  28.7 2.6 %collective-permute-start.9 = (bf16[304,768]{1,0:T(8,128)(2,1)S(1)}, bf16[304,768]{1,0:T(8,128)(2,1)S(1)}, u32[]{:S(2)}, u32[]{:S(2)}) collective-permute-start(bf16[304,768]{1,0:T(8,128)(2,1)S(1)} %shard_map.52.own), channel_id=1, source_target_pairs={{34,0},{98,64},{162,128},{226,192},{0,32},{64,96},{128,160},{192,2... | collective-permute-start | bytes 1400840 | tf_op jit(solution)/shard_map/ppermute | solution.py:422
  31.3 1.3 %collective-permute-start.11 = (bf16[304,768]{1,0:T(8,128)(2,1)S(1)}, bf16[304,768]{1,0:T(8,128)(2,1)S(1)}, u32[]{:S(2)}, u32[]{:S(2)}) collective-permute-start(bf16[304,768]{1,0:T(8,128)(2,1)S(1)} %shard_map.52.own), channel_id=1, source_target_pairs={{64,0},{128,64},{192,128},{0,192},{96,32},{160,96},{224,160},{32,2... | collective-permute-start | bytes 1400840 | tf_op jit(solution)/shard_map/ppermute | solution.py:422
  32.6 0.6 shard_map.53
  33.2 0.1 collective-permute-start.10
  33.2 1.5 %collective-permute-start.12 = (bf16[304,768]{1,0:T(8,128)(2,1)S(1)}, bf16[304,768]{1,0:T(8,128)(2,1)S(1)}, u32[]{:S(2)}, u32[]{:S(2)}) collective-permute-start(bf16[304,768]{1,0:T(8,128)(2,1)S(1)} %shard_map.52.own), channel_id=1, source_target_pairs={{192,0},{0,64},{64,128},{128,192},{224,32},{32,96},{96,160},{160,2... | collective-permute-start | bytes 1400840 | tf_op jit(solution)/shard_map/ppermute | solution.py:422
  34.8 2.0 %collective-permute-done.9.x_first = bf16[304,768]{1,0:T(8,128)(2,1)S(1)} collective-permute-done((bf16[304,768]{1,0:T(8,128)(2,1)S(1)}, bf16[304,768]{1,0:T(8,128)(2,1)S(1)}, u32[]{:S(2)}, u32[]{:S(2)}) %collective-permute-start.9) | collective-permute-done | bytes 466976 | tf_op jit(solution)/shard_map/ppermute | solution.py:422
  36.8 3.1 %collective-permute-start.13 = (bf16[304,768]{1,0:T(8,128)(2,1)S(1)}, bf16[304,768]{1,0:T(8,128)(2,1)S(1)}, u32[]{:S(2)}, u32[]{:S(2)}) collective-permute-start(bf16[304,768]{1,0:T(8,128)(2,1)S(1)} %collective-permute-done.9.x_first), channel_id=1, source_target_pairs={{34,0},{98,64},{162,128},{226,192},{0,32},{64,96},{128,160},{192,2... | collective-permute-start | bytes 1400840 | tf_op jit(solution)/shard_map/ppermute | solution.py:422
  39.9 0.1 collective-permute-done.11.y_first
  40.0 4.1 %collective-permute-start.14 = (bf16[304,768]{1,0:T(8,128)(2,1)S(1)}, bf16[304,768]{1,0:T(8,128)(2,1)S(1)}, u32[]{:S(2)}, u32[]{:S(2)}) collective-permute-start(bf16[304,768]{1,0:T(8,128)(2,1)S(1)} %collective-permute-done.11.y_first), channel_id=1, source_target_pairs={{64,0},{128,64},{192,128},{0,192},{96,32},{160,96},{224,160},{32,2... | collective-permute-start | bytes 1400840 | tf_op jit(solution)/shard_map/ppermute | solution.py:422
  44.1 0.0 collective-permute-done.10.x_second
  44.1 0.3 collective-permute-done.12.y_second
  44.4 2.5 %shard_map.54 = (f32[8,384]{1,0:T(8,128)S(1)}, f32[2,304,128]{2,1,0:T(8,128)S(1)}, s32[32,128]{1,0:T(8,128)S(1)}) custom-call(bf16[304,768]{1,0:T(8,128)(2,1)S(1)} %shard_map.52.own, bf16[304,768]{1,0:T(8,128)(2,1)S(1)} %collective-permute-done.9.x_first, bf16[304,768]{1,0:T(8,128)(2,1)S(1)} %collective-permute-done.10.x_second, ...), custom_call_target="tpu_custom_call" | custom-call | flops 1135607808 | bytes 933888 | tf_op jit(solution)/shard_map/pallas_call | solution.py:60
  46.9 0.6 collective-permute-done.13.x_far
  47.5 0.9 %shard_map.55 = (f32[8,384]{1,0:T(8,128)S(1)}, s32[16,128]{1,0:T(8,128)S(1)}) custom-call(bf16[304,768]{1,0:T(8,128)(2,1)S(1)} %shard_map.52.own, bf16[304,768]{1,0:T(8,128)(2,1)S(1)} %collective-permute-done.11.y_first, bf16[304,768]{1,0:T(8,128)(2,1)S(1)} %collective-permute-done.12.y_second, bf16[304,768]{1,0:T(8,128)(2,1)S(1)} %collective-permute-done.13.x_far, ...), custom_call_target="tpu_custom_call" | custom-call | flops 425852928 | bytes 933888 | tf_op jit(solution)/shard_map/pallas_call | solution.py:60
  48.4 2.7 %collective-permute-done.14.y_far = bf16[304,768]{1,0:T(8,128)(2,1)S(1)} collective-permute-done((bf16[304,768]{1,0:T(8,128)(2,1)S(1)}, bf16[304,768]{1,0:T(8,128)(2,1)S(1)}, u32[]{:S(2)}, u32[]{:S(2)}) %collective-permute-start.14) | collective-permute-done | bytes 466976 | tf_op jit(solution)/shard_map/ppermute | solution.py:422
  51.2 2.1 %shard_map.56 = f32[64,1,128]{2,1,0:T(1,128)} custom-call(bf16[304,768]{1,0:T(8,128)(2,1)S(1)} %shard_map.52.own, bf16[304,768]{1,0:T(8,128)(2,1)S(1)} %collective-permute-done.9.x_first, bf16[304,768]{1,0:T(8,128)(2,1)S(1)} %collective-permute-done.10.x_second, bf16[304,768]{1,0:T(8,128)(2,1)S(1)} %collective-permute-done.11.y_first, ...), custom_call_target="tpu_custom_call" | custom-call | flops 567803904 | bytes 933888 | tf_op jit(solution)/shard_map/pallas_call | solution.py:60
  53.3 10.9 %all-to-all-start.1 = ((f32[64,1,128]{2,1,0:T(1,128)}), f32[64,1,128]{2,1,0:T(1,128)S(1)}, u32[]{:S(2)}, u32[]{:S(2)}) async-start(f32[64,1,128]{2,1,0:T(1,128)} %shard_map.56), calls=%async_computation.1 | async-start | bytes 65536 | tf_op jit(solution)/shard_map/all_to_all | solution.py:464
  64.2 9.2 %all-to-all-done.1.ans_ref = f32[64,1,128]{2,1,0:T(1,128)S(1)} async-done(((f32[64,1,128]{2,1,0:T(1,128)}), f32[64,1,128]{2,1,0:T(1,128)S(1)}, u32[]{:S(2)}, u32[]{:S(2)}) %all-to-all-start.1) | async-done | bytes 32800 | tf_op jit(solution)/shard_map/all_to_all | solution.py:464
  73.3 0.7 shard_map.57
  74.7 0.0 copy-start.1
  74.7 0.6 copy-done.1
  (2 shorter events, 0.0 us)
Async XLA Ops:
  0.0 1.6 %copy-start = (bf16[256,768]{1,0:T(8,128)(2,1)S(1)}, bf16[256,768]{1,0:T(8,128)(2,1)}, u32[]{:S(2)}) copy-start(bf16[256,768]{1,0:T(8,128)(2,1)} %emb_ref.1) | copy-start | bytes 1179652
  2.2 13.3 %collective-permute-start.2 = (bf16[608,128]{1,0:T(8,128)(2,1)S(1)}, bf16[608,128]{1,0:T(8,128)(2,1)S(1)}, u32[]{:S(2)}, u32[]{:S(2)}) collective-permute-start(bf16[608,128]{1,0:T(8,128)(2,1)S(1)} %get-tuple-element.85), channel_id=1, source_target_pairs={{0,8},{1,25},{4,12},{5,29},{8,16},{9,1},{12,20},{13,5},{16,24},{17... | collective-permute-start | bytes 466952 | tf_op jit(solution)/shard_map/ppermute | solution.py:393
  9.1 6.5 %collective-permute-start.1 = (bf16[304,128]{1,0:T(8,128)(2,1)S(1)}, bf16[304,128]{1,0:T(8,128)(2,1)S(1)}, u32[]{:S(2)}, u32[]{:S(2)}) collective-permute-start(bf16[304,128]{1,0:T(8,128)(2,1)S(1)} %get-tuple-element.84), channel_id=1, source_target_pairs={{0,4},{1,29},{4,8},{5,1},{8,12},{9,5},{12,16},{13,9},{16,20},{17,1... | collective-permute-start | bytes 233480 | tf_op jit(solution)/shard_map/ppermute | solution.py:393
  9.8 8.9 %collective-permute-start.3 = (bf16[304,128]{1,0:T(8,128)(2,1)S(1)}, bf16[304,128]{1,0:T(8,128)(2,1)S(1)}, u32[]{:S(2)}, u32[]{:S(2)}) collective-permute-start(bf16[304,128]{1,0:T(8,128)(2,1)S(1)} %get-tuple-element.86), channel_id=1, source_target_pairs={{0,12},{1,21},{4,16},{5,25},{8,20},{9,29},{12,24},{13,1},{16,28},{... | collective-permute-start | bytes 233480 | tf_op jit(solution)/shard_map/ppermute | solution.py:393
  10.4 9.6 %collective-permute-start.5 = (bf16[304,128]{1,0:T(8,128)(2,1)S(1)}, bf16[304,128]{1,0:T(8,128)(2,1)S(1)}, u32[]{:S(2)}, u32[]{:S(2)}) collective-permute-start(bf16[304,128]{1,0:T(8,128)(2,1)S(1)} %get-tuple-element.87), channel_id=1, source_target_pairs={{0,20},{1,13},{4,24},{5,17},{8,28},{9,21},{12,0},{13,25},{16,4},{1... | collective-permute-start | bytes 233480 | tf_op jit(solution)/shard_map/ppermute | solution.py:393
  13.1 8.6 %collective-permute-start.6 = (bf16[304,128]{1,0:T(8,128)(2,1)S(1)}, bf16[304,128]{1,0:T(8,128)(2,1)S(1)}, u32[]{:S(2)}, u32[]{:S(2)}) collective-permute-start(bf16[304,128]{1,0:T(8,128)(2,1)S(1)} %get-tuple-element.88), channel_id=1, source_target_pairs={{0,24},{1,9},{4,28},{5,13},{8,0},{9,17},{12,4},{13,21},{16,8},{17,... | collective-permute-start | bytes 233480 | tf_op jit(solution)/shard_map/ppermute | solution.py:393
  15.5 9.4 %collective-permute-start.7 = (bf16[304,128]{1,0:T(8,128)(2,1)S(1)}, bf16[304,128]{1,0:T(8,128)(2,1)S(1)}, u32[]{:S(2)}, u32[]{:S(2)}) collective-permute-start(bf16[304,128]{1,0:T(8,128)(2,1)S(1)} %get-tuple-element.89), channel_id=1, source_target_pairs={{0,28},{1,5},{4,0},{5,9},{8,4},{9,13},{12,8},{13,17},{16,12},{17,2... | collective-permute-start | bytes 233480 | tf_op jit(solution)/shard_map/ppermute | solution.py:393
  15.6 9.3 %collective-permute-start.4 = (bf16[304,128]{1,0:T(8,128)(2,1)S(1)}, bf16[304,128]{1,0:T(8,128)(2,1)S(1)}, u32[]{:S(2)}, u32[]{:S(2)}) collective-permute-start(bf16[304,128]{1,0:T(8,128)(2,1)S(1)} %slice.65), channel_id=1, source_target_pairs={{0,8},{1,25},{4,12},{5,29},{8,16},{9,1},{12,20},{13,5},{16,24},{17... | collective-permute-start | bytes 233480 | tf_op jit(solution)/shard_map/ppermute | solution.py:393
  25.0 2.9 %collective-permute-start.8 = (bf16[416,768]{1,0:T(8,128)(2,1)S(1)}, bf16[416,768]{1,0:T(8,128)(2,1)S(1)}, u32[]{:S(2)}, u32[]{:S(2)}) collective-permute-start(bf16[416,768]{1,0:T(8,128)(2,1)S(1)} %shard_map.50.own_ref), channel_id=1, source_target_pairs={{0,1},{1,0},{2,3},{3,2},{4,5},{5,4},{6,7},{7,6},{8,9},{9,8},{10,11... | collective-permute-start | bytes 1916936 | tf_op jit(solution)/shard_map/ppermute | solution.py:410
  28.7 8.1 %collective-permute-start.9 = (bf16[304,768]{1,0:T(8,128)(2,1)S(1)}, bf16[304,768]{1,0:T(8,128)(2,1)S(1)}, u32[]{:S(2)}, u32[]{:S(2)}) collective-permute-start(bf16[304,768]{1,0:T(8,128)(2,1)S(1)} %shard_map.52.own), channel_id=1, source_target_pairs={{34,0},{98,64},{162,128},{226,192},{0,32},{64,96},{128,160},{192,2... | collective-permute-start | bytes 1400840 | tf_op jit(solution)/shard_map/ppermute | solution.py:422
  31.3 8.7 %collective-permute-start.11 = (bf16[304,768]{1,0:T(8,128)(2,1)S(1)}, bf16[304,768]{1,0:T(8,128)(2,1)S(1)}, u32[]{:S(2)}, u32[]{:S(2)}) collective-permute-start(bf16[304,768]{1,0:T(8,128)(2,1)S(1)} %shard_map.52.own), channel_id=1, source_target_pairs={{64,0},{128,64},{192,128},{0,192},{96,32},{160,96},{224,160},{32,2... | collective-permute-start | bytes 1400840 | tf_op jit(solution)/shard_map/ppermute | solution.py:422
  33.2 10.9 %collective-permute-start.10 = (bf16[304,768]{1,0:T(8,128)(2,1)S(1)}, bf16[304,768]{1,0:T(8,128)(2,1)S(1)}, u32[]{:S(2)}, u32[]{:S(2)}) collective-permute-start(bf16[304,768]{1,0:T(8,128)(2,1)S(1)} %shard_map.52.own), channel_id=1, source_target_pairs={{32,0},{96,64},{160,128},{224,192},{2,32},{66,96},{130,160},{194,2... | collective-permute-start | bytes 1400840 | tf_op jit(solution)/shard_map/ppermute | solution.py:422
  33.2 11.2 %collective-permute-start.12 = (bf16[304,768]{1,0:T(8,128)(2,1)S(1)}, bf16[304,768]{1,0:T(8,128)(2,1)S(1)}, u32[]{:S(2)}, u32[]{:S(2)}) collective-permute-start(bf16[304,768]{1,0:T(8,128)(2,1)S(1)} %shard_map.52.own), channel_id=1, source_target_pairs={{192,0},{0,64},{64,128},{128,192},{224,32},{32,96},{96,160},{160,2... | collective-permute-start | bytes 1400840 | tf_op jit(solution)/shard_map/ppermute | solution.py:422
  36.8 10.7 %collective-permute-start.13 = (bf16[304,768]{1,0:T(8,128)(2,1)S(1)}, bf16[304,768]{1,0:T(8,128)(2,1)S(1)}, u32[]{:S(2)}, u32[]{:S(2)}) collective-permute-start(bf16[304,768]{1,0:T(8,128)(2,1)S(1)} %collective-permute-done.9.x_first), channel_id=1, source_target_pairs={{34,0},{98,64},{162,128},{226,192},{0,32},{64,96},{128,160},{192,2... | collective-permute-start | bytes 1400840 | tf_op jit(solution)/shard_map/ppermute | solution.py:422
  40.0 11.2 %collective-permute-start.14 = (bf16[304,768]{1,0:T(8,128)(2,1)S(1)}, bf16[304,768]{1,0:T(8,128)(2,1)S(1)}, u32[]{:S(2)}, u32[]{:S(2)}) collective-permute-start(bf16[304,768]{1,0:T(8,128)(2,1)S(1)} %collective-permute-done.11.y_first), channel_id=1, source_target_pairs={{64,0},{128,64},{192,128},{0,192},{96,32},{160,96},{224,160},{32,2... | collective-permute-start | bytes 1400840 | tf_op jit(solution)/shard_map/ppermute | solution.py:422
  53.3 20.0 %all-to-all-start.1 = ((f32[64,1,128]{2,1,0:T(1,128)}), f32[64,1,128]{2,1,0:T(1,128)S(1)}, u32[]{:S(2)}, u32[]{:S(2)}) async-start(f32[64,1,128]{2,1,0:T(1,128)} %shard_map.56), calls=%async_computation.1 | async-start | bytes 65536 | tf_op jit(solution)/shard_map/all_to_all | solution.py:464
  74.7 0.6 copy-start.1
